TPU v7x, 32 devices: a whole 2x2x4 slice. The times are simulated.
32 devices in a mesh: sub: 4 (over z), blk: 2 (over y), rep: 4 (over x, core).
Axes of the slice: x: 2, y: 2, z: 4, core: 2. Of those that a mesh axis runs over, the one named last changes fastest.
Arguments:
- start_vector: float32 [4, 4, 2048], P('rep', 'sub', 'blk'), may hold values from -120 to 120
- blocks: bfloat16 [4, 4, 8, 32, 4096], P('rep', 'sub', 'blk'), may hold values from -0.4 to 2.4
- pattern: int32 [4, 4, 8, 32], P('rep', 'sub'), may hold values from 0 to 31, as said below
- trace_map: int32 [4, 4, 256], P('rep', 'sub', 'blk'), may hold values from 0 to 2047, as said below
- neighbours: int32 [4, 4, 2], P('rep', 'sub'), may hold values from 0 to 3, as said below
- coupling: float32 [4, 4, 2, 256], P('rep', 'sub', None, 'blk'), may hold values from -1 to 1
Outputs:
- basis_second: float32 [4, 4, 2048], P('rep', 'sub', 'blk')
- basis_third: float32 [4, 4, 2048], P('rep', 'sub', 'blk')
- hessenberg: float32 [5], replicated
Inputs may be any that keep to these rules, and one draw needn't show every extreme that they name: `pattern`: slot 0 of block row r names r itself; the other slots name any block row of the subdomain. `trace_map`: place t names a cell from (t // 128) * 16 * 64 to (t // 128 + 1) * 16 * 64 - 1; cells may repeat. The 2 neighbours of subdomain s are distinct and each lies one or two subdomains away from s in the same group.
All inputs are finite; a program needn't handle non-finite values.
Results may differ from a plain program's by a relative error of at most 0.0075.
Values may be sent and summed in bfloat16 or wider, within the bound.
No kernel may reach another device: no remote copies, remote signals or barrier semaphores. Data moves between devices by JAX's collectives and lax.ppermute only.
A program may use at most 64 MiB of HBM per device.

v0:
```python
import jax
import jax.numpy as jnp
from jax import lax
from jax.sharding import PartitionSpec as P

BS = 64
NNB = 2


epsilon = 1e-06
near_offsets = (-2, -1, 1, 2)


def shifted(block, axis, distance):
    devices = range(lax.axis_size(axis))
    route = [(i - distance, i) for i in devices if i - distance in devices]
    return lax.ppermute(block, axis, route)


def per_device(start_vector, blocks, pattern, trace_map, neighbours, coupling):
    own_cells = start_vector.shape[2]
    own_rows = own_cells // BS
    blk_index = lax.axis_index("blk")
    sub_index = lax.axis_index("sub")
    cell_total = own_cells * lax.axis_size("sub") * lax.axis_size("blk") * lax.axis_size("rep")
    global_map = trace_map[0, 0]
    local_map = global_map - blk_index * own_cells
    distance = neighbours[0, 0] - sub_index
    exchanged = lax.all_to_all(blocks, "blk", split_axis=3, concat_axis=2, tiled=True)[0, 0]
    exchanged = exchanged.reshape((exchanged.shape[0], own_rows, BS, BS))
    own_pattern = lax.dynamic_slice_in_dim(pattern[0, 0], blk_index * own_rows, own_rows, 1)

    def apply_op(vector_in):
        rounded = vector_in.astype(jnp.bfloat16)
        gathered = lax.all_gather(rounded, "blk", axis=0, tiled=True)
        own_trace = gathered[global_map]
        received = [shifted(own_trace, "sub", -step_off) for step_off in near_offsets]
        block_rows = gathered.reshape(-1, BS)
        picked = block_rows[own_pattern]
        product = jnp.einsum("kbij,kbj->bi", exchanged, picked, preferred_element_type=jnp.float32)
        inflow = jnp.zeros(global_map.shape, jnp.float32)
        for slot_n in range(NNB):
            arrived = jnp.zeros(global_map.shape, jnp.float32)
            for position, step_off in enumerate(near_offsets):
                arrived = arrived + jnp.where(
                    distance[slot_n] == step_off, received[position].astype(jnp.float32), 0.0
                )
            inflow = inflow + coupling[0, 0, slot_n] * arrived
        return product.reshape(-1).at[local_map].add(inflow)

    vector_own = start_vector[0, 0]
    square = lax.psum(jnp.sum(vector_own * vector_own), ("sub", "blk", "rep")) / cell_total
    basis_one = vector_own / jnp.sqrt(square + epsilon)
    image_one = apply_op(basis_one)
    diag_first = lax.psum(jnp.sum(basis_one * image_one), ("sub", "blk", "rep")) / cell_total
    residue_one = image_one - diag_first * basis_one
    first_square = lax.psum(jnp.sum(residue_one * residue_one), ("sub", "blk", "rep")) / cell_total
    below_first = jnp.sqrt(first_square + epsilon)
    basis_second = residue_one / below_first
    image_two = apply_op(basis_second)
    upper_sum, diag_sum = lax.psum(
        (jnp.sum(basis_one * image_two), jnp.sum(basis_second * image_two)), ("sub", "blk", "rep")
    )
    upper_second = upper_sum / cell_total
    diag_second = diag_sum / cell_total
    residue_two = image_two - upper_second * basis_one - diag_second * basis_second
    second_square = lax.psum(jnp.sum(residue_two * residue_two), ("sub", "blk", "rep")) / cell_total
    below_second = jnp.sqrt(second_square + epsilon)
    basis_third = residue_two / below_second
    hessenberg = jnp.stack([diag_first, below_first, upper_second, diag_second, below_second])
    return (basis_second[None, None], basis_third[None, None], hessenberg)


def solution(mesh):
    return jax.shard_map(
        per_device,
        mesh=mesh,
        in_specs=(
            P("rep", "sub", "blk"),
            P("rep", "sub", "blk", None, None),
            P("rep", "sub", None, None),
            P("rep", "sub", "blk"),
            P("rep", "sub", None),
            P("rep", "sub", None, "blk"),
        ),
        out_specs=(P("rep", "sub", "blk"), P("rep", "sub", "blk"), P()),
        check_vma=False,
    )
```

profile of v0, /device:TPU:0, one launch (start us, length us, event | category | flops | bytes accessed | tf_op | source)
XLA Modules:
  0.0 275.9 jit_solution(964030903460945465)
XLA Ops:
  0.6 1.3 multiply_reduce_fusion.5
  1.9 42.2 %psum.42 = f32[]{:T(128)} all-reduce(f32[]{:T(128)} %multiply_reduce_fusion.5), channel_id=1, replica_groups=mesh['sub'=4,'blk'=2,'rep'=4] {'sub','blk','rep'}, use_global_device_ids=true, to_apply=%region_1.0 | all-reduce | flops 1 | bytes 8 | tf_op jit(solution)/shard_map/psum | solution.py:52
  44.8 0.7 broadcast_divide_fusion.2
  45.5 4.7 %all_gather.6 = bf16[2048]{0:T(1024)(128)(2,1)S(1)} all-gather(bf16[1024]{0:T(1024)(128)(2,1)S(1)} %convert_element_type.38), channel_id=1, replica_groups=mesh['sub'=4,'blk'=2,'rep'=4] {'blk'}, dimensions={0}, use_global_device_ids=true | all-gather | bytes 6144 | tf_op jit(solution)/shard_map/all_gather | solution.py:35
  50.3 0.7 fusion.19
  50.9 1.3 gather_fusion.1
  52.2 0.0 copy-start.3
  52.2 0.0 copy-start.2
  52.2 0.0 copy-start.1
  52.3 1.4 collective-permute-start.3
  53.7 1.3 collective-permute-start.2
  55.0 4.5 %collective-permute-start.1 = (bf16[128]{0:T(256)(128)(2,1)S(1)}, bf16[128]{0:T(256)(128)(2,1)S(1)}, u32[]{:S(2)}, u32[]{:S(2)}) collective-permute-start(bf16[128]{0:T(256)(128)(2,1)S(1)} %gather_fusion.1), channel_id=1, source_target_pairs={{0,8},{8,16},{16,24},{1,9},{9,17},{17,25},{2,10},{10,18},{18,26},{... | collective-permute-start | bytes 776 | tf_op jit(solution)/shard_map/ppermute | solution.py:17
  59.5 5.4 %collective-permute-start = (bf16[128]{0:T(256)(128)(2,1)S(1)}, bf16[128]{0:T(256)(128)(2,1)S(1)}, u32[]{:S(2)}, u32[]{:S(2)}) collective-permute-start(bf16[128]{0:T(256)(128)(2,1)S(1)} %gather_fusion.1), channel_id=1, source_target_pairs={{0,16},{8,24},{1,17},{9,25},{2,18},{10,26},{3,19},{11,27},{4,20},{... | collective-permute-start | bytes 776 | tf_op jit(solution)/shard_map/ppermute | solution.py:17
  65.0 3.0 %copy.10 = bf16[1,1,4,32,4096]{4,2,1,0,3:T(4,128)(2,1)} copy(bf16[1,1,4,32,4096]{4,3,2,1,0:T(8,128)(2,1)} %param.7) | data formatting | bytes 2097152 | tf_op args[1]
  68.0 3.6 %all-to-all-start = ((bf16[1,1,4,32,4096]{4,2,1,0,3:T(4,128)(2,1)}), bf16[1,1,4,32,4096]{4,2,1,0,3:T(4,128)(2,1)S(1)}, u32[]{:S(2)}, u32[]{:S(2)}) async-start(bf16[1,1,4,32,4096]{4,2,1,0,3:T(4,128)(2,1)} %copy.10), calls=%async_computation | async-start | bytes 2097152 | tf_op jit(solution)/shard_map/all_to_all | solution.py:29
  71.6 0.1 reshape.142
  71.7 0.0 copy-done.3
  71.7 0.6 fusion.23
  74.9 0.0 copy-done.2
  74.9 0.1 compare_select_fusion
  75.0 0.1 reshape.148
  77.7 0.7 gather_fusion
  78.4 0.0 collective-permute-done.3
  78.4 0.0 collective-permute-done.2
  78.4 0.0 collective-permute-done.1
  78.4 0.0 collective-permute-done
  78.4 0.0 copy-done.1
  78.4 3.7 %all-to-all-done = bf16[1,1,4,32,4096]{4,2,1,0,3:T(4,128)(2,1)S(1)} async-done(((bf16[1,1,4,32,4096]{4,2,1,0,3:T(4,128)(2,1)}), bf16[1,1,4,32,4096]{4,2,1,0,3:T(4,128)(2,1)S(1)}, u32[]{:S(2)}, u32[]{:S(2)}) %all-to-all-start) | async-done | bytes 1048608 | tf_op jit(solution)/shard_map/all_to_all | solution.py:29
  82.1 0.6 copy.26
  82.7 2.3 reshape_squeeze.3
  85.0 0.6 fusion.2
  85.7 0.1 reshape.143
  85.7 1.5 scatter_fusion
  87.2 0.6 multiply_reduce_fusion.4
  87.8 37.6 %psum.43 = f32[]{:T(128)} all-reduce(f32[]{:T(128)} %multiply_reduce_fusion.4), channel_id=1, replica_groups=mesh['sub'=4,'blk'=2,'rep'=4] {'sub','blk','rep'}, use_global_device_ids=true, to_apply=%region_4.5 | all-reduce | flops 1 | bytes 8 | tf_op jit(solution)/shard_map/psum | solution.py:55
  126.1 0.6 multiply_reduce_fusion.3
  126.7 42.0 %psum.44 = f32[]{:T(128)} all-reduce(f32[]{:T(128)} %multiply_reduce_fusion.3), channel_id=1, replica_groups=mesh['sub'=4,'blk'=2,'rep'=4] {'sub','blk','rep'}, use_global_device_ids=true, to_apply=%region_6.7 | all-reduce | flops 1 | bytes 8 | tf_op jit(solution)/shard_map/psum | solution.py:57
  169.4 0.0 copy-start
  169.4 4.8 %all_gather.7 = bf16[2048]{0:T(1024)(128)(2,1)S(1)} all-gather(bf16[1024]{0:T(1024)(128)(2,1)S(1)} %get-tuple-element.9), channel_id=1, replica_groups=mesh['sub'=4,'blk'=2,'rep'=4] {'blk'}, dimensions={0}, use_global_device_ids=true | all-gather | bytes 6144 | tf_op jit(solution)/shard_map/all_gather | solution.py:35
  174.2 0.1 reshape.144
  174.3 1.3 gather_fusion.3
  175.5 1.3 collective-permute-start.7
  176.8 1.3 collective-permute-start.6
  178.1 4.5 %collective-permute-start.5 = (bf16[128]{0:T(256)(128)(2,1)S(1)}, bf16[128]{0:T(256)(128)(2,1)S(1)}, u32[]{:S(2)}, u32[]{:S(2)}) collective-permute-start(bf16[128]{0:T(256)(128)(2,1)S(1)} %gather_fusion.3), channel_id=1, source_target_pairs={{0,8},{8,16},{16,24},{1,9},{9,17},{17,25},{2,10},{10,18},{18,26},{... | collective-permute-start | bytes 776 | tf_op jit(solution)/shard_map/ppermute | solution.py:17
  182.7 5.4 %collective-permute-start.4 = (bf16[128]{0:T(256)(128)(2,1)S(1)}, bf16[128]{0:T(256)(128)(2,1)S(1)}, u32[]{:S(2)}, u32[]{:S(2)}) collective-permute-start(bf16[128]{0:T(256)(128)(2,1)S(1)} %gather_fusion.3), channel_id=1, source_target_pairs={{0,16},{8,24},{1,17},{9,25},{2,18},{10,26},{3,19},{11,27},{4,20},{... | collective-permute-start | bytes 776 | tf_op jit(solution)/shard_map/ppermute | solution.py:17
  188.1 0.7 gather_fusion.2
  188.8 0.6 fusion
  189.5 0.1 reshape.145
  189.5 0.0 collective-permute-done.7
  189.5 0.0 collective-permute-done.6
  189.6 0.0 collective-permute-done.5
  189.6 0.0 collective-permute-done.4
  189.6 1.4 scatter_fusion.1
  191.1 0.6 multiply_reduce_fusion.2
  191.7 40.8 %all-reduce = (f32[]{:T(128)}, f32[]{:T(128)}) all-reduce(f32[]{:T(128)} %get-tuple-element.4, f32[]{:T(128)} %get-tuple-element.3), channel_id=1, replica_groups=mesh['sub'=4,'blk'=2,'rep'=4] {'sub','blk','rep'}, use_global_device_ids=true, to_apply=%region_11.12 | all-reduce | flops 2 | bytes 16 | tf_op jit(solution)/shard_map/psum | solution.py:61
  233.8 0.0 copy-done
  233.8 0.6 multiply_reduce_fusion
  234.4 39.6 %psum.47 = f32[]{:T(128)} all-reduce(f32[]{:T(128)} %get-tuple-element.7), channel_id=1, replica_groups=mesh['sub'=4,'blk'=2,'rep'=4] {'sub','blk','rep'}, use_global_device_ids=true, to_apply=%region_13.14 | all-reduce | flops 1 | bytes 8 | tf_op jit(solution)/shard_map/psum | solution.py:67
  274.7 0.6 broadcast_divide_fusion
  275.3 0.6 stack.23
  (7 shorter events, 0.1 us)
Async XLA Ops:
  52.2 19.5 %copy-start.3 = (s32[1,1,2]{2,1,0:T(1,128)S(1)}, s32[1,1,2]{2,1,0:T(1,128)}, u32[]{:S(2)}) copy-start(s32[1,1,2]{2,1,0:T(1,128)} %param.10) | copy-start | bytes 28
  52.2 22.6 %copy-start.2 = (s32[1,1,8,32]{3,2,1,0:T(8,128)S(1)}, s32[1,1,8,32]{3,2,1,0:T(8,128)}, u32[]{:S(2)}) copy-start(s32[1,1,8,32]{3,2,1,0:T(8,128)} %param.8) | copy-start | bytes 3076
  52.2 26.2 %copy-start.1 = (f32[1,1,2,128]{3,2,1,0:T(2,128)S(1)}, f32[1,1,2,128]{3,2,1,0:T(2,128)}, u32[]{:S(2)}) copy-start(f32[1,1,2,128]{3,2,1,0:T(2,128)} %param.11) | copy-start | bytes 3076
  52.3 26.1 %collective-permute-start.3 = (bf16[128]{0:T(256)(128)(2,1)S(1)}, bf16[128]{0:T(256)(128)(2,1)S(1)}, u32[]{:S(2)}, u32[]{:S(2)}) collective-permute-start(bf16[128]{0:T(256)(128)(2,1)S(1)} %gather_fusion.1), channel_id=1, source_target_pairs={{16,0},{24,8},{17,1},{25,9},{18,2},{26,10},{19,3},{27,11},{20,4},{... | collective-permute-start | bytes 776 | tf_op jit(solution)/shard_map/ppermute | solution.py:17
  53.7 24.7 %collective-permute-start.2 = (bf16[128]{0:T(256)(128)(2,1)S(1)}, bf16[128]{0:T(256)(128)(2,1)S(1)}, u32[]{:S(2)}, u32[]{:S(2)}) collective-permute-start(bf16[128]{0:T(256)(128)(2,1)S(1)} %gather_fusion.1), channel_id=1, source_target_pairs={{8,0},{16,8},{24,16},{9,1},{17,9},{25,17},{10,2},{18,10},{26,18},{... | collective-permute-start | bytes 776 | tf_op jit(solution)/shard_map/ppermute | solution.py:17
  55.0 23.4 %collective-permute-start.1 = (bf16[128]{0:T(256)(128)(2,1)S(1)}, bf16[128]{0:T(256)(128)(2,1)S(1)}, u32[]{:S(2)}, u32[]{:S(2)}) collective-permute-start(bf16[128]{0:T(256)(128)(2,1)S(1)} %gather_fusion.1), channel_id=1, source_target_pairs={{0,8},{8,16},{16,24},{1,9},{9,17},{17,25},{2,10},{10,18},{18,26},{... | collective-permute-start | bytes 776 | tf_op jit(solution)/shard_map/ppermute | solution.py:17
  59.5 18.9 %collective-permute-start = (bf16[128]{0:T(256)(128)(2,1)S(1)}, bf16[128]{0:T(256)(128)(2,1)S(1)}, u32[]{:S(2)}, u32[]{:S(2)}) collective-permute-start(bf16[128]{0:T(256)(128)(2,1)S(1)} %gather_fusion.1), channel_id=1, source_target_pairs={{0,16},{8,24},{1,17},{9,25},{2,18},{10,26},{3,19},{11,27},{4,20},{... | collective-permute-start | bytes 776 | tf_op jit(solution)/shard_map/ppermute | solution.py:17
  68.0 14.1 %all-to-all-start = ((bf16[1,1,4,32,4096]{4,2,1,0,3:T(4,128)(2,1)}), bf16[1,1,4,32,4096]{4,2,1,0,3:T(4,128)(2,1)S(1)}, u32[]{:S(2)}, u32[]{:S(2)}) async-start(bf16[1,1,4,32,4096]{4,2,1,0,3:T(4,128)(2,1)} %copy.10), calls=%async_computation | async-start | bytes 2097152 | tf_op jit(solution)/shard_map/all_to_all | solution.py:29
  169.4 64.3 %copy-start = (f32[1024]{0:T(1024)}, f32[1024]{0:T(1024)S(1)}, u32[]{:S(2)}) copy-start(f32[1024]{0:T(1024)S(1)} %get-tuple-element.10) | copy-start | bytes 12292
  175.5 14.0 %collective-permute-start.7 = (bf16[128]{0:T(256)(128)(2,1)S(1)}, bf16[128]{0:T(256)(128)(2,1)S(1)}, u32[]{:S(2)}, u32[]{:S(2)}) collective-permute-start(bf16[128]{0:T(256)(128)(2,1)S(1)} %gather_fusion.3), channel_id=1, source_target_pairs={{16,0},{24,8},{17,1},{25,9},{18,2},{26,10},{19,3},{27,11},{20,4},{... | collective-permute-start | bytes 776 | tf_op jit(solution)/shard_map/ppermute | solution.py:17
  176.8 12.7 %collective-permute-start.6 = (bf16[128]{0:T(256)(128)(2,1)S(1)}, bf16[128]{0:T(256)(128)(2,1)S(1)}, u32[]{:S(2)}, u32[]{:S(2)}) collective-permute-start(bf16[128]{0:T(256)(128)(2,1)S(1)} %gather_fusion.3), channel_id=1, source_target_pairs={{8,0},{16,8},{24,16},{9,1},{17,9},{25,17},{10,2},{18,10},{26,18},{... | collective-permute-start | bytes 776 | tf_op jit(solution)/shard_map/ppermute | solution.py:17
  178.1 11.4 %collective-permute-start.5 = (bf16[128]{0:T(256)(128)(2,1)S(1)}, bf16[128]{0:T(256)(128)(2,1)S(1)}, u32[]{:S(2)}, u32[]{:S(2)}) collective-permute-start(bf16[128]{0:T(256)(128)(2,1)S(1)} %gather_fusion.3), channel_id=1, source_target_pairs={{0,8},{8,16},{16,24},{1,9},{9,17},{17,25},{2,10},{10,18},{18,26},{... | collective-permute-start | bytes 776 | tf_op jit(solution)/shard_map/ppermute | solution.py:17
  182.7 6.9 %collective-permute-start.4 = (bf16[128]{0:T(256)(128)(2,1)S(1)}, bf16[128]{0:T(256)(128)(2,1)S(1)}, u32[]{:S(2)}, u32[]{:S(2)}) collective-permute-start(bf16[128]{0:T(256)(128)(2,1)S(1)} %gather_fusion.3), channel_id=1, source_target_pairs={{0,16},{8,24},{1,17},{9,25},{2,18},{10,26},{3,19},{11,27},{4,20},{... | collective-permute-start | bytes 776 | tf_op jit(solution)/shard_map/ppermute | solution.py:17
where the time goes:
time: 277 us; the launch traced here: 276 us
  blocking collectives  212 us (77%)
  starting transfers between devices  28.9 us (10%)
  local copies, waits for them, and re-layouts  11.4 us (4%)
  between operations  10.1 us (4%)
  other arithmetic  8.7 us (3%)
  waiting for transfers between devices  3.76 us (1%)
    psum x1, blocking collectives, per_device(): lax.psum(jnp.sum(vector_own * vector_own), ('sub', 'blk', 'rep'))  42.2 us
    psum x1, blocking collectives, per_device(): lax.psum(jnp.sum(residue_one * residue_one), ('sub', 'blk', 'rep'))  42 us
    psum x1, blocking collectives, per_device(): lax.psum((jnp.sum(basis_one * image_two), jnp.sum(basis_second * image_tw...  40.8 us
    psum x1, blocking collectives, per_device(): lax.psum(jnp.sum(residue_two * residue_two), ('sub', 'blk', 'rep'))  39.6 us
    psum x1, blocking collectives, per_device(): lax.psum(jnp.sum(basis_one * image_one), ('sub', 'blk', 'rep')) / cell_total  37.6 us
    ppermute x8, starting transfers between devices, shifted(): return lax.ppermute(block, axis, route)  25.3 us
    all_gather x2, blocking collectives, apply_op(): gathered = lax.all_gather(rounded, 'blk', axis=0, tiled=True)  9.5 us
  transfers between devices with their start and end apart: 9, of which 1 were waited for; matrix products, arithmetic and copies ran while one was open for 2% of the time, Pallas kernels for 0%

commit v1 on v0

v1 whole, which is shorter than its diff:
```python
import functools

import jax
import jax.numpy as jnp
from jax import lax
from jax.experimental import pallas as pl
from jax.experimental.pallas import tpu as pltpu
from jax.sharding import PartitionSpec as P

BS = 64
LANES = 128
SUBL = 8
epsilon = 1e-06


def pieces(value):
    high = value.astype(jnp.bfloat16)
    rest = value - high.astype(jnp.float32)
    middle = rest.astype(jnp.bfloat16)
    low = (rest - middle.astype(jnp.float32)).astype(jnp.bfloat16)
    return high, middle, low


def lane_iota(shape):
    return lax.broadcasted_iota(jnp.int32, shape, len(shape) - 1)


def row_iota(shape):
    return lax.broadcasted_iota(jnp.int32, shape, 0)


def block_product(vector, blocks_ref, pattern_ref, first_slot, fold_ref):
    slots, block_rows, width = blocks_ref.shape
    half = block_rows // 2
    lower = lane_iota(vector.shape) < BS
    turned = pltpu.roll(vector, BS, 1)
    table = jnp.concatenate([jnp.where(lower, vector, turned), jnp.where(lower, turned, vector)], 0)
    table = jnp.concatenate(pieces(table), 0)
    place = row_iota((block_rows, block_rows))
    place = jnp.where(place < half, 2 * place, 2 * (place - half) + 1)
    picked = []
    for k in range(slots):
        names = pattern_ref[pl.ds(first_slot + k, 1), :]
        chosen = (place == names).astype(jnp.float32).astype(jnp.bfloat16)
        chosen = jnp.concatenate([chosen] * 3, 0)
        picked.append(
            lax.dot_general(chosen, table, (((0,), (0,)), ((), ())), preferred_element_type=jnp.float32)
        )
    ones = (row_iota((2 * LANES, LANES)) % LANES) // BS == lane_iota((2 * LANES, LANES)) % 2
    ones = ones.astype(jnp.float32).astype(jnp.bfloat16)
    pair = (lane_iota((block_rows, LANES)) % BS) // 2
    result = jnp.zeros((block_rows, LANES), jnp.float32)
    for c in range(width // LANES):
        total = None
        for k in range(slots):
            term = blocks_ref[k, :, pl.ds(c * LANES, LANES)].astype(jnp.float32) * picked[k]
            total = term if total is None else total + term
        high = total.astype(jnp.bfloat16)
        low = (total - high.astype(jnp.float32)).astype(jnp.bfloat16)
        sums = lax.dot_general(
            jnp.concatenate([high, low], 1), ones, (((1,), (0,)), ((), ())), preferred_element_type=jnp.float32
        )
        result = jnp.where(pair == c, sums, result)
    fold_ref[...] = result
    even = fold_ref[pl.ds(0, half, stride=2), :]
    odd = fold_ref[pl.ds(1, half, stride=2), :]
    return jnp.where(lane_iota((half, LANES)) < BS, even, odd)


def take_trace(rows, places):
    count = rows.shape[0]
    low = jnp.broadcast_to(places % LANES, (count, LANES))
    picked = jnp.take_along_axis(rows, low, axis=1)
    return jnp.sum(jnp.where(row_iota((count, LANES)) == places // LANES, picked, 0.0), axis=0, keepdims=True)


def spread(values, places, count):
    aimed = jnp.where(row_iota((count, LANES)) == places // LANES, values, 0.0)
    high = aimed.astype(jnp.bfloat16).astype(jnp.float32)
    rest = aimed - high
    middle = rest.astype(jnp.bfloat16).astype(jnp.float32)
    stack = jnp.concatenate([high, middle, rest - middle], 0).astype(jnp.bfloat16)
    target = (row_iota((LANES, LANES)) == places % LANES).astype(jnp.float32).astype(jnp.bfloat16)
    landed = lax.dot_general(stack, target, (((1,), (1,)), ((), ())), preferred_element_type=jnp.float32)
    return landed[0:count] + landed[count : 2 * count] + landed[2 * count : 3 * count]


def first_kernel(near_ref, blocks_ref, pattern_ref, map_ref, neighbours_ref, coupling_ref, out_ref, fold_ref):
    rows = out_ref.shape[0]
    parts = lax.axis_size("blk")
    own_rows = rows // parts
    sub, blk = lax.axis_index("sub"), lax.axis_index("blk")
    first_cell = blk * own_rows * LANES
    vector = jnp.concatenate([near_ref[sub * parts + b, 0:own_rows, :] for b in range(parts)], 0)
    out_ref[...] = block_product(vector, blocks_ref, pattern_ref, blk * blocks_ref.shape[0], fold_ref)
    inflow = jnp.zeros((1, LANES), jnp.float32)
    for n in range(coupling_ref.shape[0]):
        source = neighbours_ref[n] * parts + blk
        places = near_ref[source, own_rows : own_rows + 1, :].astype(jnp.int32) - first_cell
        trace = take_trace(near_ref[source, 0:own_rows, :], places)
        inflow = inflow + coupling_ref[n : n + 1, :] * trace
    own = pl.ds(pl.multiple_of(blk * own_rows, SUBL), own_rows)
    out_ref[own, :] = out_ref[own, :] + spread(inflow, map_ref[...] - first_cell, own_rows)


def second_kernel(
    near_ref, image_ref, blocks_ref, pattern_ref, map_ref, neighbours_ref, coupling_ref, out_ref, own_ref, fold_ref
):
    rows = image_ref.shape[1]
    parts = lax.axis_size("blk")
    own_rows = rows // parts
    sub, blk = lax.axis_index("sub"), lax.axis_index("blk")
    first_cell = blk * own_rows * LANES
    own = pl.ds(pl.multiple_of(blk * own_rows, SUBL), own_rows)

    def summed(index, where):
        total = image_ref[index * parts, where, :]
        for b in range(1, parts):
            total = total + image_ref[index * parts + b, where, :]
        return total

    vector = jnp.concatenate([near_ref[sub * parts + b, 0:own_rows, :] for b in range(parts)], 0)
    image = summed(sub, pl.ds(0, rows))
    out_ref[0:rows, :] = block_product(image, blocks_ref, pattern_ref, blk * blocks_ref.shape[0], fold_ref)
    inflow = jnp.zeros((1, LANES), jnp.float32)
    for n in range(coupling_ref.shape[0]):
        source = neighbours_ref[n]
        places = near_ref[source * parts + blk, own_rows : own_rows + 1, :].astype(jnp.int32) - first_cell
        trace = take_trace(summed(source, own), places)
        inflow = inflow + coupling_ref[n : n + 1, :] * trace
    out_ref[own, :] = out_ref[own, :] + spread(inflow, map_ref[...] - first_cell, own_rows)
    second = out_ref[0:rows, :]
    vector_own = near_ref[sub * parts + blk, 0:own_rows, :]
    image_own = summed(sub, own)
    own_ref[...] = image_own

    def down(left, right):
        return jnp.sum(left * right, axis=0, keepdims=True)

    sums = [
        down(vector_own, vector_own),
        down(vector_own, image_own),
        down(image_own, image_own),
        down(vector, second),
        down(image, second),
        jnp.zeros((SUBL - 5, LANES), jnp.float32),
    ]
    out_ref[rows : rows + SUBL, :] = jnp.concatenate(sums, 0)


def last_kernel(cells, start_ref, own_ref, all_ref, second_ref, third_ref, entries_ref):
    devices, height, _ = all_ref.shape
    rows = height - SUBL
    parts = lax.axis_size("blk")
    subs = lax.axis_size("sub")
    own_rows = rows // parts
    rep, sub, blk = lax.axis_index("rep"), lax.axis_index("sub"), lax.axis_index("blk")
    own = pl.ds(pl.multiple_of(blk * own_rows, SUBL), own_rows)

    sums = jnp.zeros((SUBL, LANES), jnp.float32)
    square = jnp.zeros((rows, LANES), jnp.float32)
    for pair in range(devices // parts):
        total = None
        for b in range(parts):
            sums = sums + all_ref[pair * parts + b, rows:height, :]
            term = all_ref[pair * parts + b, 0:rows, :]
            total = term if total is None else total + term
        square = square + total * total
    square = jnp.sum(square, axis=0, keepdims=True)

    def whole(line):
        return jnp.broadcast_to(jnp.sum(line, axis=1, keepdims=True), (1, LANES)) / cells

    vv, vw, ww, vy, wy = (whole(sums[i : i + 1, :]) for i in range(5))
    yy = whole(square)
    norm_square = vv + epsilon
    h11 = vw / norm_square
    first_square = jnp.maximum(ww - 2.0 * h11 * vw + h11 * h11 * vv, 0.0) / norm_square
    h21 = jnp.sqrt(first_square + epsilon)
    scale = 1.0 / (jnp.sqrt(norm_square) * h21)
    h12 = (vy - h11 * vw) / (norm_square * h21)
    h22 = (wy - h11 * (ww + vy - h11 * vw)) * scale * scale
    near = h11 + h22
    far = h12 * h21 - h11 * h22
    second_square = yy + near * near * ww + far * far * vv + 2.0 * (near * far * vw - near * wy - far * vy)
    h32 = jnp.sqrt(jnp.maximum(second_square, 0.0) * scale * scale + epsilon)

    vector = start_ref[...]
    image = own_ref[...]
    base = (rep * subs + sub) * parts
    again = all_ref[base, own, :]
    for b in range(1, parts):
        again = again + all_ref[base + b, own, :]
    second_ref[...] = (image - h11 * vector) * scale
    third_ref[...] = (again - near * image - far * vector) * (scale / h32)
    lane = lane_iota((1, LANES))
    entries = h32
    for i, value in enumerate((h11, h21, h12, h22)):
        entries = jnp.where(lane == i, value, entries)
    entries_ref[...] = entries[:, 0:5]


def per_device(start_vector, blocks, pattern, trace_map, neighbours, coupling):
    own_cells = start_vector.shape[2]
    own_rows = own_cells // LANES
    parts = lax.axis_size("blk")
    rows = own_rows * parts
    cells = own_cells * parts * lax.axis_size("sub") * lax.axis_size("rep")
    start = start_vector.reshape(own_rows, LANES)
    local_map = trace_map[0]
    blocks, pattern, neighbours, coupling = blocks[0, 0], pattern[0, 0], neighbours[0, 0], coupling[0, 0]
    vmem = pl.BlockSpec(memory_space=pltpu.VMEM)
    smem = pl.BlockSpec(memory_space=pltpu.SMEM)
    fold = pltpu.VMEM((blocks.shape[1], LANES), jnp.float32)
    params = pltpu.CompilerParams(vmem_limit_bytes=40 * 1024 * 1024)

    near = lax.all_gather(jnp.concatenate([start, local_map.astype(jnp.float32)], 0), ("sub", "blk"))
    partial = pl.pallas_call(
        first_kernel,
        out_shape=jax.ShapeDtypeStruct((rows, LANES), jnp.float32),
        in_specs=[vmem, vmem, vmem, vmem, smem, vmem],
        out_specs=vmem,
        scratch_shapes=[fold],
        compiler_params=params,
        name="first_image",
    )(near, blocks, pattern, local_map, neighbours, coupling)
    images = lax.all_gather(partial, ("sub", "blk"))
    partial, image = pl.pallas_call(
        second_kernel,
        out_shape=(
            jax.ShapeDtypeStruct((rows + SUBL, LANES), jnp.float32),
            jax.ShapeDtypeStruct((own_rows, LANES), jnp.float32),
        ),
        in_specs=[vmem, vmem, vmem, vmem, vmem, smem, vmem],
        out_specs=(vmem, vmem),
        scratch_shapes=[fold],
        compiler_params=params,
        name="second_image",
    )(near, images, blocks, pattern, local_map, neighbours, coupling)
    everything = lax.all_gather(partial, ("rep", "sub", "blk"))
    second, third, entries = pl.pallas_call(
        functools.partial(last_kernel, float(cells)),
        out_shape=(
            jax.ShapeDtypeStruct((own_rows, LANES), jnp.float32),
            jax.ShapeDtypeStruct((own_rows, LANES), jnp.float32),
            jax.ShapeDtypeStruct((1, 5), jnp.float32),
        ),
        in_specs=[vmem, vmem, vmem],
        out_specs=(vmem, vmem, vmem),
        compiler_params=params,
        name="arnoldi_entries",
    )(start, image, everything)
    return second.reshape(start_vector.shape), third.reshape(start_vector.shape), entries.reshape(5)


def solution(mesh):
    return jax.shard_map(
        per_device,
        mesh=mesh,
        in_specs=(
            P("rep", "sub", "blk"),
            P("rep", "sub", "blk", None, None),
            P("rep", "sub", None, None),
            P("rep", "sub", "blk"),
            P("rep", "sub", None),
            P("rep", "sub", None, "blk"),
        ),
        out_specs=(P("rep", "sub", "blk"), P("rep", "sub", "blk"), P()),
        check_vma=False,
    )
```

time: 277 us -> 136 us (0.49)
  blocking collectives: 212 us -> 130 us
  starting transfers between devices: 28.9 us -> 0 us
  local copies, waits for them, and re-layouts: 11.4 us -> 1.9 us
  between operations: 10.1 us -> 0.69 us
  other arithmetic: 8.7 us -> 0.01 us
  waiting for transfers between devices: 3.76 us -> 0 us
  Pallas kernels: 0 us -> 3.27 us
    psum x5 -> x0, blocking collectives: 202 us -> none  [the longest x1 42.2 us: per_device(): lax.psum(jnp.sum(vector_own * vector_own), ('sub', 'blk', 'rep'))]
    all_gather x2 -> x3, blocking collectives: 9.5 us -> 130 us  [the longest x1 67.1 us: per_device(): everything = lax.all_gather(partial, ('rep', 'sub', 'blk'))]
    ppermute x8 -> x0, starting transfers between devices: 25.3 us -> none  [shifted(): return lax.ppermute(block, axis, route)]
    gather x4 -> x0, local copies, waits for them, and re-layouts: 3.95 us -> none  [the longest x2 2.52 us: apply_op(): own_trace = gathered[global_map]]
    reduce_sum x5 -> x0, other arithmetic: 3.72 us -> none  [the longest x1 1.3 us: per_device(): jnp.sum(vector_own * vector_own)]
    all_to_all x1 -> x0, waiting for transfers between devices: 3.71 us -> none  [per_device(): lax.all_to_all(blocks, 'blk', split_axis=3, concat_axis=2, tiled=True)[0, 0]]
    all_to_all x1 -> x0, starting transfers between devices: 3.58 us -> none  [per_device(): lax.all_to_all(blocks, 'blk', split_axis=3, concat_axis=2, tiled=True)[0, 0]]
    pallas_call x0 -> x3, Pallas kernels: none -> 3.27 us  [the longest x1 1.26 us: per_device(): pl.pallas_call(second_kernel, out_shape=(jax.ShapeDtypeStruct((rows + SUB...]
  transfers between devices with their start and end apart: 9 -> 0, of which waited for: 1 -> 0; matrix products, arithmetic and copies ran while one was open for 2% -> 0% of each run, Pallas kernels for 0% -> 0%
where the time goes in v1:
time: 136 us
  blocking collectives  130 us (96%)
  Pallas kernels  3.27 us (2%)
  local copies, waits for them, and re-layouts  1.9 us (1%)
    all_gather x1, blocking collectives, per_device(): everything = lax.all_gather(partial, ('rep', 'sub', 'blk'))  67.1 us
    all_gather x1, blocking collectives, per_device(): lax.all_gather(jnp.concatenate([start, local_map.astype(jnp.float32)], 0)...  32.4 us
    all_gather x1, blocking collectives, per_device(): images = lax.all_gather(partial, ('sub', 'blk'))  30.5 us

profile of v1, /device:TPU:0, one launch (start us, length us, event | category | flops | bytes accessed | tf_op | source)
XLA Modules:
  0.0 135.9 jit_solution(18004084918872892109)
XLA Ops:
  0.6 0.0 copy-start.2
  0.6 0.0 copy-start.4
  0.6 0.7 copy-done.4
  1.3 0.0 copy-done.2
  1.3 0.0 copy-start.1
  1.3 0.0 copy-start.3
  1.3 0.0 copy-start.5
  1.4 32.4 %all-gather.3.near_ref = f32[8,9,128]{2,1,0:T(8,128)S(1)} all-gather(f32[1,9,128]{2,1,0:T(8,128)S(1)} %maximum_bitcast_fusion), channel_id=2, replica_groups=mesh['sub'=4,'blk'=2,'rep'=4] {'sub','blk'}, dimensions={0}, use_global_device_ids=true | all-gather | bytes 41472 | tf_op jit(solution)/shard_map/all_gather | solution.py:217
  33.8 0.0 copy-done.1
  33.8 0.0 copy-done.3
  33.8 0.0 copy-done.5
  33.8 0.0 copy-start
  33.8 1.2 copy-done
  35.0 1.2 first_image.1
  36.2 30.5 %all-gather.1 = f32[128,128]{1,0:T(8,128)S(1)} all-gather(f32[16,128]{1,0:T(8,128)S(1)} %first_image.1), channel_id=3, replica_groups=mesh['sub'=4,'blk'=2,'rep'=4] {'sub','blk'}, dimensions={0}, use_global_device_ids=true | all-gather | bytes 73728 | tf_op jit(solution)/shard_map/all_gather | solution.py:227
  66.8 1.3 second_image.1
  68.0 67.1 %all-gather.2 = f32[768,128]{1,0:T(8,128)S(1)} all-gather(f32[24,128]{1,0:T(8,128)S(1)} %get-tuple-element.9), channel_id=4, replica_groups=mesh['sub'=4,'blk'=2,'rep'=4] {'rep','sub','blk'}, dimensions={0}, use_global_device_ids=true | all-gather | bytes 405504 | tf_op jit(solution)/shard_map/all_gather | solution.py:240
  135.2 0.8 arnoldi_entries.1
  (2 shorter events, 0.0 us)
Async XLA Ops:
  0.6 0.7 copy-start.2
  0.6 0.7 copy-start.4
  1.3 32.4 %copy-start.1 = (s32[1,1,8,32]{3,2,1,0:T(8,128)S(1)}, s32[1,1,8,32]{3,2,1,0:T(8,128)}, u32[]{:S(2)}) copy-start(s32[1,1,8,32]{3,2,1,0:T(8,128)} %param.8) | copy-start | bytes 3076
  1.3 32.4 %copy-start.3 = (f32[1,1,2,128]{3,2,1,0:T(2,128)S(1)}, f32[1,1,2,128]{3,2,1,0:T(2,128)}, u32[]{:S(2)}) copy-start(f32[1,1,2,128]{3,2,1,0:T(2,128)} %param.11) | copy-start | bytes 3076
  1.3 32.4 %copy-start.5 = (s32[1,1,2]{2,1,0:T(1,128)S(1)}, s32[1,1,2]{2,1,0:T(1,128)}, u32[]{:S(2)}) copy-start(s32[1,1,2]{2,1,0:T(1,128)} %param.10) | copy-start | bytes 28
  33.8 1.2 copy-start

commit v2 on v1

--- a/solution.py
+++ b/solution.py
@@ -85,14 +85,14 @@
     return landed[0:count] + landed[count : 2 * count] + landed[2 * count : 3 * count]
 
 
-def first_kernel(near_ref, blocks_ref, pattern_ref, map_ref, neighbours_ref, coupling_ref, out_ref, fold_ref):
-    rows = out_ref.shape[0]
+def first_kernel(near_ref, blocks_ref, pattern_ref, map_ref, neighbours_ref, coupling_ref, out_ref, fold_ref, sum_ref):
+    rows = sum_ref.shape[0]
     parts = lax.axis_size("blk")
     own_rows = rows // parts
     sub, blk = lax.axis_index("sub"), lax.axis_index("blk")
     first_cell = blk * own_rows * LANES
     vector = jnp.concatenate([near_ref[sub * parts + b, 0:own_rows, :] for b in range(parts)], 0)
-    out_ref[...] = block_product(vector, blocks_ref, pattern_ref, blk * blocks_ref.shape[0], fold_ref)
+    sum_ref[...] = block_product(vector, blocks_ref, pattern_ref, blk * blocks_ref.shape[0], fold_ref)
     inflow = jnp.zeros((1, LANES), jnp.float32)
     for n in range(coupling_ref.shape[0]):
         source = neighbours_ref[n] * parts + blk
@@ -100,7 +100,10 @@
         trace = take_trace(near_ref[source, 0:own_rows, :], places)
         inflow = inflow + coupling_ref[n : n + 1, :] * trace
     own = pl.ds(pl.multiple_of(blk * own_rows, SUBL), own_rows)
-    out_ref[own, :] = out_ref[own, :] + spread(inflow, map_ref[...] - first_cell, own_rows)
+    sum_ref[own, :] = sum_ref[own, :] + spread(inflow, map_ref[...] - first_cell, own_rows)
+    partial = sum_ref[...]
+    for device in range(out_ref.shape[0]):
+        out_ref[device] = partial
 
 
 def second_kernel(
@@ -148,31 +151,31 @@
     out_ref[rows : rows + SUBL, :] = jnp.concatenate(sums, 0)
 
 
-def last_kernel(cells, start_ref, own_ref, all_ref, second_ref, third_ref, entries_ref):
-    devices, height, _ = all_ref.shape
+def pair_kernel(pair_ref, out_ref, own_ref):
+    parts, height, _ = pair_ref.shape
     rows = height - SUBL
-    parts = lax.axis_size("blk")
-    subs = lax.axis_size("sub")
     own_rows = rows // parts
-    rep, sub, blk = lax.axis_index("rep"), lax.axis_index("sub"), lax.axis_index("blk")
-    own = pl.ds(pl.multiple_of(blk * own_rows, SUBL), own_rows)
-
-    sums = jnp.zeros((SUBL, LANES), jnp.float32)
-    square = jnp.zeros((rows, LANES), jnp.float32)
-    for pair in range(devices // parts):
-        total = None
-        for b in range(parts):
-            sums = sums + all_ref[pair * parts + b, rows:height, :]
-            term = all_ref[pair * parts + b, 0:rows, :]
-            total = term if total is None else total + term
-        square = square + total * total
-    square = jnp.sum(square, axis=0, keepdims=True)
-
-    def whole(line):
-        return jnp.broadcast_to(jnp.sum(line, axis=1, keepdims=True), (1, LANES)) / cells
-
-    vv, vw, ww, vy, wy = (whole(sums[i : i + 1, :]) for i in range(5))
-    yy = whole(square)
+    total = pair_ref[0]
+    for b in range(1, parts):
+        total = total + pair_ref[b]
+    square = jnp.sum(total[0:rows] * total[0:rows], axis=0, keepdims=True)
+    sums = jnp.where(row_iota((SUBL, LANES)) == 5, square, total[rows:height])
+    for device in range(out_ref.shape[0]):
+        out_ref[device] = sums
+    own = pl.ds(pl.multiple_of(lax.axis_index("blk") * own_rows, SUBL), own_rows)
+    again = pair_ref[0, own, :]
+    for b in range(1, parts):
+        again = again + pair_ref[b, own, :]
+    own_ref[...] = again
+
+
+def last_kernel(cells, start_ref, own_ref, again_ref, sums_ref, second_ref, third_ref, entries_ref):
+    sums = jnp.sum(sums_ref[...], axis=0)
+
+    def whole(i):
+        return jnp.broadcast_to(jnp.sum(sums[i : i + 1, :], axis=1, keepdims=True), (1, LANES)) / cells
+
+    vv, vw, ww, vy, wy, yy = (whole(i) for i in range(6))
     norm_square = vv + epsilon
     h11 = vw / norm_square
     first_square = jnp.maximum(ww - 2.0 * h11 * vw + h11 * h11 * vv, 0.0) / norm_square
@@ -185,14 +188,9 @@
     second_square = yy + near * near * ww + far * far * vv + 2.0 * (near * far * vw - near * wy - far * vy)
     h32 = jnp.sqrt(jnp.maximum(second_square, 0.0) * scale * scale + epsilon)
 
-    vector = start_ref[...]
-    image = own_ref[...]
-    base = (rep * subs + sub) * parts
-    again = all_ref[base, own, :]
-    for b in range(1, parts):
-        again = again + all_ref[base + b, own, :]
+    vector, image = start_ref[...], own_ref[...]
     second_ref[...] = (image - h11 * vector) * scale
-    third_ref[...] = (again - near * image - far * vector) * (scale / h32)
+    third_ref[...] = (again_ref[...] - near * image - far * vector) * (scale / h32)
     lane = lane_iota((1, LANES))
     entries = h32
     for i, value in enumerate((h11, h21, h12, h22)):
@@ -203,53 +201,61 @@
 def per_device(start_vector, blocks, pattern, trace_map, neighbours, coupling):
     own_cells = start_vector.shape[2]
     own_rows = own_cells // LANES
-    parts = lax.axis_size("blk")
+    parts, subs, reps = lax.axis_size("blk"), lax.axis_size("sub"), lax.axis_size("rep")
     rows = own_rows * parts
-    cells = own_cells * parts * lax.axis_size("sub") * lax.axis_size("rep")
+    cells = own_cells * parts * subs * reps
     start = start_vector.reshape(own_rows, LANES)
     local_map = trace_map[0]
     blocks, pattern, neighbours, coupling = blocks[0, 0], pattern[0, 0], neighbours[0, 0], coupling[0, 0]
     vmem = pl.BlockSpec(memory_space=pltpu.VMEM)
     smem = pl.BlockSpec(memory_space=pltpu.SMEM)
+    params = pltpu.CompilerParams(vmem_limit_bytes=40 * 1024 * 1024)
+
+    def rowed(*shape):
+        return jax.ShapeDtypeStruct((*shape, LANES), jnp.float32)
+
+    payload = jnp.concatenate([start, local_map.astype(jnp.float32)], 0)
+    payload = jnp.pad(payload, ((0, SUBL - 1), (0, 0)))
+    payload = jnp.broadcast_to(payload, (subs * parts, *payload.shape))
+    near = lax.all_to_all(payload, ("sub", "blk"), 0, 0, tiled=True)
     fold = pltpu.VMEM((blocks.shape[1], LANES), jnp.float32)
-    params = pltpu.CompilerParams(vmem_limit_bytes=40 * 1024 * 1024)
-
-    near = lax.all_gather(jnp.concatenate([start, local_map.astype(jnp.float32)], 0), ("sub", "blk"))
     partial = pl.pallas_call(
         first_kernel,
-        out_shape=jax.ShapeDtypeStruct((rows, LANES), jnp.float32),
+        out_shape=rowed(subs * parts, rows),
         in_specs=[vmem, vmem, vmem, vmem, smem, vmem],
         out_specs=vmem,
-        scratch_shapes=[fold],
+        scratch_shapes=[fold, pltpu.VMEM((rows, LANES), jnp.float32)],
         compiler_params=params,
         name="first_image",
     )(near, blocks, pattern, local_map, neighbours, coupling)
-    images = lax.all_gather(partial, ("sub", "blk"))
+    images = lax.all_to_all(partial, ("sub", "blk"), 0, 0, tiled=True)
     partial, image = pl.pallas_call(
         second_kernel,
-        out_shape=(
-            jax.ShapeDtypeStruct((rows + SUBL, LANES), jnp.float32),
-            jax.ShapeDtypeStruct((own_rows, LANES), jnp.float32),
-        ),
+        out_shape=(rowed(rows + SUBL), rowed(own_rows)),
         in_specs=[vmem, vmem, vmem, vmem, vmem, smem, vmem],
         out_specs=(vmem, vmem),
         scratch_shapes=[fold],
         compiler_params=params,
         name="second_image",
     )(near, images, blocks, pattern, local_map, neighbours, coupling)
-    everything = lax.all_gather(partial, ("rep", "sub", "blk"))
+    pair = lax.all_gather(partial, "blk")
+    sums, again = pl.pallas_call(
+        pair_kernel,
+        out_shape=(rowed(reps * subs, SUBL), rowed(own_rows)),
+        in_specs=[vmem],
+        out_specs=(vmem, vmem),
+        compiler_params=params,
+        name="pair_sums",
+    )(pair)
+    sums = lax.all_to_all(sums, ("rep", "sub"), 0, 0, tiled=True)
     second, third, entries = pl.pallas_call(
         functools.partial(last_kernel, float(cells)),
-        out_shape=(
-            jax.ShapeDtypeStruct((own_rows, LANES), jnp.float32),
-            jax.ShapeDtypeStruct((own_rows, LANES), jnp.float32),
-            jax.ShapeDtypeStruct((1, 5), jnp.float32),
-        ),
-        in_specs=[vmem, vmem, vmem],
+        out_shape=(rowed(own_rows), rowed(own_rows), jax.ShapeDtypeStruct((1, 5), jnp.float32)),
+        in_specs=[vmem] * 4,
         out_specs=(vmem, vmem, vmem),
         compiler_params=params,
         name="arnoldi_entries",
-    )(start, image, everything)
+    )(start, image, again, sums)
     return second.reshape(start_vector.shape), third.reshape(start_vector.shape), entries.reshape(5)
 
 

time: 136 us -> 44.6 us (0.33)
  blocking collectives: 130 us -> 37 us
    all_gather x3 -> x1, blocking collectives: 130 us -> 4.4 us  [per_device(): pair = lax.all_gather(partial, 'blk')]
    all_to_all x0 -> x3, blocking collectives: none -> 32.6 us  [the longest x1 14 us: per_device(): near = lax.all_to_all(payload, ('sub', 'blk'), 0, 0, tiled=True)]
    pallas_call x3 -> x4, Pallas kernels: 3.27 us -> 3.28 us  [the longest x1 1.26 us: per_device(): pl.pallas_call(second_kernel, out_shape=(rowed(rows + SUBL), rowed(own_ro...]
where the time goes in v2:
time: 44.6 us; the launch traced here: 44.2 us
  blocking collectives  37 us (83%)
  Pallas kernels  3.28 us (7%)
  local copies, waits for them, and re-layouts  1.95 us (4%)
  other arithmetic  1.35 us (3%)
  between operations  0.66 us (1%)
    all_to_all x1, blocking collectives, per_device(): near = lax.all_to_all(payload, ('sub', 'blk'), 0, 0, tiled=True)  14 us
    all_to_all x1, blocking collectives, per_device(): sums = lax.all_to_all(sums, ('rep', 'sub'), 0, 0, tiled=True)  9.3 us
    all_to_all x1, blocking collectives, per_device(): images = lax.all_to_all(partial, ('sub', 'blk'), 0, 0, tiled=True)  9.29 us
    all_gather x1, blocking collectives, per_device(): pair = lax.all_gather(partial, 'blk')  4.4 us
    unnamed x12, local copies, waits for them, and re-layouts  1.94 us
    pallas_call x1, Pallas kernels, per_device(): pl.pallas_call(second_kernel, out_shape=(rowed(rows + SUBL), rowed(own_ro...  1.26 us
    pallas_call x1, Pallas kernels, per_device(): pl.pallas_call(first_kernel, out_shape=rowed(subs * parts, rows), in_spec...  1.25 us

profile of v2, /device:TPU:0, one launch (start us, length us, event | category | flops | bytes accessed | tf_op | source)
XLA Modules:
  0.0 44.2 jit_solution(3820319706680421746)
XLA Ops:
  0.6 0.7 %bitcast_convert_fusion = f32[1,128]{1,0:T(1,128)S(1)} fusion(s32[1,1,128]{2,1,0:T(1,128)} %param.9), kind=kLoop, calls=%fused_computation.2 | loop fusion | flops 128 | bytes 1024 | tf_op jit(solution)/shard_map/convert_element_type | solution.py:217
  1.3 0.7 %select_maximum_fusion = f32[16,128]{1,0:T(8,128)S(1)} fusion(f32[1,128]{1,0:T(1,128)S(1)} %bitcast_convert_fusion, f32[8,128]{1,0:T(8,128)} %bitcast.16), kind=kLoop, calls=%fused_computation | loop fusion | flops 8192 | bytes 12800 | tf_op jit(solution)/shard_map/concatenate | solution.py:217
  2.0 14.0 %all_to_all.15.near_ref = f32[8,16,128]{2,1,0:T(8,128)S(1)} all-to-all(f32[8,16,128]{2,1,0:T(8,128)S(1)} %broadcast_in_dim.3), channel_id=1, replica_groups=mesh['sub'=4,'blk'=2,'rep'=4] {'sub','blk'}, dimensions={0} | all-to-all | bytes 131072 | tf_op jit(solution)/shard_map/all_to_all | solution.py:220
  16.0 0.0 copy-start.1
  16.0 0.0 copy-start.5
  16.0 0.0 copy-start.3
  16.0 0.0 copy-start.4
  16.0 0.7 %copy-done.1 = s32[1,1,8,32]{3,2,1,0:T(8,128)S(1)} copy-done((s32[1,1,8,32]{3,2,1,0:T(8,128)S(1)}, s32[1,1,8,32]{3,2,1,0:T(8,128)}, u32[]{:S(2)}) %copy-start.1) | copy-done | bytes 1048
  16.7 0.0 copy-done.5
  16.7 0.0 copy-done.3
  16.7 0.0 copy-done.4
  16.7 0.0 copy-start
  16.7 1.2 %copy-done = bf16[1,1,4,32,4096]{4,3,2,1,0:T(8,128)(2,1)S(1)} copy-done((bf16[1,1,4,32,4096]{4,3,2,1,0:T(8,128)(2,1)S(1)}, bf16[1,1,4,32,4096]{4,3,2,1,0:T(8,128)(2,1)}, u32[]{:S(2)}) %copy-start) | copy-done | bytes 1048600
  17.9 1.3 %first_image.1 = f32[8,16,128]{2,1,0:T(8,128)S(1)} custom-call(f32[8,16,128]{2,1,0:T(8,128)S(1)} %all_to_all.15.near_ref, bf16[4,32,4096]{2,1,0:T(8,128)(2,1)S(1)} %bitcast.11, s32[8,32]{1,0:T(8,128)S(1)} %bitcast.14, s32[1,128]{1,0:T(1,128)S(1)} %bitcast.20, s32[2]{0:T(128)S(1)} %bitcast.22, f32[2,128]{1,0:T(2,128)S(1)} %bitcast.18), custom_call_target="tpu_custom_call" | custom-call | tf_op jit(solution)/shard_map/first_image/pallas_call | solution.py:222
  19.2 9.3 %all_to_all.16.image_ref = f32[8,16,128]{2,1,0:T(8,128)S(1)} all-to-all(f32[8,16,128]{2,1,0:T(8,128)S(1)} %first_image.1), channel_id=1, replica_groups=mesh['sub'=4,'blk'=2,'rep'=4] {'sub','blk'}, dimensions={0} | all-to-all | bytes 131072 | tf_op jit(solution)/shard_map/all_to_all | solution.py:231
  28.5 1.3 %second_image.1 = (f32[24,128]{1,0:T(8,128)S(1)}, f32[8,128]{1,0:T(8,128)S(1)}) custom-call(f32[8,16,128]{2,1,0:T(8,128)S(1)} %all_to_all.15.near_ref, f32[8,16,128]{2,1,0:T(8,128)S(1)} %all_to_all.16.image_ref, bf16[4,32,4096]{2,1,0:T(8,128)(2,1)S(1)} %bitcast.12, s32[8,32]{1,0:T(8,128)S(1)} %bitcast.15, s32[1,128]{1,0:T(1,128)S(1)} %bitcast.21, ...), custom_call_target="tpu_custom_call" | custom-call | tf_op jit(solution)/shard_map/second_image/pallas_call | solution.py:232
  29.7 4.4 %all-gather = f32[48,128]{1,0:T(8,128)S(1)} all-gather(f32[24,128]{1,0:T(8,128)S(1)} %get-tuple-element.11), channel_id=2, replica_groups=mesh['sub'=4,'blk'=2,'rep'=4] {'blk'}, dimensions={0}, use_global_device_ids=true | all-gather | bytes 36864 | tf_op jit(solution)/shard_map/all_gather | solution.py:241
  34.1 0.0 copy-start.2
  34.1 9.3 %all_to_all.17.sums_ref = f32[16,8,128]{2,1,0:T(8,128)S(1)} all-to-all(f32[16,8,128]{2,1,0:T(8,128)S(1)} %get-tuple-element.13), channel_id=1, replica_groups=mesh['sub'=4,'blk'=2,'rep'=4] {'rep','sub'}, dimensions={0} | all-to-all | bytes 131072 | tf_op jit(solution)/shard_map/all_to_all | solution.py:250
  43.5 0.0 copy-done.2
  43.5 0.8 %arnoldi_entries.1 = (f32[8,128]{1,0:T(8,128)}, f32[8,128]{1,0:T(8,128)}, f32[1,5]{1,0:T(1,128)}) custom-call(f32[8,128]{1,0:T(8,128)S(1)} %bitcast.17, f32[8,128]{1,0:T(8,128)S(1)} %get-tuple-element.10.own_ref, f32[8,128]{1,0:T(8,128)S(1)} %get-tuple-element.12.again_ref, f32[16,8,128]{2,1,0:T(8,128)S(1)} %all_to_all.17.sums_ref), custom_call_target="tpu_custom_call" | custom-call | tf_op jit(solution)/shard_map/arnoldi_entries/pallas_call | solution.py:251
  (2 shorter events, 0.0 us)
Async XLA Ops:
  16.0 0.7 %copy-start.1 = (s32[1,1,8,32]{3,2,1,0:T(8,128)S(1)}, s32[1,1,8,32]{3,2,1,0:T(8,128)}, u32[]{:S(2)}) copy-start(s32[1,1,8,32]{3,2,1,0:T(8,128)} %param.8) | copy-start | bytes 3076
  16.0 0.7 %copy-start.5 = (s32[1,1,2]{2,1,0:T(1,128)S(1)}, s32[1,1,2]{2,1,0:T(1,128)}, u32[]{:S(2)}) copy-start(s32[1,1,2]{2,1,0:T(1,128)} %param.10) | copy-start | bytes 28
  16.0 0.7 %copy-start.3 = (f32[1,1,2,128]{3,2,1,0:T(2,128)S(1)}, f32[1,1,2,128]{3,2,1,0:T(2,128)}, u32[]{:S(2)}) copy-start(f32[1,1,2,128]{3,2,1,0:T(2,128)} %param.11) | copy-start | bytes 3076
  16.0 0.7 %copy-start.4 = (s32[1,1,128]{2,1,0:T(1,128)S(1)}, s32[1,1,128]{2,1,0:T(1,128)}, u32[]{:S(2)}) copy-start(s32[1,1,128]{2,1,0:T(1,128)} %param.9) | copy-start | bytes 1540
  16.7 1.2 %copy-start = (bf16[1,1,4,32,4096]{4,3,2,1,0:T(8,128)(2,1)S(1)}, bf16[1,1,4,32,4096]{4,3,2,1,0:T(8,128)(2,1)}, u32[]{:S(2)}) copy-start(bf16[1,1,4,32,4096]{4,3,2,1,0:T(8,128)(2,1)} %param.7) | copy-start | bytes 3145732
  34.1 9.3 %copy-start.2 = (f32[1,1,1024]{2,1,0:T(1,128)S(1)}, f32[1,1,1024]{2,1,0:T(1,128)}, u32[]{:S(2)}) copy-start(f32[1,1,1024]{2,1,0:T(1,128)} %param.6) | copy-start | bytes 12292

commit v3 on v2

--- a/solution.py
+++ b/solution.py
@@ -29,8 +29,19 @@
     return lax.broadcasted_iota(jnp.int32, shape, 0)
 
 
-def block_product(vector, blocks_ref, pattern_ref, first_slot, fold_ref):
-    slots, block_rows, width = blocks_ref.shape
+def start_blocks(blocks_ref, held_ref, sems):
+    count = sems.shape[0]
+    step = blocks_ref.shape[2] // count
+    copies = []
+    for i in range(count):
+        part = pl.ds(i * step, step)
+        copies.append(pltpu.make_async_copy(blocks_ref.at[:, :, part], held_ref.at[:, :, part], sems.at[i]))
+        copies[-1].start()
+    return copies
+
+
+def block_product(vector, held_ref, copies, pattern_ref, first_slot, fold_ref):
+    slots, block_rows, width = held_ref.shape
     half = block_rows // 2
     lower = lane_iota(vector.shape) < BS
     turned = pltpu.roll(vector, BS, 1)
@@ -50,10 +61,13 @@
     ones = ones.astype(jnp.float32).astype(jnp.bfloat16)
     pair = (lane_iota((block_rows, LANES)) % BS) // 2
     result = jnp.zeros((block_rows, LANES), jnp.float32)
+    pieces_each = width // LANES // len(copies)
     for c in range(width // LANES):
+        if c % pieces_each == 0:
+            copies[c // pieces_each].wait()
         total = None
         for k in range(slots):
-            term = blocks_ref[k, :, pl.ds(c * LANES, LANES)].astype(jnp.float32) * picked[k]
+            term = held_ref[k, :, pl.ds(c * LANES, LANES)].astype(jnp.float32) * picked[k]
             total = term if total is None else total + term
         high = total.astype(jnp.bfloat16)
         low = (total - high.astype(jnp.float32)).astype(jnp.bfloat16)
@@ -85,56 +99,83 @@
     return landed[0:count] + landed[count : 2 * count] + landed[2 * count : 3 * count]
 
 
-def first_kernel(near_ref, blocks_ref, pattern_ref, map_ref, neighbours_ref, coupling_ref, out_ref, fold_ref, sum_ref):
-    rows = sum_ref.shape[0]
-    parts = lax.axis_size("blk")
-    own_rows = rows // parts
+def first_kernel(
+    pair_ref, blocks_ref, pattern_ref, map_ref, neighbours_ref, coupling_ref, out_ref, held_ref, sems, fold_ref
+):
+    copies = start_blocks(blocks_ref, held_ref, sems)
+    parts, own_rows, _ = pair_ref.shape
+    rows = parts * own_rows
+    blk = lax.axis_index("blk")
+    places = map_ref[...]
+    count = coupling_ref.shape[0]
+    lines = [take_trace(pair_ref[blk], places - blk * own_rows * LANES), places.astype(jnp.float32)]
+    lines += [coupling_ref[n : n + 1, :] for n in range(count)]
+    lines += [jnp.full((1, LANES), neighbours_ref[n], jnp.int32).astype(jnp.float32) for n in range(count)]
+    lines += [jnp.zeros((out_ref.shape[1] - rows - len(lines), LANES), jnp.float32)]
+    lines = jnp.concatenate(lines, 0)
+    vector = jnp.concatenate([pair_ref[b] for b in range(parts)], 0)
+    partial = block_product(vector, held_ref, copies, pattern_ref, blk * held_ref.shape[0], fold_ref)
+    for device in range(out_ref.shape[0]):
+        out_ref[device, 0:rows, :] = partial
+        out_ref[device, rows : rows + SUBL, :] = lines
+
+
+def second_kernel(
+    pair_ref,
+    group_ref,
+    blocks_ref,
+    pattern_ref,
+    map_ref,
+    neighbours_ref,
+    coupling_ref,
+    out_ref,
+    own_ref,
+    held_ref,
+    sems,
+    fold_ref,
+    image_ref,
+):
+    copies = start_blocks(blocks_ref, held_ref, sems)
+    parts, own_rows, _ = pair_ref.shape
+    rows = parts * own_rows
+    count = coupling_ref.shape[0]
+    subs = lax.axis_size("sub")
     sub, blk = lax.axis_index("sub"), lax.axis_index("blk")
-    first_cell = blk * own_rows * LANES
-    vector = jnp.concatenate([near_ref[sub * parts + b, 0:own_rows, :] for b in range(parts)], 0)
-    sum_ref[...] = block_product(vector, blocks_ref, pattern_ref, blk * blocks_ref.shape[0], fold_ref)
+    own = pl.ds(pl.multiple_of(blk * own_rows, SUBL), own_rows)
+
+    def line(sub_at, part, i):
+        return group_ref[sub_at * parts + part, rows + i : rows + i + 1, :]
+
+    def landed(sub_at, part):
+        traces = jnp.concatenate([line(other, part, 0) for other in range(subs)], 0)
+        names = row_iota(traces.shape).astype(jnp.float32)
+        inflow = jnp.zeros((1, LANES), jnp.float32)
+        for n in range(count):
+            chosen = jnp.where(names == line(sub_at, part, 2 + count + n), traces, 0.0)
+            inflow = inflow + line(sub_at, part, 2 + n) * jnp.sum(chosen, axis=0, keepdims=True)
+        places = line(sub_at, part, 1).astype(jnp.int32) - part * own_rows * LANES
+        return spread(inflow, places, own_rows), places
+
+    def summed(index, where):
+        total = group_ref[index * parts, where, :]
+        for b in range(1, parts):
+            total = total + group_ref[index * parts + b, where, :]
+        return total
+
+    added = jnp.concatenate([landed(sub, b)[0] for b in range(parts)], 0)
+    image = summed(sub, pl.ds(0, rows)) + added
+    image_ref[...] = image
+    second = block_product(image, held_ref, copies, pattern_ref, blk * held_ref.shape[0], fold_ref)
     inflow = jnp.zeros((1, LANES), jnp.float32)
-    for n in range(coupling_ref.shape[0]):
-        source = neighbours_ref[n] * parts + blk
-        places = near_ref[source, own_rows : own_rows + 1, :].astype(jnp.int32) - first_cell
-        trace = take_trace(near_ref[source, 0:own_rows, :], places)
-        inflow = inflow + coupling_ref[n : n + 1, :] * trace
-    own = pl.ds(pl.multiple_of(blk * own_rows, SUBL), own_rows)
-    sum_ref[own, :] = sum_ref[own, :] + spread(inflow, map_ref[...] - first_cell, own_rows)
-    partial = sum_ref[...]
-    for device in range(out_ref.shape[0]):
-        out_ref[device] = partial
-
-
-def second_kernel(
-    near_ref, image_ref, blocks_ref, pattern_ref, map_ref, neighbours_ref, coupling_ref, out_ref, own_ref, fold_ref
-):
-    rows = image_ref.shape[1]
-    parts = lax.axis_size("blk")
-    own_rows = rows // parts
-    sub, blk = lax.axis_index("sub"), lax.axis_index("blk")
-    first_cell = blk * own_rows * LANES
-    own = pl.ds(pl.multiple_of(blk * own_rows, SUBL), own_rows)
-
-    def summed(index, where):
-        total = image_ref[index * parts, where, :]
-        for b in range(1, parts):
-            total = total + image_ref[index * parts + b, where, :]
-        return total
-
-    vector = jnp.concatenate([near_ref[sub * parts + b, 0:own_rows, :] for b in range(parts)], 0)
-    image = summed(sub, pl.ds(0, rows))
-    out_ref[0:rows, :] = block_product(image, blocks_ref, pattern_ref, blk * blocks_ref.shape[0], fold_ref)
-    inflow = jnp.zeros((1, LANES), jnp.float32)
-    for n in range(coupling_ref.shape[0]):
+    for n in range(count):
         source = neighbours_ref[n]
-        places = near_ref[source * parts + blk, own_rows : own_rows + 1, :].astype(jnp.int32) - first_cell
-        trace = take_trace(summed(source, own), places)
-        inflow = inflow + coupling_ref[n : n + 1, :] * trace
-    out_ref[own, :] = out_ref[own, :] + spread(inflow, map_ref[...] - first_cell, own_rows)
+        added, places = landed(source, blk)
+        inflow = inflow + coupling_ref[n : n + 1, :] * take_trace(summed(source, own) + added, places)
+    out_ref[0:rows, :] = second
+    out_ref[own, :] = out_ref[own, :] + spread(inflow, map_ref[...] - blk * own_rows * LANES, own_rows)
     second = out_ref[0:rows, :]
-    vector_own = near_ref[sub * parts + blk, 0:own_rows, :]
-    image_own = summed(sub, own)
+    vector = jnp.concatenate([pair_ref[b] for b in range(parts)], 0)
+    vector_own, image_own = pair_ref[blk], image_ref[own, :]
     own_ref[...] = image_own
 
     def down(left, right):
@@ -160,6 +201,9 @@
         total = total + pair_ref[b]
     square = jnp.sum(total[0:rows] * total[0:rows], axis=0, keepdims=True)
     sums = jnp.where(row_iota((SUBL, LANES)) == 5, square, total[rows:height])
+    sums = jnp.sum(sums, axis=1, keepdims=True)
+    sums = jnp.where(row_iota((SUBL, LANES)) == lane_iota((SUBL, LANES)), sums, 0.0)
+    sums = jnp.sum(sums, axis=0, keepdims=True)
     for device in range(out_ref.shape[0]):
         out_ref[device] = sums
     own = pl.ds(pl.multiple_of(lax.axis_index("blk") * own_rows, SUBL), own_rows)
@@ -170,10 +214,10 @@
 
 
 def last_kernel(cells, start_ref, own_ref, again_ref, sums_ref, second_ref, third_ref, entries_ref):
-    sums = jnp.sum(sums_ref[...], axis=0)
+    sums = jnp.sum(sums_ref[...], axis=0) / cells
 
     def whole(i):
-        return jnp.broadcast_to(jnp.sum(sums[i : i + 1, :], axis=1, keepdims=True), (1, LANES)) / cells
+        return jnp.broadcast_to(sums[:, i : i + 1], (1, LANES))
 
     vv, vw, ww, vy, wy, yy = (whole(i) for i in range(6))
     norm_square = vv + epsilon
@@ -214,39 +258,39 @@
     def rowed(*shape):
         return jax.ShapeDtypeStruct((*shape, LANES), jnp.float32)
 
-    payload = jnp.concatenate([start, local_map.astype(jnp.float32)], 0)
-    payload = jnp.pad(payload, ((0, SUBL - 1), (0, 0)))
-    payload = jnp.broadcast_to(payload, (subs * parts, *payload.shape))
-    near = lax.all_to_all(payload, ("sub", "blk"), 0, 0, tiled=True)
+    pair = lax.all_gather(start, "blk")
+    chunks = 8
     fold = pltpu.VMEM((blocks.shape[1], LANES), jnp.float32)
+    held = [pltpu.VMEM(blocks.shape, jnp.bfloat16), pltpu.SemaphoreType.DMA((chunks,))]
+    anywhere = pl.BlockSpec(memory_space=pl.ANY)
     partial = pl.pallas_call(
         first_kernel,
-        out_shape=rowed(subs * parts, rows),
-        in_specs=[vmem, vmem, vmem, vmem, smem, vmem],
+        out_shape=rowed(subs * parts, rows + SUBL),
+        in_specs=[vmem, anywhere, vmem, vmem, smem, vmem],
         out_specs=vmem,
-        scratch_shapes=[fold, pltpu.VMEM((rows, LANES), jnp.float32)],
+        scratch_shapes=[*held, fold],
         compiler_params=params,
         name="first_image",
-    )(near, blocks, pattern, local_map, neighbours, coupling)
-    images = lax.all_to_all(partial, ("sub", "blk"), 0, 0, tiled=True)
+    )(pair, blocks, pattern, local_map, neighbours, coupling)
+    group = lax.all_to_all(partial, ("sub", "blk"), 0, 0, tiled=True)
     partial, image = pl.pallas_call(
         second_kernel,
         out_shape=(rowed(rows + SUBL), rowed(own_rows)),
-        in_specs=[vmem, vmem, vmem, vmem, vmem, smem, vmem],
+        in_specs=[vmem, vmem, anywhere, vmem, vmem, smem, vmem],
         out_specs=(vmem, vmem),
-        scratch_shapes=[fold],
+        scratch_shapes=[*held, fold, pltpu.VMEM((rows, LANES), jnp.float32)],
         compiler_params=params,
         name="second_image",
-    )(near, images, blocks, pattern, local_map, neighbours, coupling)
-    pair = lax.all_gather(partial, "blk")
+    )(pair, group, blocks, pattern, local_map, neighbours, coupling)
+    both = lax.all_gather(partial, "blk")
     sums, again = pl.pallas_call(
         pair_kernel,
-        out_shape=(rowed(reps * subs, SUBL), rowed(own_rows)),
+        out_shape=(rowed(reps * subs, 1), rowed(own_rows)),
         in_specs=[vmem],
         out_specs=(vmem, vmem),
         compiler_params=params,
         name="pair_sums",
-    )(pair)
+    )(both)
     sums = lax.all_to_all(sums, ("rep", "sub"), 0, 0, tiled=True)
     second, third, entries = pl.pallas_call(
         functools.partial(last_kernel, float(cells)),

time: 44.6 us -> 41.6 us (0.933)
  blocking collectives: 37 us -> 32.1 us
  Pallas kernels: 3.28 us -> 5.87 us
  other arithmetic: 1.35 us -> 0 us
  local copies, waits for them, and re-layouts: 1.95 us -> 2.61 us
    all_to_all x2 -> x1, blocking collectives: 23.3 us -> 13.2 us  [per_device(): group = lax.all_to_all(partial, ('sub', 'blk'), 0, 0, tiled=True)]
    all_gather x1 -> x2, blocking collectives: 4.4 us -> 9.86 us  [the longest x1 5.46 us: per_device(): pair = lax.all_gather(start, 'blk')]
    pallas_call x1, Pallas kernels: 1.26 us -> 2.74 us  [per_device(): pl.pallas_call(second_kernel, out_shape=(rowed(rows + SUBL), rowed(own_ro...]
    pallas_call x2, Pallas kernels: 1.27 us -> 2.4 us  [the longest x1 2.3 us: per_device(): pl.pallas_call(first_kernel, out_shape=rowed(subs * parts, rows + SUBL),...]
    concatenate x1 -> x0, other arithmetic: 0.69 us -> none  [per_device(): payload = jnp.concatenate([start, local_map.astype(jnp.float32)], 0)]
    unnamed x12, local copies, waits for them, and re-layouts: 1.94 us -> 2.61 us
    convert_element_type x1 -> x0, other arithmetic: 0.66 us -> none  [per_device(): payload = jnp.concatenate([start, local_map.astype(jnp.float32)], 0)]
where the time goes in v3:
time: 41.6 us; the launch traced here: 41.3 us
  blocking collectives  32.1 us (77%)
  Pallas kernels  5.87 us (14%)
  local copies, waits for them, and re-layouts  2.61 us (6%)
  between operations  0.66 us (2%)
    all_to_all x1, blocking collectives, per_device(): group = lax.all_to_all(partial, ('sub', 'blk'), 0, 0, tiled=True)  13.2 us
    all_to_all x1, blocking collectives, per_device(): sums = lax.all_to_all(sums, ('rep', 'sub'), 0, 0, tiled=True)  9.03 us
    all_gather x1, blocking collectives, per_device(): pair = lax.all_gather(start, 'blk')  5.46 us
    all_gather x1, blocking collectives, per_device(): both = lax.all_gather(partial, 'blk')  4.4 us
    pallas_call x1, Pallas kernels, per_device(): pl.pallas_call(second_kernel, out_shape=(rowed(rows + SUBL), rowed(own_ro...  2.74 us
    unnamed x12, local copies, waits for them, and re-layouts  2.61 us
    pallas_call x1, Pallas kernels, per_device(): pl.pallas_call(first_kernel, out_shape=rowed(subs * parts, rows + SUBL),...  2.3 us

profile of v3, /device:TPU:0, one launch (start us, length us, event | category | flops | bytes accessed | tf_op | source)
XLA Modules:
  0.0 41.3 jit_solution(17614605475348960449)
XLA Ops:
  0.6 5.5 %all_gather.9.pair_ref = f32[2,8,128]{2,1,0:T(8,128)S(1)} all-gather(f32[1,8,128]{2,1,0:T(8,128)} %bitcast.16), channel_id=1, replica_groups=mesh['sub'=4,'blk'=2,'rep'=4] {'blk'}, dimensions={0}, use_global_device_ids=true | all-gather | bytes 12288 | tf_op jit(solution)/shard_map/all_gather | solution.py:261
  6.1 0.0 copy-start.1
  6.1 0.0 copy-start.5
  6.1 0.0 copy-start.3
  6.1 0.0 copy-start.4
  6.1 0.7 %copy-done.1 = s32[1,1,8,32]{3,2,1,0:T(8,128)S(1)} copy-done((s32[1,1,8,32]{3,2,1,0:T(8,128)S(1)}, s32[1,1,8,32]{3,2,1,0:T(8,128)}, u32[]{:S(2)}) %copy-start.1) | copy-done | bytes 1048
  6.8 0.0 copy-done.5
  6.8 0.0 copy-done.3
  6.8 0.0 copy-done.4
  6.8 0.0 copy-start
  6.8 1.2 %copy-done = bf16[1,1,4,32,4096]{4,3,2,1,0:T(8,128)(2,1)S(1)} copy-done((bf16[1,1,4,32,4096]{4,3,2,1,0:T(8,128)(2,1)S(1)}, bf16[1,1,4,32,4096]{4,3,2,1,0:T(8,128)(2,1)}, u32[]{:S(2)}) %copy-start) | copy-done | bytes 1048600
  8.0 2.3 %first_image.1 = f32[8,24,128]{2,1,0:T(8,128)S(1)} custom-call(f32[2,8,128]{2,1,0:T(8,128)S(1)} %all_gather.9.pair_ref, bf16[4,32,4096]{2,1,0:T(8,128)(2,1)S(1)} %bitcast.11, s32[8,32]{1,0:T(8,128)S(1)} %bitcast.14, s32[1,128]{1,0:T(1,128)S(1)} %bitcast.20, s32[2]{0:T(128)S(1)} %bitcast.22, f32[2,128]{1,0:T(2,128)S(1)} %bitcast.18), custom_call_target="tpu_custom_call" | custom-call | tf_op jit(solution)/shard_map/first_image/pallas_call | solution.py:266
  10.3 13.2 %all_to_all.10.group_ref = f32[8,24,128]{2,1,0:T(8,128)S(1)} all-to-all(f32[8,24,128]{2,1,0:T(8,128)S(1)} %first_image.1), channel_id=1, replica_groups=mesh['sub'=4,'blk'=2,'rep'=4] {'sub','blk'}, dimensions={0} | all-to-all | bytes 196608 | tf_op jit(solution)/shard_map/all_to_all | solution.py:275
  23.6 2.7 %second_image.1 = (f32[24,128]{1,0:T(8,128)S(1)}, f32[8,128]{1,0:T(8,128)S(1)}) custom-call(f32[2,8,128]{2,1,0:T(8,128)S(1)} %all_gather.9.pair_ref, f32[8,24,128]{2,1,0:T(8,128)S(1)} %all_to_all.10.group_ref, bf16[4,32,4096]{2,1,0:T(8,128)(2,1)S(1)} %bitcast.12, s32[8,32]{1,0:T(8,128)S(1)} %bitcast.15, s32[1,128]{1,0:T(1,128)S(1)} %bitcast.21, ...), custom_call_target="tpu_custom_call" | custom-call | tf_op jit(solution)/shard_map/second_image/pallas_call | solution.py:276
  26.3 4.4 %all-gather = f32[48,128]{1,0:T(8,128)S(1)} all-gather(f32[24,128]{1,0:T(8,128)S(1)} %get-tuple-element.11), channel_id=2, replica_groups=mesh['sub'=4,'blk'=2,'rep'=4] {'blk'}, dimensions={0}, use_global_device_ids=true | all-gather | bytes 36864 | tf_op jit(solution)/shard_map/all_gather | solution.py:285
  30.7 0.1 pair_sums.1
  30.8 9.0 %all_to_all.11.sums_ref = f32[16,1,128]{2,1,0:T(1,128)S(1)} all-to-all(f32[16,1,128]{2,1,0:T(1,128)S(1)} %get-tuple-element.13), channel_id=1, replica_groups=mesh['sub'=4,'blk'=2,'rep'=4] {'rep','sub'}, dimensions={0} | all-to-all | bytes 16384 | tf_op jit(solution)/shard_map/all_to_all | solution.py:294
  39.8 0.0 copy-start.2
  39.8 0.7 %copy-done.2 = f32[1,1,1024]{2,1,0:T(1,128)S(1)} copy-done((f32[1,1,1024]{2,1,0:T(1,128)S(1)}, f32[1,1,1024]{2,1,0:T(1,128)}, u32[]{:S(2)}) %copy-start.2) | copy-done | bytes 4120
  40.5 0.7 %arnoldi_entries.1 = (f32[8,128]{1,0:T(8,128)}, f32[8,128]{1,0:T(8,128)}, f32[1,5]{1,0:T(1,128)}) custom-call(f32[8,128]{1,0:T(8,128)S(1)} %bitcast.17, f32[8,128]{1,0:T(8,128)S(1)} %get-tuple-element.10.own_ref, f32[8,128]{1,0:T(8,128)S(1)} %get-tuple-element.12.again_ref, f32[16,1,128]{2,1,0:T(1,128)S(1)} %all_to_all.11.sums_ref), custom_call_target="tpu_custom_call" | custom-call | tf_op jit(solution)/shard_map/arnoldi_entries/pallas_call | solution.py:295
Async XLA Ops:
  6.1 0.7 %copy-start.1 = (s32[1,1,8,32]{3,2,1,0:T(8,128)S(1)}, s32[1,1,8,32]{3,2,1,0:T(8,128)}, u32[]{:S(2)}) copy-start(s32[1,1,8,32]{3,2,1,0:T(8,128)} %param.8) | copy-start | bytes 3076
  6.1 0.7 %copy-start.5 = (s32[1,1,2]{2,1,0:T(1,128)S(1)}, s32[1,1,2]{2,1,0:T(1,128)}, u32[]{:S(2)}) copy-start(s32[1,1,2]{2,1,0:T(1,128)} %param.10) | copy-start | bytes 28
  6.1 0.7 %copy-start.3 = (f32[1,1,2,128]{3,2,1,0:T(2,128)S(1)}, f32[1,1,2,128]{3,2,1,0:T(2,128)}, u32[]{:S(2)}) copy-start(f32[1,1,2,128]{3,2,1,0:T(2,128)} %param.11) | copy-start | bytes 3076
  6.1 0.7 %copy-start.4 = (s32[1,1,128]{2,1,0:T(1,128)S(1)}, s32[1,1,128]{2,1,0:T(1,128)}, u32[]{:S(2)}) copy-start(s32[1,1,128]{2,1,0:T(1,128)} %param.9) | copy-start | bytes 1540
  6.8 1.2 %copy-start = (bf16[1,1,4,32,4096]{4,3,2,1,0:T(8,128)(2,1)S(1)}, bf16[1,1,4,32,4096]{4,3,2,1,0:T(8,128)(2,1)}, u32[]{:S(2)}) copy-start(bf16[1,1,4,32,4096]{4,3,2,1,0:T(8,128)(2,1)} %param.7) | copy-start | bytes 3145732
  39.8 0.7 %copy-start.2 = (f32[1,1,1024]{2,1,0:T(1,128)S(1)}, f32[1,1,1024]{2,1,0:T(1,128)}, u32[]{:S(2)}) copy-start(f32[1,1,1024]{2,1,0:T(1,128)} %param.6) | copy-start | bytes 12292

commit v4 on v3

--- a/solution.py
+++ b/solution.py
@@ -29,19 +29,8 @@
     return lax.broadcasted_iota(jnp.int32, shape, 0)
 
 
-def start_blocks(blocks_ref, held_ref, sems):
-    count = sems.shape[0]
-    step = blocks_ref.shape[2] // count
-    copies = []
-    for i in range(count):
-        part = pl.ds(i * step, step)
-        copies.append(pltpu.make_async_copy(blocks_ref.at[:, :, part], held_ref.at[:, :, part], sems.at[i]))
-        copies[-1].start()
-    return copies
-
-
-def block_product(vector, held_ref, copies, pattern_ref, first_slot, fold_ref):
-    slots, block_rows, width = held_ref.shape
+def block_product(vector, blocks_ref, pattern_ref, first_slot, fold_ref):
+    slots, block_rows, width = blocks_ref.shape
     half = block_rows // 2
     lower = lane_iota(vector.shape) < BS
     turned = pltpu.roll(vector, BS, 1)
@@ -61,13 +50,10 @@
     ones = ones.astype(jnp.float32).astype(jnp.bfloat16)
     pair = (lane_iota((block_rows, LANES)) % BS) // 2
     result = jnp.zeros((block_rows, LANES), jnp.float32)
-    pieces_each = width // LANES // len(copies)
     for c in range(width // LANES):
-        if c % pieces_each == 0:
-            copies[c // pieces_each].wait()
         total = None
         for k in range(slots):
-            term = held_ref[k, :, pl.ds(c * LANES, LANES)].astype(jnp.float32) * picked[k]
+            term = blocks_ref[k, :, pl.ds(c * LANES, LANES)].astype(jnp.float32) * picked[k]
             total = term if total is None else total + term
         high = total.astype(jnp.bfloat16)
         low = (total - high.astype(jnp.float32)).astype(jnp.bfloat16)
@@ -99,48 +85,38 @@
     return landed[0:count] + landed[count : 2 * count] + landed[2 * count : 3 * count]
 
 
-def first_kernel(
-    pair_ref, blocks_ref, pattern_ref, map_ref, neighbours_ref, coupling_ref, out_ref, held_ref, sems, fold_ref
-):
-    copies = start_blocks(blocks_ref, held_ref, sems)
-    parts, own_rows, _ = pair_ref.shape
-    rows = parts * own_rows
-    blk = lax.axis_index("blk")
+def lines_kernel(start_ref, map_ref, near_ref, coupling_ref, out_ref):
     places = map_ref[...]
     count = coupling_ref.shape[0]
-    lines = [take_trace(pair_ref[blk], places - blk * own_rows * LANES), places.astype(jnp.float32)]
+    first_cell = lax.axis_index("blk") * start_ref.shape[0] * LANES
+    lines = [take_trace(start_ref[...], places - first_cell), places.astype(jnp.float32)]
     lines += [coupling_ref[n : n + 1, :] for n in range(count)]
-    lines += [jnp.full((1, LANES), neighbours_ref[n], jnp.int32).astype(jnp.float32) for n in range(count)]
-    lines += [jnp.zeros((out_ref.shape[1] - rows - len(lines), LANES), jnp.float32)]
-    lines = jnp.concatenate(lines, 0)
-    vector = jnp.concatenate([pair_ref[b] for b in range(parts)], 0)
-    partial = block_product(vector, held_ref, copies, pattern_ref, blk * held_ref.shape[0], fold_ref)
+    near = near_ref[...].astype(jnp.float32)
+    lines += [jnp.broadcast_to(near[:, n : n + 1], (1, LANES)) for n in range(count)]
+    lines += [jnp.zeros((SUBL - len(lines), LANES), jnp.float32)]
+    out_ref[...] = jnp.concatenate(lines, 0)
+
+
+def first_kernel(start_ref, lines_ref, other_ref, blocks_ref, pattern_ref, out_ref, vector_ref, fold_ref):
+    own_rows, rows = start_ref.shape[0], vector_ref.shape[0]
+    blk, parts = lax.axis_index("blk"), lax.axis_size("blk")
+    for step in range(parts):
+        place = lax.rem(blk + step, parts)
+        place = pl.ds(pl.multiple_of(place * own_rows, SUBL), own_rows)
+        vector_ref[place, :] = other_ref[step - 1] if step else start_ref[...]
+    partial = block_product(vector_ref[...], blocks_ref, pattern_ref, blk * blocks_ref.shape[0], fold_ref)
     for device in range(out_ref.shape[0]):
         out_ref[device, 0:rows, :] = partial
-        out_ref[device, rows : rows + SUBL, :] = lines
+        out_ref[device, rows : rows + SUBL, :] = lines_ref[...]
 
 
 def second_kernel(
-    pair_ref,
-    group_ref,
-    blocks_ref,
-    pattern_ref,
-    map_ref,
-    neighbours_ref,
-    coupling_ref,
-    out_ref,
-    own_ref,
-    held_ref,
-    sems,
-    fold_ref,
-    image_ref,
+    start_ref, vector_ref, group_ref, blocks_ref, pattern_ref, near_ref, out_ref, own_ref, fold_ref, image_ref
 ):
-    copies = start_blocks(blocks_ref, held_ref, sems)
-    parts, own_rows, _ = pair_ref.shape
-    rows = parts * own_rows
-    count = coupling_ref.shape[0]
-    subs = lax.axis_size("sub")
+    own_rows, rows = start_ref.shape[0], vector_ref.shape[0]
     sub, blk = lax.axis_index("sub"), lax.axis_index("blk")
+    subs, parts = lax.axis_size("sub"), lax.axis_size("blk")
+    count = near_ref.shape[1]
     own = pl.ds(pl.multiple_of(blk * own_rows, SUBL), own_rows)
 
     def line(sub_at, part, i):
@@ -165,17 +141,18 @@
     added = jnp.concatenate([landed(sub, b)[0] for b in range(parts)], 0)
     image = summed(sub, pl.ds(0, rows)) + added
     image_ref[...] = image
-    second = block_product(image, held_ref, copies, pattern_ref, blk * held_ref.shape[0], fold_ref)
+    second = block_product(image, blocks_ref, pattern_ref, blk * blocks_ref.shape[0], fold_ref)
     inflow = jnp.zeros((1, LANES), jnp.float32)
     for n in range(count):
-        source = neighbours_ref[n]
+        source = near_ref[0, n]
         added, places = landed(source, blk)
-        inflow = inflow + coupling_ref[n : n + 1, :] * take_trace(summed(source, own) + added, places)
+        inflow = inflow + line(sub, blk, 2 + n) * take_trace(summed(source, own) + added, places)
+    places = line(sub, blk, 1).astype(jnp.int32) - blk * own_rows * LANES
     out_ref[0:rows, :] = second
-    out_ref[own, :] = out_ref[own, :] + spread(inflow, map_ref[...] - blk * own_rows * LANES, own_rows)
+    out_ref[own, :] = out_ref[own, :] + spread(inflow, places, own_rows)
     second = out_ref[0:rows, :]
-    vector = jnp.concatenate([pair_ref[b] for b in range(parts)], 0)
-    vector_own, image_own = pair_ref[blk], image_ref[own, :]
+    vector = vector_ref[...]
+    vector_own, image_own = start_ref[...], image_ref[own, :]
     own_ref[...] = image_own
 
     def down(left, right):
@@ -250,38 +227,48 @@
     cells = own_cells * parts * subs * reps
     start = start_vector.reshape(own_rows, LANES)
     local_map = trace_map[0]
-    blocks, pattern, neighbours, coupling = blocks[0, 0], pattern[0, 0], neighbours[0, 0], coupling[0, 0]
+    blocks, pattern, neighbours, coupling = blocks[0, 0], pattern[0, 0], neighbours[0], coupling[0, 0]
     vmem = pl.BlockSpec(memory_space=pltpu.VMEM)
-    smem = pl.BlockSpec(memory_space=pltpu.SMEM)
-    params = pltpu.CompilerParams(vmem_limit_bytes=40 * 1024 * 1024)
+    params = pltpu.CompilerParams(vmem_limit_bytes=32 * 1024 * 1024)
 
     def rowed(*shape):
         return jax.ShapeDtypeStruct((*shape, LANES), jnp.float32)
 
-    pair = lax.all_gather(start, "blk")
-    chunks = 8
+    smem = pl.BlockSpec(memory_space=pltpu.SMEM)
+    others = [
+        lax.ppermute(start[None], "blk", [((i + step) % parts, i) for i in range(parts)])
+        for step in range(1, parts)
+    ]
+    others = others[0] if parts == 2 else jnp.concatenate(others, 0)
     fold = pltpu.VMEM((blocks.shape[1], LANES), jnp.float32)
-    held = [pltpu.VMEM(blocks.shape, jnp.bfloat16), pltpu.SemaphoreType.DMA((chunks,))]
-    anywhere = pl.BlockSpec(memory_space=pl.ANY)
-    partial = pl.pallas_call(
+    lines = pl.pallas_call(
+        lines_kernel,
+        out_shape=rowed(SUBL),
+        in_specs=[vmem] * 4,
+        out_specs=vmem,
+        compiler_params=params,
+        cost_estimate=pl.CostEstimate(flops=1 << 32, bytes_accessed=1 << 20, transcendentals=0),
+        name="group_lines",
+    )(start, local_map, neighbours, coupling)
+    partial, vector = pl.pallas_call(
         first_kernel,
-        out_shape=rowed(subs * parts, rows + SUBL),
-        in_specs=[vmem, anywhere, vmem, vmem, smem, vmem],
-        out_specs=vmem,
-        scratch_shapes=[*held, fold],
+        out_shape=(rowed(subs * parts, rows + SUBL), rowed(rows)),
+        in_specs=[vmem] * 5,
+        out_specs=(vmem, vmem),
+        scratch_shapes=[fold],
         compiler_params=params,
         name="first_image",
-    )(pair, blocks, pattern, local_map, neighbours, coupling)
+    )(start, lines, others, blocks, pattern)
     group = lax.all_to_all(partial, ("sub", "blk"), 0, 0, tiled=True)
     partial, image = pl.pallas_call(
         second_kernel,
         out_shape=(rowed(rows + SUBL), rowed(own_rows)),
-        in_specs=[vmem, vmem, anywhere, vmem, vmem, smem, vmem],
+        in_specs=[vmem, vmem, vmem, vmem, vmem, smem],
         out_specs=(vmem, vmem),
-        scratch_shapes=[*held, fold, pltpu.VMEM((rows, LANES), jnp.float32)],
+        scratch_shapes=[fold, pltpu.VMEM((rows, LANES), jnp.float32)],
         compiler_params=params,
         name="second_image",
-    )(pair, group, blocks, pattern, local_map, neighbours, coupling)
+    )(start, vector, group, blocks, pattern, neighbours)
     both = lax.all_gather(partial, "blk")
     sums, again = pl.pallas_call(
         pair_kernel,

time: 41.6 us -> 35.6 us (0.86)
  blocking collectives: 32.1 us -> 26.6 us
  starting transfers between devices: 0 us -> 3.03 us
  Pallas kernels: 5.87 us -> 3.26 us
  local copies, waits for them, and re-layouts: 2.61 us -> 0.85 us
  waiting for transfers between devices: 0 us -> 0.99 us
    all_gather x1 -> x0, blocking collectives: 5.46 us -> none  [per_device(): pair = lax.all_gather(start, 'blk')]
    ppermute x0 -> x1, starting transfers between devices: none -> 3.03 us  [per_device(): lax.ppermute(start[None], 'blk', [((i + step) % parts, i) for i in range(...]
    unnamed x12, local copies, waits for them, and re-layouts: 2.61 us -> 0.85 us
    pallas_call x1 -> x2, Pallas kernels: 2.3 us -> 0.77 us  [the longest x1 0.68 us: per_device(): pl.pallas_call(first_kernel, out_shape=(rowed(subs * parts, rows + SUBL),...]
    pallas_call x1, Pallas kernels: 2.74 us -> 1.65 us  [per_device(): pl.pallas_call(second_kernel, out_shape=(rowed(rows + SUBL), rowed(own_ro...]
    ppermute x0 -> x1, waiting for transfers between devices: none -> 0.99 us  [per_device(): lax.ppermute(start[None], 'blk', [((i + step) % parts, i) for i in range(...]
  transfers between devices with their start and end apart: 0 -> 1, of which waited for: 0 -> 1; matrix products, arithmetic and copies ran while one was open for 0% -> 0% of each run, Pallas kernels for 0% -> 0%
where the time goes in v4:
time: 35.6 us; the launch traced here: 35.4 us
  blocking collectives  26.6 us (75%)
  Pallas kernels  3.26 us (9%)
  starting transfers between devices  3.03 us (9%)
  waiting for transfers between devices  0.99 us (3%)
  local copies, waits for them, and re-layouts  0.85 us (2%)
  between operations  0.67 us (2%)
    all_to_all x1, blocking collectives, per_device(): group = lax.all_to_all(partial, ('sub', 'blk'), 0, 0, tiled=True)  13.1 us
    all_to_all x1, blocking collectives, per_device(): sums = lax.all_to_all(sums, ('rep', 'sub'), 0, 0, tiled=True)  9.03 us
    all_gather x1, blocking collectives, per_device(): both = lax.all_gather(partial, 'blk')  4.4 us
    ppermute x1, starting transfers between devices, per_device(): lax.ppermute(start[None], 'blk', [((i + step) % parts, i) for i in range(...  3.03 us
    pallas_call x1, Pallas kernels, per_device(): pl.pallas_call(second_kernel, out_shape=(rowed(rows + SUBL), rowed(own_ro...  1.65 us
    ppermute x1, waiting for transfers between devices, per_device(): lax.ppermute(start[None], 'blk', [((i + step) % parts, i) for i in range(...  0.99 us
    unnamed x12, local copies, waits for them, and re-layouts  0.85 us
    pallas_call x1, Pallas kernels, per_device(): pl.pallas_call(functools.partial(last_kernel, float(cells)), out_shape=(r...  0.74 us
  transfers between devices with their start and end apart: 1, of which 1 were waited for; matrix products, arithmetic and copies ran while one was open for 0% of the time, Pallas kernels for 0%

profile of v4, /device:TPU:0, one launch (start us, length us, event | category | flops | bytes accessed | tf_op | source)
XLA Modules:
  0.0 35.4 jit_solution(3704642041002361491)
XLA Ops:
  0.6 0.0 copy-start.1
  0.6 3.0 %collective-permute-start = (f32[1,8,128]{2,1,0:T(8,128)}, f32[1,8,128]{2,1,0:T(8,128)S(1)}, u32[]{:S(2)}, u32[]{:S(2)}) collective-permute-start(f32[1,8,128]{2,1,0:T(8,128)} %bitcast.14), channel_id=1, source_target_pairs={{4,0},{0,4},{5,1},{1,5},{6,2},{2,6},{7,3},{3,7},{12,8},{8,12},{13,... | collective-permute-start | bytes 12296 | tf_op jit(solution)/shard_map/ppermute | solution.py:239
  3.7 0.0 copy-start.5
  3.7 0.0 copy-start.3
  3.7 0.0 copy-start.4
  3.7 0.0 copy-done.1
  3.7 0.6 %copy-done.5 = s32[1,1,128]{2,1,0:T(1,128)S(1)} copy-done((s32[1,1,128]{2,1,0:T(1,128)S(1)}, s32[1,1,128]{2,1,0:T(1,128)}, u32[]{:S(2)}) %copy-start.5) | copy-done | bytes 536
  4.3 0.0 copy-done.3
  4.3 0.0 copy-done.4
  4.4 0.0 copy-start
  4.4 0.0 copy-start.2
  4.4 0.1 group_lines.1.lines_ref
  4.5 1.0 %collective-permute-done.other_ref = f32[1,8,128]{2,1,0:T(8,128)S(1)} collective-permute-done((f32[1,8,128]{2,1,0:T(8,128)}, f32[1,8,128]{2,1,0:T(8,128)S(1)}, u32[]{:S(2)}, u32[]{:S(2)}) %collective-permute-start) | collective-permute-done | bytes 4128 | tf_op jit(solution)/shard_map/ppermute | solution.py:239
  5.5 0.1 copy-done
  5.6 0.0 copy-done.2
  5.6 0.7 %first_image.1 = (f32[8,24,128]{2,1,0:T(8,128)S(1)}, f32[16,128]{1,0:T(8,128)S(1)}) custom-call(f32[8,128]{1,0:T(8,128)S(1)} %bitcast.16, f32[8,128]{1,0:T(8,128)S(1)} %group_lines.1.lines_ref, f32[1,8,128]{2,1,0:T(8,128)S(1)} %collective-permute-done.other_ref, bf16[4,32,4096]{2,1,0:T(8,128)(2,1)S(1)} %bitcast.11, s32[8,32]{1,0:T(8,128)S(1)} %bitcast.19), custom_call_target="tpu_custom_call" | custom-call | tf_op jit(solution)/shard_map/first_image/pallas_call | solution.py:253
  6.3 13.1 %all_to_all.10.group_ref = f32[8,24,128]{2,1,0:T(8,128)S(1)} all-to-all(f32[8,24,128]{2,1,0:T(8,128)S(1)} %get-tuple-element.13), channel_id=1, replica_groups=mesh['sub'=4,'blk'=2,'rep'=4] {'sub','blk'}, dimensions={0} | all-to-all | bytes 196608 | tf_op jit(solution)/shard_map/all_to_all | solution.py:262
  19.4 1.7 %second_image.1 = (f32[24,128]{1,0:T(8,128)S(1)}, f32[8,128]{1,0:T(8,128)S(1)}) custom-call(f32[8,128]{1,0:T(8,128)S(1)} %bitcast.17, f32[16,128]{1,0:T(8,128)S(1)} %get-tuple-element.12.vector_ref, f32[8,24,128]{2,1,0:T(8,128)S(1)} %all_to_all.10.group_ref, bf16[4,32,4096]{2,1,0:T(8,128)(2,1)S(1)} %bitcast.12, s32[8,32]{1,0:T(8,128)S(1)} %bitcast.20, ...), custom_call_target="tpu_custom_call" | custom-call | tf_op jit(solution)/shard_map/second_image/pallas_call | solution.py:263
  21.1 4.4 %all-gather = f32[48,128]{1,0:T(8,128)S(1)} all-gather(f32[24,128]{1,0:T(8,128)S(1)} %get-tuple-element.15), channel_id=2, replica_groups=mesh['sub'=4,'blk'=2,'rep'=4] {'blk'}, dimensions={0}, use_global_device_ids=true | all-gather | bytes 36864 | tf_op jit(solution)/shard_map/all_gather | solution.py:272
  25.5 0.1 pair_sums.1
  25.6 9.0 %all_to_all.11.sums_ref = f32[16,1,128]{2,1,0:T(1,128)S(1)} all-to-all(f32[16,1,128]{2,1,0:T(1,128)S(1)} %get-tuple-element.17), channel_id=1, replica_groups=mesh['sub'=4,'blk'=2,'rep'=4] {'rep','sub'}, dimensions={0} | all-to-all | bytes 16384 | tf_op jit(solution)/shard_map/all_to_all | solution.py:281
  34.6 0.7 %arnoldi_entries.1 = (f32[8,128]{1,0:T(8,128)}, f32[8,128]{1,0:T(8,128)}, f32[1,5]{1,0:T(1,128)}) custom-call(f32[8,128]{1,0:T(8,128)S(1)} %bitcast.18, f32[8,128]{1,0:T(8,128)S(1)} %get-tuple-element.14.own_ref, f32[8,128]{1,0:T(8,128)S(1)} %get-tuple-element.16.again_ref, f32[16,1,128]{2,1,0:T(1,128)S(1)} %all_to_all.11.sums_ref), custom_call_target="tpu_custom_call" | custom-call | tf_op jit(solution)/shard_map/arnoldi_entries/pallas_call | solution.py:282
Async XLA Ops:
  0.6 3.1 %copy-start.1 = (f32[1,1,1024]{2,1,0:T(1,128)S(1)}, f32[1,1,1024]{2,1,0:T(1,128)}, u32[]{:S(2)}) copy-start(f32[1,1,1024]{2,1,0:T(1,128)} %param.6) | copy-start | bytes 12292
  0.6 4.8 %collective-permute-start = (f32[1,8,128]{2,1,0:T(8,128)}, f32[1,8,128]{2,1,0:T(8,128)S(1)}, u32[]{:S(2)}, u32[]{:S(2)}) collective-permute-start(f32[1,8,128]{2,1,0:T(8,128)} %bitcast.14), channel_id=1, source_target_pairs={{4,0},{0,4},{5,1},{1,5},{6,2},{2,6},{7,3},{3,7},{12,8},{8,12},{13,... | collective-permute-start | bytes 12296 | tf_op jit(solution)/shard_map/ppermute | solution.py:239
  3.7 0.7 %copy-start.5 = (s32[1,1,128]{2,1,0:T(1,128)S(1)}, s32[1,1,128]{2,1,0:T(1,128)}, u32[]{:S(2)}) copy-start(s32[1,1,128]{2,1,0:T(1,128)} %param.9) | copy-start | bytes 1540
  3.7 0.7 %copy-start.3 = (s32[1,1,2]{2,1,0:T(1,128)S(1)}, s32[1,1,2]{2,1,0:T(1,128)}, u32[]{:S(2)}) copy-start(s32[1,1,2]{2,1,0:T(1,128)} %param.10) | copy-start | bytes 28
  3.7 0.7 %copy-start.4 = (f32[1,1,2,128]{3,2,1,0:T(2,128)S(1)}, f32[1,1,2,128]{3,2,1,0:T(2,128)}, u32[]{:S(2)}) copy-start(f32[1,1,2,128]{3,2,1,0:T(2,128)} %param.11) | copy-start | bytes 3076
  4.4 1.2 %copy-start = (bf16[1,1,4,32,4096]{4,3,2,1,0:T(8,128)(2,1)S(1)}, bf16[1,1,4,32,4096]{4,3,2,1,0:T(8,128)(2,1)}, u32[]{:S(2)}) copy-start(bf16[1,1,4,32,4096]{4,3,2,1,0:T(8,128)(2,1)} %param.7) | copy-start | bytes 3145732
  4.4 1.2 %copy-start.2 = (s32[1,1,8,32]{3,2,1,0:T(8,128)S(1)}, s32[1,1,8,32]{3,2,1,0:T(8,128)}, u32[]{:S(2)}) copy-start(s32[1,1,8,32]{3,2,1,0:T(8,128)} %param.8) | copy-start | bytes 3076

commit v5 on v4

--- a/solution.py
+++ b/solution.py
@@ -110,87 +110,84 @@
         out_ref[device, rows : rows + SUBL, :] = lines_ref[...]
 
 
-def second_kernel(
-    start_ref, vector_ref, group_ref, blocks_ref, pattern_ref, near_ref, out_ref, own_ref, fold_ref, image_ref
-):
-    own_rows, rows = start_ref.shape[0], vector_ref.shape[0]
-    sub, blk = lax.axis_index("sub"), lax.axis_index("blk")
-    subs, parts = lax.axis_size("sub"), lax.axis_size("blk")
+def line(group_ref, device, i):
+    first = group_ref.shape[1] - SUBL + i
+    return group_ref[device, first : first + 1, :]
+
+
+def landed(group_ref, sub_at, part, own_rows, count):
+    parts = lax.axis_size("blk")
+    traces = [line(group_ref, other * parts + part, 0) for other in range(lax.axis_size("sub"))]
+    traces = jnp.concatenate(traces, 0)
+    names = row_iota(traces.shape).astype(jnp.float32)
+    device = sub_at * parts + part
+    inflow = jnp.zeros((1, LANES), jnp.float32)
+    for n in range(count):
+        chosen = jnp.where(names == line(group_ref, device, 2 + count + n), traces, 0.0)
+        inflow = inflow + line(group_ref, device, 2 + n) * jnp.sum(chosen, axis=0, keepdims=True)
+    places = line(group_ref, device, 1).astype(jnp.int32) - part * own_rows * LANES
+    return spread(inflow, places, own_rows), places
+
+
+def summed(group_ref, sub_at, first, count):
+    parts = lax.axis_size("blk")
+    total = group_ref[sub_at * parts, first : first + count, :]
+    for b in range(1, parts):
+        total = total + group_ref[sub_at * parts + b, first : first + count, :]
+    return total
+
+
+def second_kernel(count, group_ref, blocks_ref, pattern_ref, out_ref, image_ref, fold_ref):
+    rows = image_ref.shape[0]
+    sub, blk, parts = lax.axis_index("sub"), lax.axis_index("blk"), lax.axis_size("blk")
+    added = [landed(group_ref, sub, part, rows // parts, count)[0] for part in range(parts)]
+    image = summed(group_ref, sub, 0, rows) + jnp.concatenate(added, 0)
+    image_ref[...] = image
+    out_ref[...] = block_product(image, blocks_ref, pattern_ref, blk * blocks_ref.shape[0], fold_ref)
+
+
+def down(left, right):
+    return jnp.sum(left * right, axis=0, keepdims=True)
+
+
+def inflow_kernel(vector_ref, image_ref, group_ref, near_ref, out_ref, sums_ref):
+    rows = image_ref.shape[0]
     count = near_ref.shape[1]
-    own = pl.ds(pl.multiple_of(blk * own_rows, SUBL), own_rows)
-
-    def line(sub_at, part, i):
-        return group_ref[sub_at * parts + part, rows + i : rows + i + 1, :]
-
-    def landed(sub_at, part):
-        traces = jnp.concatenate([line(other, part, 0) for other in range(subs)], 0)
-        names = row_iota(traces.shape).astype(jnp.float32)
+    sub, parts = lax.axis_index("sub"), lax.axis_size("blk")
+    own_rows = rows // parts
+    for part in range(parts):
+        device = sub * parts + part
         inflow = jnp.zeros((1, LANES), jnp.float32)
         for n in range(count):
-            chosen = jnp.where(names == line(sub_at, part, 2 + count + n), traces, 0.0)
-            inflow = inflow + line(sub_at, part, 2 + n) * jnp.sum(chosen, axis=0, keepdims=True)
-        places = line(sub_at, part, 1).astype(jnp.int32) - part * own_rows * LANES
-        return spread(inflow, places, own_rows), places
-
-    def summed(index, where):
-        total = group_ref[index * parts, where, :]
-        for b in range(1, parts):
-            total = total + group_ref[index * parts + b, where, :]
-        return total
-
-    added = jnp.concatenate([landed(sub, b)[0] for b in range(parts)], 0)
-    image = summed(sub, pl.ds(0, rows)) + added
-    image_ref[...] = image
-    second = block_product(image, blocks_ref, pattern_ref, blk * blocks_ref.shape[0], fold_ref)
-    inflow = jnp.zeros((1, LANES), jnp.float32)
-    for n in range(count):
-        source = near_ref[0, n]
-        added, places = landed(source, blk)
-        inflow = inflow + line(sub, blk, 2 + n) * take_trace(summed(source, own) + added, places)
-    places = line(sub, blk, 1).astype(jnp.int32) - blk * own_rows * LANES
-    out_ref[0:rows, :] = second
-    out_ref[own, :] = out_ref[own, :] + spread(inflow, places, own_rows)
-    second = out_ref[0:rows, :]
-    vector = vector_ref[...]
-    vector_own, image_own = start_ref[...], image_ref[own, :]
-    own_ref[...] = image_own
-
-    def down(left, right):
-        return jnp.sum(left * right, axis=0, keepdims=True)
-
-    sums = [
-        down(vector_own, vector_own),
-        down(vector_own, image_own),
-        down(image_own, image_own),
-        down(vector, second),
-        down(image, second),
-        jnp.zeros((SUBL - 5, LANES), jnp.float32),
-    ]
-    out_ref[rows : rows + SUBL, :] = jnp.concatenate(sums, 0)
-
-
-def pair_kernel(pair_ref, out_ref, own_ref):
-    parts, height, _ = pair_ref.shape
-    rows = height - SUBL
-    own_rows = rows // parts
-    total = pair_ref[0]
-    for b in range(1, parts):
-        total = total + pair_ref[b]
-    square = jnp.sum(total[0:rows] * total[0:rows], axis=0, keepdims=True)
-    sums = jnp.where(row_iota((SUBL, LANES)) == 5, square, total[rows:height])
+            source = near_ref[0, n]
+            added, places = landed(group_ref, source, part, own_rows, count)
+            trace = take_trace(summed(group_ref, source, part * own_rows, own_rows) + added, places)
+            inflow = inflow + line(group_ref, device, 2 + n) * trace
+        places = line(group_ref, device, 1).astype(jnp.int32) - part * own_rows * LANES
+        out_ref[part * own_rows : (part + 1) * own_rows, :] = spread(inflow, places, own_rows)
+    vector, image = vector_ref[...], image_ref[...]
+    sums = [down(vector, vector), down(vector, image), down(image, image)]
+    sums_ref[...] = jnp.concatenate([*sums, jnp.zeros((SUBL - len(sums), LANES), jnp.float32)], 0)
+
+
+def pair_kernel(vector_ref, image_ref, sums_ref, inflow_ref, mine_ref, other_ref, out_ref, again_ref, part_ref):
+    parts = part_ref.shape[0]
+    for step in range(parts):
+        part_ref[lax.rem(lax.axis_index("blk") + step, parts)] = other_ref[step - 1] if step else mine_ref[...]
+    again = inflow_ref[...]
+    for part in range(parts):
+        again = again + part_ref[part]
+    again_ref[...] = again
+    sums = [down(vector_ref[...], again), down(image_ref[...], again), down(again, again)]
+    sums = jnp.concatenate([sums_ref[0:3, :], *sums, sums_ref[6:SUBL, :]], 0)
     sums = jnp.sum(sums, axis=1, keepdims=True)
     sums = jnp.where(row_iota((SUBL, LANES)) == lane_iota((SUBL, LANES)), sums, 0.0)
     sums = jnp.sum(sums, axis=0, keepdims=True)
     for device in range(out_ref.shape[0]):
         out_ref[device] = sums
-    own = pl.ds(pl.multiple_of(lax.axis_index("blk") * own_rows, SUBL), own_rows)
-    again = pair_ref[0, own, :]
-    for b in range(1, parts):
-        again = again + pair_ref[b, own, :]
-    own_ref[...] = again
-
-
-def last_kernel(cells, start_ref, own_ref, again_ref, sums_ref, second_ref, third_ref, entries_ref):
+
+
+def last_kernel(cells, start_ref, image_ref, again_ref, sums_ref, second_ref, third_ref, entries_ref):
     sums = jnp.sum(sums_ref[...], axis=0) / cells
 
     def whole(i):
@@ -209,9 +206,11 @@
     second_square = yy + near * near * ww + far * far * vv + 2.0 * (near * far * vw - near * wy - far * vy)
     h32 = jnp.sqrt(jnp.maximum(second_square, 0.0) * scale * scale + epsilon)
 
-    vector, image = start_ref[...], own_ref[...]
+    own_rows = start_ref.shape[0]
+    own = pl.ds(pl.multiple_of(lax.axis_index("blk") * own_rows, SUBL), own_rows)
+    vector, image = start_ref[...], image_ref[own, :]
     second_ref[...] = (image - h11 * vector) * scale
-    third_ref[...] = (again_ref[...] - near * image - far * vector) * (scale / h32)
+    third_ref[...] = (again_ref[own, :] - near * image - far * vector) * (scale / h32)
     lane = lane_iota((1, LANES))
     entries = h32
     for i, value in enumerate((h11, h21, h12, h22)):
@@ -235,11 +234,15 @@
         return jax.ShapeDtypeStruct((*shape, LANES), jnp.float32)
 
     smem = pl.BlockSpec(memory_space=pltpu.SMEM)
-    others = [
-        lax.ppermute(start[None], "blk", [((i + step) % parts, i) for i in range(parts)])
-        for step in range(1, parts)
-    ]
-    others = others[0] if parts == 2 else jnp.concatenate(others, 0)
+
+    def from_others(value):
+        got = [
+            lax.ppermute(value[None], "blk", [((i + step) % parts, i) for i in range(parts)])
+            for step in range(1, parts)
+        ]
+        return got[0] if parts == 2 else jnp.concatenate(got, 0)
+
+    others = from_others(start)
     fold = pltpu.VMEM((blocks.shape[1], LANES), jnp.float32)
     lines = pl.pallas_call(
         lines_kernel,
@@ -260,24 +263,34 @@
         name="first_image",
     )(start, lines, others, blocks, pattern)
     group = lax.all_to_all(partial, ("sub", "blk"), 0, 0, tiled=True)
-    partial, image = pl.pallas_call(
-        second_kernel,
-        out_shape=(rowed(rows + SUBL), rowed(own_rows)),
-        in_specs=[vmem, vmem, vmem, vmem, vmem, smem],
+    second, image = pl.pallas_call(
+        functools.partial(second_kernel, coupling.shape[0]),
+        out_shape=(rowed(rows), rowed(rows)),
+        in_specs=[vmem] * 3,
         out_specs=(vmem, vmem),
-        scratch_shapes=[fold, pltpu.VMEM((rows, LANES), jnp.float32)],
+        scratch_shapes=[fold],
         compiler_params=params,
         name="second_image",
-    )(start, vector, group, blocks, pattern, neighbours)
-    both = lax.all_gather(partial, "blk")
+    )(group, blocks, pattern)
+    others = from_others(second)
+    inflow, sums = pl.pallas_call(
+        inflow_kernel,
+        out_shape=(rowed(rows), rowed(SUBL)),
+        in_specs=[vmem, vmem, vmem, smem],
+        out_specs=(vmem, vmem),
+        compiler_params=params,
+        cost_estimate=pl.CostEstimate(flops=1 << 32, bytes_accessed=1 << 20, transcendentals=0),
+        name="second_inflow",
+    )(vector, image, group, neighbours)
     sums, again = pl.pallas_call(
         pair_kernel,
-        out_shape=(rowed(reps * subs, 1), rowed(own_rows)),
-        in_specs=[vmem],
+        out_shape=(rowed(reps * subs, 1), rowed(rows)),
+        in_specs=[vmem] * 6,
         out_specs=(vmem, vmem),
+        scratch_shapes=[pltpu.VMEM((parts, rows, LANES), jnp.float32)],
         compiler_params=params,
         name="pair_sums",
-    )(both)
+    )(vector, image, sums, inflow, second, others)
     sums = lax.all_to_all(sums, ("rep", "sub"), 0, 0, tiled=True)
     second, third, entries = pl.pallas_call(
         functools.partial(last_kernel, float(cells)),

time: 35.6 us -> 34.1 us (0.958)
  blocking collectives: 26.6 us -> 22.2 us
  waiting for transfers between devices: 0.99 us -> 3.22 us
  starting transfers between devices: 3.03 us -> 3.4 us
    all_gather x1 -> x0, blocking collectives: 4.4 us -> none  [per_device(): both = lax.all_gather(partial, 'blk')]
    ppermute x1 -> x2, waiting for transfers between devices: 0.99 us -> 3.22 us  [from_others(): lax.ppermute(value[None], 'blk', [((i + step) % parts, i) for i in range(...]
    ppermute x1 -> x2, starting transfers between devices: 3.03 us -> 3.4 us  [from_others(): lax.ppermute(value[None], 'blk', [((i + step) % parts, i) for i in range(...]
    pallas_call x2 -> x3, Pallas kernels: 1.75 us -> 2.08 us  [the longest x1 1.13 us: per_device(): pl.pallas_call(inflow_kernel, out_shape=(rowed(rows), rowed(SUBL)), in_sp...]
  transfers between devices with their start and end apart: 1 -> 2, of which waited for: 1 -> 2; matrix products, arithmetic and copies ran while one was open for 0% -> 0% of each run, Pallas kernels for 0% -> 4%
where the time goes in v5:
time: 34.1 us; the launch traced here: 33.9 us
  blocking collectives  22.2 us (65%)
  Pallas kernels  3.59 us (11%)
  starting transfers between devices  3.4 us (10%)
  waiting for transfers between devices  3.22 us (9%)
  local copies, waits for them, and re-layouts  0.82 us (2%)
  between operations  0.67 us (2%)
    all_to_all x1, blocking collectives, per_device(): group = lax.all_to_all(partial, ('sub', 'blk'), 0, 0, tiled=True)  13.1 us
    all_to_all x1, blocking collectives, per_device(): sums = lax.all_to_all(sums, ('rep', 'sub'), 0, 0, tiled=True)  9.04 us
    ppermute x2, starting transfers between devices, from_others(): lax.ppermute(value[None], 'blk', [((i + step) % parts, i) for i in range(...  3.4 us
    ppermute x2, waiting for transfers between devices, from_others(): lax.ppermute(value[None], 'blk', [((i + step) % parts, i) for i in range(...  3.22 us
    pallas_call x1, Pallas kernels, per_device(): pl.pallas_call(inflow_kernel, out_shape=(rowed(rows), rowed(SUBL)), in_sp...  1.13 us
    pallas_call x1, Pallas kernels, per_device(): pl.pallas_call(functools.partial(second_kernel, coupling.shape[0]), out_s...  0.83 us
    unnamed x12, local copies, waits for them, and re-layouts  0.82 us
    pallas_call x1, Pallas kernels, per_device(): pl.pallas_call(functools.partial(last_kernel, float(cells)), out_shape=(r...  0.74 us
  transfers between devices with their start and end apart: 2, of which 2 were waited for; matrix products, arithmetic and copies ran while one was open for 0% of the time, Pallas kernels for 4%

profile of v5, /device:TPU:0, one launch (start us, length us, event | category | flops | bytes accessed | tf_op | source)
XLA Modules:
  0.0 33.9 jit_solution(6100618621369411095)
XLA Ops:
  0.6 0.0 copy-start.2
  0.6 3.0 %collective-permute-start = (f32[1,8,128]{2,1,0:T(8,128)}, f32[1,8,128]{2,1,0:T(8,128)S(1)}, u32[]{:S(2)}, u32[]{:S(2)}) collective-permute-start(f32[1,8,128]{2,1,0:T(8,128)} %bitcast.15), channel_id=1, source_target_pairs={{4,0},{0,4},{5,1},{1,5},{6,2},{2,6},{7,3},{3,7},{12,8},{8,12},{13,... | collective-permute-start | bytes 12296 | tf_op jit(solution)/shard_map/ppermute | solution.py:240
  3.7 0.0 copy-start.5
  3.7 0.0 copy-start.3
  3.7 0.0 copy-start.4
  3.7 0.0 copy-done.2
  3.7 0.6 %copy-done.5 = s32[1,1,2]{2,1,0:T(1,128)S(1)} copy-done((s32[1,1,2]{2,1,0:T(1,128)S(1)}, s32[1,1,2]{2,1,0:T(1,128)}, u32[]{:S(2)}) %copy-start.5) | copy-done | bytes 32
  4.3 0.0 copy-done.3
  4.4 0.0 copy-done.4
  4.4 0.0 copy-start
  4.4 0.0 copy-start.1
  4.4 0.1 group_lines.1.lines_ref
  4.5 1.0 %collective-permute-done.other_ref = f32[1,8,128]{2,1,0:T(8,128)S(1)} collective-permute-done((f32[1,8,128]{2,1,0:T(8,128)}, f32[1,8,128]{2,1,0:T(8,128)S(1)}, u32[]{:S(2)}, u32[]{:S(2)}) %collective-permute-start) | collective-permute-done | bytes 4128 | tf_op jit(solution)/shard_map/ppermute | solution.py:240
  5.5 0.1 copy-done
  5.6 0.0 copy-done.1
  5.6 0.7 %first_image.1 = (f32[8,24,128]{2,1,0:T(8,128)S(1)}, f32[16,128]{1,0:T(8,128)S(1)}) custom-call(f32[8,128]{1,0:T(8,128)S(1)} %bitcast.17, f32[8,128]{1,0:T(8,128)S(1)} %group_lines.1.lines_ref, f32[1,8,128]{2,1,0:T(8,128)S(1)} %collective-permute-done.other_ref, bf16[4,32,4096]{2,1,0:T(8,128)(2,1)S(1)} %bitcast.11, s32[8,32]{1,0:T(8,128)S(1)} %bitcast.13), custom_call_target="tpu_custom_call" | custom-call | tf_op jit(solution)/shard_map/first_image/pallas_call | solution.py:256
  6.3 13.1 %all_to_all.10.group_ref = f32[8,24,128]{2,1,0:T(8,128)S(1)} all-to-all(f32[8,24,128]{2,1,0:T(8,128)S(1)} %get-tuple-element.14), channel_id=1, replica_groups=mesh['sub'=4,'blk'=2,'rep'=4] {'sub','blk'}, dimensions={0} | all-to-all | bytes 196608 | tf_op jit(solution)/shard_map/all_to_all | solution.py:265
  19.4 0.8 %second_image.1 = (f32[16,128]{1,0:T(8,128)S(1)}, f32[16,128]{1,0:T(8,128)S(1)}) custom-call(f32[8,24,128]{2,1,0:T(8,128)S(1)} %all_to_all.10.group_ref, bf16[4,32,4096]{2,1,0:T(8,128)(2,1)S(1)} %bitcast.12, s32[8,32]{1,0:T(8,128)S(1)} %bitcast.14), custom_call_target="tpu_custom_call" | custom-call | tf_op jit(solution)/shard_map/second_image/pallas_call | solution.py:266
  20.3 0.4 %collective-permute-start.1 = (f32[1,16,128]{2,1,0:T(8,128)S(1)}, f32[1,16,128]{2,1,0:T(8,128)S(1)}, u32[]{:S(2)}, u32[]{:S(2)}) collective-permute-start(f32[1,16,128]{2,1,0:T(8,128)S(1)} %bitcast.19), channel_id=1, source_target_pairs={{4,0},{0,4},{5,1},{1,5},{6,2},{2,6},{7,3},{3,7},{12,8},{8,12},{13,... | collective-permute-start | bytes 24584 | tf_op jit(solution)/shard_map/ppermute | solution.py:240
  20.6 1.1 %second_inflow.1 = (f32[16,128]{1,0:T(8,128)S(1)}, f32[8,128]{1,0:T(8,128)S(1)}) custom-call(f32[16,128]{1,0:T(8,128)S(1)} %get-tuple-element.16.vector_ref, f32[16,128]{1,0:T(8,128)S(1)} %get-tuple-element.15.image_ref, f32[8,24,128]{2,1,0:T(8,128)S(1)} %all_to_all.10.group_ref, s32[1,2]{1,0:T(1,128)S(1)} %bitcast.23), custom_call_target="tpu_custom_call" | custom-call | flops 4294967296 | bytes 1048576 | tf_op jit(solution)/shard_map/second_inflow/pallas_call | solution.py:276
  21.8 2.2 %collective-permute-done.1.other_ref = f32[1,16,128]{2,1,0:T(8,128)S(1)} collective-permute-done((f32[1,16,128]{2,1,0:T(8,128)S(1)}, f32[1,16,128]{2,1,0:T(8,128)S(1)}, u32[]{:S(2)}, u32[]{:S(2)}) %collective-permute-start.1) | collective-permute-done | bytes 8224 | tf_op jit(solution)/shard_map/ppermute | solution.py:240
  24.0 0.1 pair_sums.1
  24.1 9.0 %all_to_all.11.sums_ref = f32[16,1,128]{2,1,0:T(1,128)S(1)} all-to-all(f32[16,1,128]{2,1,0:T(1,128)S(1)} %get-tuple-element.21), channel_id=1, replica_groups=mesh['sub'=4,'blk'=2,'rep'=4] {'rep','sub'}, dimensions={0} | all-to-all | bytes 16384 | tf_op jit(solution)/shard_map/all_to_all | solution.py:294
  33.1 0.7 %arnoldi_entries.1 = (f32[8,128]{1,0:T(8,128)}, f32[8,128]{1,0:T(8,128)}, f32[1,5]{1,0:T(1,128)}) custom-call(f32[8,128]{1,0:T(8,128)S(1)} %bitcast.18, f32[16,128]{1,0:T(8,128)S(1)} %get-tuple-element.15.image_ref, f32[16,128]{1,0:T(8,128)S(1)} %get-tuple-element.20.again_ref, f32[16,1,128]{2,1,0:T(1,128)S(1)} %all_to_all.11.sums_ref), custom_call_target="tpu_custom_call" | custom-call | tf_op jit(solution)/shard_map/arnoldi_entries/pallas_call | solution.py:295
Async XLA Ops:
  0.6 3.1 %copy-start.2 = (f32[1,1,1024]{2,1,0:T(1,128)S(1)}, f32[1,1,1024]{2,1,0:T(1,128)}, u32[]{:S(2)}) copy-start(f32[1,1,1024]{2,1,0:T(1,128)} %param.6) | copy-start | bytes 12292
  0.6 4.8 %collective-permute-start = (f32[1,8,128]{2,1,0:T(8,128)}, f32[1,8,128]{2,1,0:T(8,128)S(1)}, u32[]{:S(2)}, u32[]{:S(2)}) collective-permute-start(f32[1,8,128]{2,1,0:T(8,128)} %bitcast.15), channel_id=1, source_target_pairs={{4,0},{0,4},{5,1},{1,5},{6,2},{2,6},{7,3},{3,7},{12,8},{8,12},{13,... | collective-permute-start | bytes 12296 | tf_op jit(solution)/shard_map/ppermute | solution.py:240
  3.7 0.7 %copy-start.5 = (s32[1,1,2]{2,1,0:T(1,128)S(1)}, s32[1,1,2]{2,1,0:T(1,128)}, u32[]{:S(2)}) copy-start(s32[1,1,2]{2,1,0:T(1,128)} %param.10) | copy-start | bytes 28
  3.7 0.7 %copy-start.3 = (f32[1,1,2,128]{3,2,1,0:T(2,128)S(1)}, f32[1,1,2,128]{3,2,1,0:T(2,128)}, u32[]{:S(2)}) copy-start(f32[1,1,2,128]{3,2,1,0:T(2,128)} %param.11) | copy-start | bytes 3076
  3.7 0.7 %copy-start.4 = (s32[1,1,128]{2,1,0:T(1,128)S(1)}, s32[1,1,128]{2,1,0:T(1,128)}, u32[]{:S(2)}) copy-start(s32[1,1,128]{2,1,0:T(1,128)} %param.9) | copy-start | bytes 1540
  4.4 1.2 %copy-start = (bf16[1,1,4,32,4096]{4,3,2,1,0:T(8,128)(2,1)S(1)}, bf16[1,1,4,32,4096]{4,3,2,1,0:T(8,128)(2,1)}, u32[]{:S(2)}) copy-start(bf16[1,1,4,32,4096]{4,3,2,1,0:T(8,128)(2,1)} %param.7) | copy-start | bytes 3145732
  4.4 1.2 %copy-start.1 = (s32[1,1,8,32]{3,2,1,0:T(8,128)S(1)}, s32[1,1,8,32]{3,2,1,0:T(8,128)}, u32[]{:S(2)}) copy-start(s32[1,1,8,32]{3,2,1,0:T(8,128)} %param.8) | copy-start | bytes 3076
  20.3 3.7 %collective-permute-start.1 = (f32[1,16,128]{2,1,0:T(8,128)S(1)}, f32[1,16,128]{2,1,0:T(8,128)S(1)}, u32[]{:S(2)}, u32[]{:S(2)}) collective-permute-start(f32[1,16,128]{2,1,0:T(8,128)S(1)} %bitcast.19), channel_id=1, source_target_pairs={{4,0},{0,4},{5,1},{1,5},{6,2},{2,6},{7,3},{3,7},{12,8},{8,12},{13,... | collective-permute-start | bytes 24584 | tf_op jit(solution)/shard_map/ppermute | solution.py:240

commit v6 on v5

--- a/solution.py
+++ b/solution.py
@@ -53,7 +53,7 @@
     for c in range(width // LANES):
         total = None
         for k in range(slots):
-            term = blocks_ref[k, :, pl.ds(c * LANES, LANES)].astype(jnp.float32) * picked[k]
+            term = blocks_ref[k, :, pl.ds(c * LANES, LANES)] * picked[k]
             total = term if total is None else total + term
         high = total.astype(jnp.bfloat16)
         low = (total - high.astype(jnp.float32)).astype(jnp.bfloat16)
@@ -95,6 +95,10 @@
     lines += [jnp.broadcast_to(near[:, n : n + 1], (1, LANES)) for n in range(count)]
     lines += [jnp.zeros((SUBL - len(lines), LANES), jnp.float32)]
     out_ref[...] = jnp.concatenate(lines, 0)
+
+
+def widen_kernel(blocks_ref, out_ref):
+    out_ref[...] = blocks_ref[...].astype(jnp.float32)
 
 
 def first_kernel(start_ref, lines_ref, other_ref, blocks_ref, pattern_ref, out_ref, vector_ref, fold_ref):
@@ -195,22 +199,27 @@
 
     vv, vw, ww, vy, wy, yy = (whole(i) for i in range(6))
     norm_square = vv + epsilon
-    h11 = vw / norm_square
-    first_square = jnp.maximum(ww - 2.0 * h11 * vw + h11 * h11 * vv, 0.0) / norm_square
-    h21 = jnp.sqrt(first_square + epsilon)
-    scale = 1.0 / (jnp.sqrt(norm_square) * h21)
-    h12 = (vy - h11 * vw) / (norm_square * h21)
-    h22 = (wy - h11 * (ww + vy - h11 * vw)) * scale * scale
+    inverse = 1.0 / norm_square
+    h11 = vw * inverse
+    skew = vy - h11 * vw
+    first_square = jnp.maximum(ww - 2.0 * h11 * vw + h11 * h11 * vv, 0.0) * inverse + epsilon
+    over_first = lax.rsqrt(first_square)
+    h21 = first_square * over_first
+    scale = lax.rsqrt(norm_square) * over_first
+    h12 = skew * inverse * over_first
+    h22 = (wy - h11 * (ww + skew)) * scale * scale
     near = h11 + h22
-    far = h12 * h21 - h11 * h22
+    far = skew * inverse - h11 * h22
     second_square = yy + near * near * ww + far * far * vv + 2.0 * (near * far * vw - near * wy - far * vy)
-    h32 = jnp.sqrt(jnp.maximum(second_square, 0.0) * scale * scale + epsilon)
+    second_square = jnp.maximum(second_square, 0.0) * scale * scale + epsilon
+    over_second = lax.rsqrt(second_square)
+    h32 = second_square * over_second
 
     own_rows = start_ref.shape[0]
     own = pl.ds(pl.multiple_of(lax.axis_index("blk") * own_rows, SUBL), own_rows)
     vector, image = start_ref[...], image_ref[own, :]
     second_ref[...] = (image - h11 * vector) * scale
-    third_ref[...] = (again_ref[own, :] - near * image - far * vector) * (scale / h32)
+    third_ref[...] = (again_ref[own, :] - near * image - far * vector) * (scale * over_second)
     lane = lane_iota((1, LANES))
     entries = h32
     for i, value in enumerate((h11, h21, h12, h22)):
@@ -253,6 +262,15 @@
         cost_estimate=pl.CostEstimate(flops=1 << 32, bytes_accessed=1 << 20, transcendentals=0),
         name="group_lines",
     )(start, local_map, neighbours, coupling)
+    wide = pl.pallas_call(
+        widen_kernel,
+        out_shape=jax.ShapeDtypeStruct(blocks.shape, jnp.float32),
+        in_specs=[vmem],
+        out_specs=vmem,
+        compiler_params=params,
+        cost_estimate=pl.CostEstimate(flops=1 << 32, bytes_accessed=3 << 20, transcendentals=0),
+        name="wide_blocks",
+    )(blocks)
     partial, vector = pl.pallas_call(
         first_kernel,
         out_shape=(rowed(subs * parts, rows + SUBL), rowed(rows)),
@@ -261,7 +279,7 @@
         scratch_shapes=[fold],
         compiler_params=params,
         name="first_image",
-    )(start, lines, others, blocks, pattern)
+    )(start, lines, others, wide, pattern)
     group = lax.all_to_all(partial, ("sub", "blk"), 0, 0, tiled=True)
     second, image = pl.pallas_call(
         functools.partial(second_kernel, coupling.shape[0]),
@@ -271,7 +289,7 @@
         scratch_shapes=[fold],
         compiler_params=params,
         name="second_image",
-    )(group, blocks, pattern)
+    )(group, wide, pattern)
     others = from_others(second)
     inflow, sums = pl.pallas_call(
         inflow_kernel,

time: 34.1 us -> 34.1 us (level)
  local copies, waits for them, and re-layouts: 0.82 us -> 2.36 us
  waiting for transfers between devices: 3.22 us -> 2.22 us
  blocking collectives: 22.2 us -> 21.5 us
    unnamed x12, local copies, waits for them, and re-layouts: 0.82 us -> 2.36 us
    ppermute x2, waiting for transfers between devices: 3.22 us -> 2.22 us  [from_others(): lax.ppermute(value[None], 'blk', [((i + step) % parts, i) for i in range(...]
    all_to_all x1, blocking collectives: 13.1 us -> 12.4 us  [per_device(): group = lax.all_to_all(partial, ('sub', 'blk'), 0, 0, tiled=True)]
  transfers between devices with their start and end apart: 2 -> 2, of which waited for: 2 -> 1; matrix products, arithmetic and copies ran while one was open for 0% -> 0% of each run, Pallas kernels for 4% -> 4%
where the time goes in v6:
time: 34.1 us; the launch traced here: 33.8 us
  blocking collectives  21.5 us (63%)
  Pallas kernels  3.69 us (11%)
  starting transfers between devices  3.4 us (10%)
  local copies, waits for them, and re-layouts  2.36 us (7%)
  waiting for transfers between devices  2.22 us (7%)
  between operations  0.67 us (2%)
    all_to_all x1, blocking collectives, per_device(): group = lax.all_to_all(partial, ('sub', 'blk'), 0, 0, tiled=True)  12.4 us
    all_to_all x1, blocking collectives, per_device(): sums = lax.all_to_all(sums, ('rep', 'sub'), 0, 0, tiled=True)  9.04 us
    ppermute x2, starting transfers between devices, from_others(): lax.ppermute(value[None], 'blk', [((i + step) % parts, i) for i in range(...  3.4 us
    unnamed x12, local copies, waits for them, and re-layouts  2.36 us
    ppermute x2, waiting for transfers between devices, from_others(): lax.ppermute(value[None], 'blk', [((i + step) % parts, i) for i in range(...  2.22 us
    pallas_call x1, Pallas kernels, per_device(): pl.pallas_call(inflow_kernel, out_shape=(rowed(rows), rowed(SUBL)), in_sp...  1.13 us
    pallas_call x1, Pallas kernels, per_device(): pl.pallas_call(functools.partial(second_kernel, coupling.shape[0]), out_s...  0.82 us
    pallas_call x1, Pallas kernels, per_device(): pl.pallas_call(functools.partial(last_kernel, float(cells)), out_shape=(r...  0.72 us
  transfers between devices with their start and end apart: 2, of which 1 were waited for; matrix products, arithmetic and copies ran while one was open for 0% of the time, Pallas kernels for 4%

profile of v6, /device:TPU:0, one launch (start us, length us, event | category | flops | bytes accessed | tf_op | source)
XLA Modules:
  0.0 33.8 jit_solution(11962234622209954743)
XLA Ops:
  0.6 3.0 %collective-permute-start = (f32[1,8,128]{2,1,0:T(8,128)}, f32[1,8,128]{2,1,0:T(8,128)S(1)}, u32[]{:S(2)}, u32[]{:S(2)}) collective-permute-start(f32[1,8,128]{2,1,0:T(8,128)} %bitcast.13), channel_id=1, source_target_pairs={{4,0},{0,4},{5,1},{1,5},{6,2},{2,6},{7,3},{3,7},{12,8},{8,12},{13,... | collective-permute-start | bytes 12296 | tf_op jit(solution)/shard_map/ppermute | solution.py:249
  3.7 0.0 copy-start.2
  3.7 1.2 %copy-done.2 = bf16[1,1,4,32,4096]{4,3,2,1,0:T(8,128)(2,1)S(1)} copy-done((bf16[1,1,4,32,4096]{4,3,2,1,0:T(8,128)(2,1)S(1)}, bf16[1,1,4,32,4096]{4,3,2,1,0:T(8,128)(2,1)}, u32[]{:S(2)}) %copy-start.2) | copy-done | bytes 1048600
  4.9 0.0 copy-start.1
  4.9 0.0 copy-start.3
  4.9 0.0 copy-start.4
  4.9 0.0 copy-start.5
  4.9 0.1 wide_blocks.1.blocks_ref
  5.0 0.5 %copy-done.1 = f32[1,1,1024]{2,1,0:T(1,128)S(1)} copy-done((f32[1,1,1024]{2,1,0:T(1,128)S(1)}, f32[1,1,1024]{2,1,0:T(1,128)}, u32[]{:S(2)}) %copy-start.1) | copy-done | bytes 4120
  5.6 0.0 copy-done.3
  5.6 0.0 copy-done.4
  5.6 0.0 copy-done.5
  5.6 0.0 copy-start
  5.6 0.1 group_lines.1.lines_ref
  5.7 0.0 collective-permute-done.other_ref
  5.7 0.6 %copy-done = s32[1,1,8,32]{3,2,1,0:T(8,128)S(1)} copy-done((s32[1,1,8,32]{3,2,1,0:T(8,128)S(1)}, s32[1,1,8,32]{3,2,1,0:T(8,128)}, u32[]{:S(2)}) %copy-start) | copy-done | bytes 1048
  6.3 0.7 %first_image.1 = (f32[8,24,128]{2,1,0:T(8,128)S(1)}, f32[16,128]{1,0:T(8,128)S(1)}) custom-call(f32[8,128]{1,0:T(8,128)S(1)} %bitcast.15, f32[8,128]{1,0:T(8,128)S(1)} %group_lines.1.lines_ref, f32[1,8,128]{2,1,0:T(8,128)S(1)} %collective-permute-done.other_ref, f32[4,32,4096]{2,1,0:T(8,128)S(1)} %wide_blocks.1.blocks_ref, s32[8,32]{1,0:T(8,128)S(1)} %bitcast.11), custom_call_target="tpu_custom_call" | custom-call | tf_op jit(solution)/shard_map/first_image/pallas_call | solution.py:274
  7.0 12.4 %all_to_all.10.group_ref = f32[8,24,128]{2,1,0:T(8,128)S(1)} all-to-all(f32[8,24,128]{2,1,0:T(8,128)S(1)} %get-tuple-element.14), channel_id=1, replica_groups=mesh['sub'=4,'blk'=2,'rep'=4] {'sub','blk'}, dimensions={0} | all-to-all | bytes 196608 | tf_op jit(solution)/shard_map/all_to_all | solution.py:283
  19.4 0.8 %second_image.1 = (f32[16,128]{1,0:T(8,128)S(1)}, f32[16,128]{1,0:T(8,128)S(1)}) custom-call(f32[8,24,128]{2,1,0:T(8,128)S(1)} %all_to_all.10.group_ref, f32[4,32,4096]{2,1,0:T(8,128)S(1)} %wide_blocks.1.blocks_ref, s32[8,32]{1,0:T(8,128)S(1)} %bitcast.12), custom_call_target="tpu_custom_call" | custom-call | tf_op jit(solution)/shard_map/second_image/pallas_call | solution.py:284
  20.2 0.4 %collective-permute-start.1 = (f32[1,16,128]{2,1,0:T(8,128)S(1)}, f32[1,16,128]{2,1,0:T(8,128)S(1)}, u32[]{:S(2)}, u32[]{:S(2)}) collective-permute-start(f32[1,16,128]{2,1,0:T(8,128)S(1)} %bitcast.17), channel_id=1, source_target_pairs={{4,0},{0,4},{5,1},{1,5},{6,2},{2,6},{7,3},{3,7},{12,8},{8,12},{13,... | collective-permute-start | bytes 24584 | tf_op jit(solution)/shard_map/ppermute | solution.py:249
  20.6 1.1 %second_inflow.1 = (f32[16,128]{1,0:T(8,128)S(1)}, f32[8,128]{1,0:T(8,128)S(1)}) custom-call(f32[16,128]{1,0:T(8,128)S(1)} %get-tuple-element.16.vector_ref, f32[16,128]{1,0:T(8,128)S(1)} %get-tuple-element.15.image_ref, f32[8,24,128]{2,1,0:T(8,128)S(1)} %all_to_all.10.group_ref, s32[1,2]{1,0:T(1,128)S(1)} %bitcast.22), custom_call_target="tpu_custom_call" | custom-call | flops 4294967296 | bytes 1048576 | tf_op jit(solution)/shard_map/second_inflow/pallas_call | solution.py:294
  21.7 2.2 %collective-permute-done.1.other_ref = f32[1,16,128]{2,1,0:T(8,128)S(1)} collective-permute-done((f32[1,16,128]{2,1,0:T(8,128)S(1)}, f32[1,16,128]{2,1,0:T(8,128)S(1)}, u32[]{:S(2)}, u32[]{:S(2)}) %collective-permute-start.1) | collective-permute-done | bytes 8224 | tf_op jit(solution)/shard_map/ppermute | solution.py:249
  23.9 0.1 pair_sums.1
  24.1 9.0 %all_to_all.11.sums_ref = f32[16,1,128]{2,1,0:T(1,128)S(1)} all-to-all(f32[16,1,128]{2,1,0:T(1,128)S(1)} %get-tuple-element.21), channel_id=1, replica_groups=mesh['sub'=4,'blk'=2,'rep'=4] {'rep','sub'}, dimensions={0} | all-to-all | bytes 16384 | tf_op jit(solution)/shard_map/all_to_all | solution.py:312
  33.1 0.7 %arnoldi_entries.1 = (f32[8,128]{1,0:T(8,128)}, f32[8,128]{1,0:T(8,128)}, f32[1,5]{1,0:T(1,128)}) custom-call(f32[8,128]{1,0:T(8,128)S(1)} %bitcast.16, f32[16,128]{1,0:T(8,128)S(1)} %get-tuple-element.15.image_ref, f32[16,128]{1,0:T(8,128)S(1)} %get-tuple-element.20.again_ref, f32[16,1,128]{2,1,0:T(1,128)S(1)} %all_to_all.11.sums_ref), custom_call_target="tpu_custom_call" | custom-call | tf_op jit(solution)/shard_map/arnoldi_entries/pallas_call | solution.py:313
Async XLA Ops:
  0.6 5.1 %collective-permute-start = (f32[1,8,128]{2,1,0:T(8,128)}, f32[1,8,128]{2,1,0:T(8,128)S(1)}, u32[]{:S(2)}, u32[]{:S(2)}) collective-permute-start(f32[1,8,128]{2,1,0:T(8,128)} %bitcast.13), channel_id=1, source_target_pairs={{4,0},{0,4},{5,1},{1,5},{6,2},{2,6},{7,3},{3,7},{12,8},{8,12},{13,... | collective-permute-start | bytes 12296 | tf_op jit(solution)/shard_map/ppermute | solution.py:249
  3.7 1.2 %copy-start.2 = (bf16[1,1,4,32,4096]{4,3,2,1,0:T(8,128)(2,1)S(1)}, bf16[1,1,4,32,4096]{4,3,2,1,0:T(8,128)(2,1)}, u32[]{:S(2)}) copy-start(bf16[1,1,4,32,4096]{4,3,2,1,0:T(8,128)(2,1)} %param.7) | copy-start | bytes 3145732
  4.9 0.7 %copy-start.1 = (f32[1,1,1024]{2,1,0:T(1,128)S(1)}, f32[1,1,1024]{2,1,0:T(1,128)}, u32[]{:S(2)}) copy-start(f32[1,1,1024]{2,1,0:T(1,128)} %param.6) | copy-start | bytes 12292
  4.9 0.7 %copy-start.3 = (f32[1,1,2,128]{3,2,1,0:T(2,128)S(1)}, f32[1,1,2,128]{3,2,1,0:T(2,128)}, u32[]{:S(2)}) copy-start(f32[1,1,2,128]{3,2,1,0:T(2,128)} %param.11) | copy-start | bytes 3076
  4.9 0.7 %copy-start.4 = (s32[1,1,128]{2,1,0:T(1,128)S(1)}, s32[1,1,128]{2,1,0:T(1,128)}, u32[]{:S(2)}) copy-start(s32[1,1,128]{2,1,0:T(1,128)} %param.9) | copy-start | bytes 1540
  4.9 0.7 %copy-start.5 = (s32[1,1,2]{2,1,0:T(1,128)S(1)}, s32[1,1,2]{2,1,0:T(1,128)}, u32[]{:S(2)}) copy-start(s32[1,1,2]{2,1,0:T(1,128)} %param.10) | copy-start | bytes 28
  5.6 0.7 %copy-start = (s32[1,1,8,32]{3,2,1,0:T(8,128)S(1)}, s32[1,1,8,32]{3,2,1,0:T(8,128)}, u32[]{:S(2)}) copy-start(s32[1,1,8,32]{3,2,1,0:T(8,128)} %param.8) | copy-start | bytes 3076
  20.2 3.7 %collective-permute-start.1 = (f32[1,16,128]{2,1,0:T(8,128)S(1)}, f32[1,16,128]{2,1,0:T(8,128)S(1)}, u32[]{:S(2)}, u32[]{:S(2)}) collective-permute-start(f32[1,16,128]{2,1,0:T(8,128)S(1)} %bitcast.17), channel_id=1, source_target_pairs={{4,0},{0,4},{5,1},{1,5},{6,2},{2,6},{7,3},{3,7},{12,8},{8,12},{13,... | collective-permute-start | bytes 24584 | tf_op jit(solution)/shard_map/ppermute | solution.py:249

commit v7 on v6

--- a/solution.py
+++ b/solution.py
@@ -29,7 +29,7 @@
     return lax.broadcasted_iota(jnp.int32, shape, 0)
 
 
-def block_product(vector, blocks_ref, pattern_ref, first_slot, fold_ref):
+def block_product(vector, blocks_ref, pattern_ref, first_slot, fold_ref, halves_ref):
     slots, block_rows, width = blocks_ref.shape
     half = block_rows // 2
     lower = lane_iota(vector.shape) < BS
@@ -49,18 +49,20 @@
     ones = (row_iota((2 * LANES, LANES)) % LANES) // BS == lane_iota((2 * LANES, LANES)) % 2
     ones = ones.astype(jnp.float32).astype(jnp.bfloat16)
     pair = (lane_iota((block_rows, LANES)) % BS) // 2
-    result = jnp.zeros((block_rows, LANES), jnp.float32)
-    for c in range(width // LANES):
+    chunks = width // LANES
+    for c in range(chunks):
         total = None
         for k in range(slots):
             term = blocks_ref[k, :, pl.ds(c * LANES, LANES)] * picked[k]
             total = term if total is None else total + term
         high = total.astype(jnp.bfloat16)
-        low = (total - high.astype(jnp.float32)).astype(jnp.bfloat16)
-        sums = lax.dot_general(
-            jnp.concatenate([high, low], 1), ones, (((1,), (0,)), ((), ())), preferred_element_type=jnp.float32
-        )
-        result = jnp.where(pair == c, sums, result)
+        here = pl.ds(c * block_rows, block_rows)
+        halves_ref[here, 0:LANES] = high
+        halves_ref[here, LANES : 2 * LANES] = (total - high.astype(jnp.float32)).astype(jnp.bfloat16)
+    sums = lax.dot_general(halves_ref[...], ones, (((1,), (0,)), ((), ())), preferred_element_type=jnp.float32)
+    result = sums[0:block_rows]
+    for c in range(1, chunks):
+        result = jnp.where(pair == c, sums[c * block_rows : (c + 1) * block_rows], result)
     fold_ref[...] = result
     even = fold_ref[pl.ds(0, half, stride=2), :]
     odd = fold_ref[pl.ds(1, half, stride=2), :]
@@ -101,14 +103,14 @@
     out_ref[...] = blocks_ref[...].astype(jnp.float32)
 
 
-def first_kernel(start_ref, lines_ref, other_ref, blocks_ref, pattern_ref, out_ref, vector_ref, fold_ref):
+def first_kernel(start_ref, lines_ref, other_ref, blocks_ref, pattern_ref, out_ref, vector_ref, fold_ref, halves_ref):
     own_rows, rows = start_ref.shape[0], vector_ref.shape[0]
     blk, parts = lax.axis_index("blk"), lax.axis_size("blk")
     for step in range(parts):
         place = lax.rem(blk + step, parts)
         place = pl.ds(pl.multiple_of(place * own_rows, SUBL), own_rows)
         vector_ref[place, :] = other_ref[step - 1] if step else start_ref[...]
-    partial = block_product(vector_ref[...], blocks_ref, pattern_ref, blk * blocks_ref.shape[0], fold_ref)
+    partial = block_product(vector_ref[...], blocks_ref, pattern_ref, blk * blocks_ref.shape[0], fold_ref, halves_ref)
     for device in range(out_ref.shape[0]):
         out_ref[device, 0:rows, :] = partial
         out_ref[device, rows : rows + SUBL, :] = lines_ref[...]
@@ -141,13 +143,13 @@
     return total
 
 
-def second_kernel(count, group_ref, blocks_ref, pattern_ref, out_ref, image_ref, fold_ref):
+def second_kernel(count, group_ref, blocks_ref, pattern_ref, out_ref, image_ref, fold_ref, halves_ref):
     rows = image_ref.shape[0]
     sub, blk, parts = lax.axis_index("sub"), lax.axis_index("blk"), lax.axis_size("blk")
     added = [landed(group_ref, sub, part, rows // parts, count)[0] for part in range(parts)]
     image = summed(group_ref, sub, 0, rows) + jnp.concatenate(added, 0)
     image_ref[...] = image
-    out_ref[...] = block_product(image, blocks_ref, pattern_ref, blk * blocks_ref.shape[0], fold_ref)
+    out_ref[...] = block_product(image, blocks_ref, pattern_ref, blk * blocks_ref.shape[0], fold_ref, halves_ref)
 
 
 def down(left, right):
@@ -252,7 +254,11 @@
         return got[0] if parts == 2 else jnp.concatenate(got, 0)
 
     others = from_others(start)
-    fold = pltpu.VMEM((blocks.shape[1], LANES), jnp.float32)
+    block_rows, width = blocks.shape[1:]
+    scratch = [
+        pltpu.VMEM((block_rows, LANES), jnp.float32),
+        pltpu.VMEM((block_rows * width // LANES, 2 * LANES), jnp.bfloat16),
+    ]
     lines = pl.pallas_call(
         lines_kernel,
         out_shape=rowed(SUBL),
@@ -276,7 +282,7 @@
         out_shape=(rowed(subs * parts, rows + SUBL), rowed(rows)),
         in_specs=[vmem] * 5,
         out_specs=(vmem, vmem),
-        scratch_shapes=[fold],
+        scratch_shapes=scratch,
         compiler_params=params,
         name="first_image",
     )(start, lines, others, wide, pattern)
@@ -286,7 +292,7 @@
         out_shape=(rowed(rows), rowed(rows)),
         in_specs=[vmem] * 3,
         out_specs=(vmem, vmem),
-        scratch_shapes=[fold],
+        scratch_shapes=scratch,
         compiler_params=params,
         name="second_image",
     )(group, wide, pattern)

time: 34.1 us -> 34 us (level)
  no operation moved by 1% of the time
where the time goes in v7:
time: 34 us; the launch traced here: 33.7 us
  blocking collectives  21.5 us (63%)
  Pallas kernels  3.62 us (11%)
  starting transfers between devices  3.4 us (10%)
  local copies, waits for them, and re-layouts  2.36 us (7%)
  waiting for transfers between devices  2.22 us (7%)
  between operations  0.67 us (2%)
    all_to_all x1, blocking collectives, per_device(): group = lax.all_to_all(partial, ('sub', 'blk'), 0, 0, tiled=True)  12.4 us
    all_to_all x1, blocking collectives, per_device(): sums = lax.all_to_all(sums, ('rep', 'sub'), 0, 0, tiled=True)  9.03 us
    ppermute x2, starting transfers between devices, from_others(): lax.ppermute(value[None], 'blk', [((i + step) % parts, i) for i in range(...  3.4 us
    unnamed x12, local copies, waits for them, and re-layouts  2.36 us
    ppermute x2, waiting for transfers between devices, from_others(): lax.ppermute(value[None], 'blk', [((i + step) % parts, i) for i in range(...  2.22 us
    pallas_call x1, Pallas kernels, per_device(): pl.pallas_call(inflow_kernel, out_shape=(rowed(rows), rowed(SUBL)), in_sp...  1.13 us
    pallas_call x1, Pallas kernels, per_device(): pl.pallas_call(functools.partial(second_kernel, coupling.shape[0]), out_s...  0.78 us
    pallas_call x1, Pallas kernels, per_device(): pl.pallas_call(functools.partial(last_kernel, float(cells)), out_shape=(r...  0.72 us
  transfers between devices with their start and end apart: 2, of which 1 were waited for; matrix products, arithmetic and copies ran while one was open for 0% of the time, Pallas kernels for 4%

profile of v7, /device:TPU:0, one launch (start us, length us, event | category | flops | bytes accessed | tf_op | source)
XLA Modules:
  0.0 33.7 jit_solution(12436584579420004040)
XLA Ops:
  0.6 3.0 %collective-permute-start = (f32[1,8,128]{2,1,0:T(8,128)}, f32[1,8,128]{2,1,0:T(8,128)S(1)}, u32[]{:S(2)}, u32[]{:S(2)}) collective-permute-start(f32[1,8,128]{2,1,0:T(8,128)} %bitcast.13), channel_id=1, source_target_pairs={{4,0},{0,4},{5,1},{1,5},{6,2},{2,6},{7,3},{3,7},{12,8},{8,12},{13,... | collective-permute-start | bytes 12296 | tf_op jit(solution)/shard_map/ppermute | solution.py:251
  3.7 0.0 copy-start.2
  3.7 1.2 %copy-done.2 = bf16[1,1,4,32,4096]{4,3,2,1,0:T(8,128)(2,1)S(1)} copy-done((bf16[1,1,4,32,4096]{4,3,2,1,0:T(8,128)(2,1)S(1)}, bf16[1,1,4,32,4096]{4,3,2,1,0:T(8,128)(2,1)}, u32[]{:S(2)}) %copy-start.2) | copy-done | bytes 1048600
  4.9 0.0 copy-start.1
  4.9 0.0 copy-start.3
  4.9 0.0 copy-start.4
  4.9 0.0 copy-start.5
  4.9 0.1 wide_blocks.1.blocks_ref
  5.0 0.5 %copy-done.1 = f32[1,1,1024]{2,1,0:T(1,128)S(1)} copy-done((f32[1,1,1024]{2,1,0:T(1,128)S(1)}, f32[1,1,1024]{2,1,0:T(1,128)}, u32[]{:S(2)}) %copy-start.1) | copy-done | bytes 4120
  5.6 0.0 copy-done.3
  5.6 0.0 copy-done.4
  5.6 0.0 copy-done.5
  5.6 0.0 copy-start
  5.6 0.1 group_lines.1.lines_ref
  5.7 0.0 collective-permute-done.other_ref
  5.7 0.6 %copy-done = s32[1,1,8,32]{3,2,1,0:T(8,128)S(1)} copy-done((s32[1,1,8,32]{3,2,1,0:T(8,128)S(1)}, s32[1,1,8,32]{3,2,1,0:T(8,128)}, u32[]{:S(2)}) %copy-start) | copy-done | bytes 1048
  6.3 0.6 %first_image.1 = (f32[8,24,128]{2,1,0:T(8,128)S(1)}, f32[16,128]{1,0:T(8,128)S(1)}) custom-call(f32[8,128]{1,0:T(8,128)S(1)} %bitcast.15, f32[8,128]{1,0:T(8,128)S(1)} %group_lines.1.lines_ref, f32[1,8,128]{2,1,0:T(8,128)S(1)} %collective-permute-done.other_ref, f32[4,32,4096]{2,1,0:T(8,128)S(1)} %wide_blocks.1.blocks_ref, s32[8,32]{1,0:T(8,128)S(1)} %bitcast.11), custom_call_target="tpu_custom_call" | custom-call | tf_op jit(solution)/shard_map/first_image/pallas_call | solution.py:280
  6.9 12.4 %all_to_all.10.group_ref = f32[8,24,128]{2,1,0:T(8,128)S(1)} all-to-all(f32[8,24,128]{2,1,0:T(8,128)S(1)} %get-tuple-element.14), channel_id=1, replica_groups=mesh['sub'=4,'blk'=2,'rep'=4] {'sub','blk'}, dimensions={0} | all-to-all | bytes 196608 | tf_op jit(solution)/shard_map/all_to_all | solution.py:289
  19.4 0.8 %second_image.1 = (f32[16,128]{1,0:T(8,128)S(1)}, f32[16,128]{1,0:T(8,128)S(1)}) custom-call(f32[8,24,128]{2,1,0:T(8,128)S(1)} %all_to_all.10.group_ref, f32[4,32,4096]{2,1,0:T(8,128)S(1)} %wide_blocks.1.blocks_ref, s32[8,32]{1,0:T(8,128)S(1)} %bitcast.12), custom_call_target="tpu_custom_call" | custom-call | tf_op jit(solution)/shard_map/second_image/pallas_call | solution.py:290
  20.1 0.4 %collective-permute-start.1 = (f32[1,16,128]{2,1,0:T(8,128)S(1)}, f32[1,16,128]{2,1,0:T(8,128)S(1)}, u32[]{:S(2)}, u32[]{:S(2)}) collective-permute-start(f32[1,16,128]{2,1,0:T(8,128)S(1)} %bitcast.17), channel_id=1, source_target_pairs={{4,0},{0,4},{5,1},{1,5},{6,2},{2,6},{7,3},{3,7},{12,8},{8,12},{13,... | collective-permute-start | bytes 24584 | tf_op jit(solution)/shard_map/ppermute | solution.py:251
  20.5 1.1 %second_inflow.1 = (f32[16,128]{1,0:T(8,128)S(1)}, f32[8,128]{1,0:T(8,128)S(1)}) custom-call(f32[16,128]{1,0:T(8,128)S(1)} %get-tuple-element.16.vector_ref, f32[16,128]{1,0:T(8,128)S(1)} %get-tuple-element.15.image_ref, f32[8,24,128]{2,1,0:T(8,128)S(1)} %all_to_all.10.group_ref, s32[1,2]{1,0:T(1,128)S(1)} %bitcast.22), custom_call_target="tpu_custom_call" | custom-call | flops 4294967296 | bytes 1048576 | tf_op jit(solution)/shard_map/second_inflow/pallas_call | solution.py:300
  21.6 2.2 %collective-permute-done.1.other_ref = f32[1,16,128]{2,1,0:T(8,128)S(1)} collective-permute-done((f32[1,16,128]{2,1,0:T(8,128)S(1)}, f32[1,16,128]{2,1,0:T(8,128)S(1)}, u32[]{:S(2)}, u32[]{:S(2)}) %collective-permute-start.1) | collective-permute-done | bytes 8224 | tf_op jit(solution)/shard_map/ppermute | solution.py:251
  23.9 0.1 pair_sums.1
  24.0 9.0 %all_to_all.11.sums_ref = f32[16,1,128]{2,1,0:T(1,128)S(1)} all-to-all(f32[16,1,128]{2,1,0:T(1,128)S(1)} %get-tuple-element.21), channel_id=1, replica_groups=mesh['sub'=4,'blk'=2,'rep'=4] {'rep','sub'}, dimensions={0} | all-to-all | bytes 16384 | tf_op jit(solution)/shard_map/all_to_all | solution.py:318
  33.0 0.7 %arnoldi_entries.1 = (f32[8,128]{1,0:T(8,128)}, f32[8,128]{1,0:T(8,128)}, f32[1,5]{1,0:T(1,128)}) custom-call(f32[8,128]{1,0:T(8,128)S(1)} %bitcast.16, f32[16,128]{1,0:T(8,128)S(1)} %get-tuple-element.15.image_ref, f32[16,128]{1,0:T(8,128)S(1)} %get-tuple-element.20.again_ref, f32[16,1,128]{2,1,0:T(1,128)S(1)} %all_to_all.11.sums_ref), custom_call_target="tpu_custom_call" | custom-call | tf_op jit(solution)/shard_map/arnoldi_entries/pallas_call | solution.py:319
Async XLA Ops:
  0.6 5.1 %collective-permute-start = (f32[1,8,128]{2,1,0:T(8,128)}, f32[1,8,128]{2,1,0:T(8,128)S(1)}, u32[]{:S(2)}, u32[]{:S(2)}) collective-permute-start(f32[1,8,128]{2,1,0:T(8,128)} %bitcast.13), channel_id=1, source_target_pairs={{4,0},{0,4},{5,1},{1,5},{6,2},{2,6},{7,3},{3,7},{12,8},{8,12},{13,... | collective-permute-start | bytes 12296 | tf_op jit(solution)/shard_map/ppermute | solution.py:251
  3.7 1.2 %copy-start.2 = (bf16[1,1,4,32,4096]{4,3,2,1,0:T(8,128)(2,1)S(1)}, bf16[1,1,4,32,4096]{4,3,2,1,0:T(8,128)(2,1)}, u32[]{:S(2)}) copy-start(bf16[1,1,4,32,4096]{4,3,2,1,0:T(8,128)(2,1)} %param.7) | copy-start | bytes 3145732
  4.9 0.7 %copy-start.1 = (f32[1,1,1024]{2,1,0:T(1,128)S(1)}, f32[1,1,1024]{2,1,0:T(1,128)}, u32[]{:S(2)}) copy-start(f32[1,1,1024]{2,1,0:T(1,128)} %param.6) | copy-start | bytes 12292
  4.9 0.7 %copy-start.3 = (f32[1,1,2,128]{3,2,1,0:T(2,128)S(1)}, f32[1,1,2,128]{3,2,1,0:T(2,128)}, u32[]{:S(2)}) copy-start(f32[1,1,2,128]{3,2,1,0:T(2,128)} %param.11) | copy-start | bytes 3076
  4.9 0.7 %copy-start.4 = (s32[1,1,128]{2,1,0:T(1,128)S(1)}, s32[1,1,128]{2,1,0:T(1,128)}, u32[]{:S(2)}) copy-start(s32[1,1,128]{2,1,0:T(1,128)} %param.9) | copy-start | bytes 1540
  4.9 0.7 %copy-start.5 = (s32[1,1,2]{2,1,0:T(1,128)S(1)}, s32[1,1,2]{2,1,0:T(1,128)}, u32[]{:S(2)}) copy-start(s32[1,1,2]{2,1,0:T(1,128)} %param.10) | copy-start | bytes 28
  5.6 0.7 %copy-start = (s32[1,1,8,32]{3,2,1,0:T(8,128)S(1)}, s32[1,1,8,32]{3,2,1,0:T(8,128)}, u32[]{:S(2)}) copy-start(s32[1,1,8,32]{3,2,1,0:T(8,128)} %param.8) | copy-start | bytes 3076
  20.1 3.7 %collective-permute-start.1 = (f32[1,16,128]{2,1,0:T(8,128)S(1)}, f32[1,16,128]{2,1,0:T(8,128)S(1)}, u32[]{:S(2)}, u32[]{:S(2)}) collective-permute-start(f32[1,16,128]{2,1,0:T(8,128)S(1)} %bitcast.17), channel_id=1, source_target_pairs={{4,0},{0,4},{5,1},{1,5},{6,2},{2,6},{7,3},{3,7},{12,8},{8,12},{13,... | collective-permute-start | bytes 24584 | tf_op jit(solution)/shard_map/ppermute | solution.py:251

commit v8 on v7

--- a/solution.py
+++ b/solution.py
@@ -96,29 +96,40 @@
     near = near_ref[...].astype(jnp.float32)
     lines += [jnp.broadcast_to(near[:, n : n + 1], (1, LANES)) for n in range(count)]
     lines += [jnp.zeros((SUBL - len(lines), LANES), jnp.float32)]
-    out_ref[...] = jnp.concatenate(lines, 0)
+    lines = jnp.concatenate(lines, 0)
+    for device in range(out_ref.shape[0]):
+        out_ref[device] = lines
 
 
 def widen_kernel(blocks_ref, out_ref):
     out_ref[...] = blocks_ref[...].astype(jnp.float32)
 
 
-def first_kernel(start_ref, lines_ref, other_ref, blocks_ref, pattern_ref, out_ref, vector_ref, fold_ref, halves_ref):
-    own_rows, rows = start_ref.shape[0], vector_ref.shape[0]
-    blk, parts = lax.axis_index("blk"), lax.axis_size("blk")
+def in_order(parts_ref, mine, other_ref):
+    parts = parts_ref.shape[0]
     for step in range(parts):
-        place = lax.rem(blk + step, parts)
-        place = pl.ds(pl.multiple_of(place * own_rows, SUBL), own_rows)
-        vector_ref[place, :] = other_ref[step - 1] if step else start_ref[...]
-    partial = block_product(vector_ref[...], blocks_ref, pattern_ref, blk * blocks_ref.shape[0], fold_ref, halves_ref)
+        parts_ref[lax.rem(lax.axis_index("blk") + step, parts)] = other_ref[step - 1] if step else mine
+    total = parts_ref[0]
+    for part in range(1, parts):
+        total = total + parts_ref[part]
+    return total
+
+
+def first_kernel(
+    start_ref, other_ref, blocks_ref, pattern_ref, out_ref, partial_ref, vector_ref, parts_ref, fold_ref, halves_ref
+):
+    in_order(parts_ref, start_ref[...], other_ref)
+    vector = jnp.concatenate([parts_ref[part] for part in range(parts_ref.shape[0])], 0)
+    vector_ref[...] = vector
+    blk = lax.axis_index("blk")
+    partial = block_product(vector, blocks_ref, pattern_ref, blk * blocks_ref.shape[0], fold_ref, halves_ref)
+    partial_ref[...] = partial
     for device in range(out_ref.shape[0]):
-        out_ref[device, 0:rows, :] = partial
-        out_ref[device, rows : rows + SUBL, :] = lines_ref[...]
+        out_ref[device] = partial
 
 
 def line(group_ref, device, i):
-    first = group_ref.shape[1] - SUBL + i
-    return group_ref[device, first : first + 1, :]
+    return group_ref[device, i : i + 1, :]
 
 
 def landed(group_ref, sub_at, part, own_rows, count):
@@ -135,19 +146,13 @@
     return spread(inflow, places, own_rows), places
 
 
-def summed(group_ref, sub_at, first, count):
-    parts = lax.axis_size("blk")
-    total = group_ref[sub_at * parts, first : first + count, :]
-    for b in range(1, parts):
-        total = total + group_ref[sub_at * parts + b, first : first + count, :]
-    return total
-
-
-def second_kernel(count, group_ref, blocks_ref, pattern_ref, out_ref, image_ref, fold_ref, halves_ref):
-    rows = image_ref.shape[0]
-    sub, blk, parts = lax.axis_index("sub"), lax.axis_index("blk"), lax.axis_size("blk")
-    added = [landed(group_ref, sub, part, rows // parts, count)[0] for part in range(parts)]
-    image = summed(group_ref, sub, 0, rows) + jnp.concatenate(added, 0)
+def second_kernel(
+    count, lines_ref, mine_ref, other_ref, blocks_ref, pattern_ref, out_ref, image_ref, parts_ref, fold_ref, halves_ref
+):
+    parts, rows, _ = parts_ref.shape
+    sub, blk = lax.axis_index("sub"), lax.axis_index("blk")
+    added = [landed(lines_ref, sub, part, rows // parts, count)[0] for part in range(parts)]
+    image = in_order(parts_ref, mine_ref[...], other_ref) + jnp.concatenate(added, 0)
     image_ref[...] = image
     out_ref[...] = block_product(image, blocks_ref, pattern_ref, blk * blocks_ref.shape[0], fold_ref, halves_ref)
 
@@ -156,36 +161,46 @@
     return jnp.sum(left * right, axis=0, keepdims=True)
 
 
-def inflow_kernel(vector_ref, image_ref, group_ref, near_ref, out_ref, sums_ref):
-    rows = image_ref.shape[0]
+def early_kernel(vector_ref, image_ref, lines_ref, near_ref, out_ref):
+    vector, image = vector_ref[...], image_ref[...]
+    own_rows = image.shape[0] // lax.axis_size("blk")
+    sub, parts = lax.axis_index("sub"), lax.axis_size("blk")
+    known = [down(vector, vector), down(vector, image), down(image, image)]
     count = near_ref.shape[1]
-    sub, parts = lax.axis_index("sub"), lax.axis_size("blk")
+    for part in range(parts):
+        share = jnp.zeros((1, LANES), jnp.float32)
+        for n in range(count):
+            added, places = landed(lines_ref, near_ref[0, n], part, own_rows, count)
+            share = share + line(lines_ref, sub * parts + part, 2 + n) * take_trace(added, places)
+        known.append(share)
+    known.append(jnp.zeros((out_ref.shape[0] - len(known), LANES), jnp.float32))
+    out_ref[...] = jnp.concatenate(known, 0)
+
+
+def pair_kernel(
+    vector_ref, image_ref, known_ref, lines_ref, group_ref, near_ref, mine_ref, other_ref, out_ref, again_ref, parts_ref
+):
+    parts, rows, _ = parts_ref.shape
     own_rows = rows // parts
+    sub = lax.axis_index("sub")
+    inflows = []
     for part in range(parts):
-        device = sub * parts + part
-        inflow = jnp.zeros((1, LANES), jnp.float32)
-        for n in range(count):
-            source = near_ref[0, n]
-            added, places = landed(group_ref, source, part, own_rows, count)
-            trace = take_trace(summed(group_ref, source, part * own_rows, own_rows) + added, places)
-            inflow = inflow + line(group_ref, device, 2 + n) * trace
-        places = line(group_ref, device, 1).astype(jnp.int32) - part * own_rows * LANES
-        out_ref[part * own_rows : (part + 1) * own_rows, :] = spread(inflow, places, own_rows)
-    vector, image = vector_ref[...], image_ref[...]
-    sums = [down(vector, vector), down(vector, image), down(image, image)]
-    sums_ref[...] = jnp.concatenate([*sums, jnp.zeros((SUBL - len(sums), LANES), jnp.float32)], 0)
-
-
-def pair_kernel(vector_ref, image_ref, sums_ref, inflow_ref, mine_ref, other_ref, out_ref, again_ref, part_ref):
-    parts = part_ref.shape[0]
-    for step in range(parts):
-        part_ref[lax.rem(lax.axis_index("blk") + step, parts)] = other_ref[step - 1] if step else mine_ref[...]
-    again = inflow_ref[...]
-    for part in range(parts):
-        again = again + part_ref[part]
+        inflow = known_ref[3 + part : 4 + part, :]
+        first_cell = part * own_rows * LANES
+        here = slice(part * own_rows, (part + 1) * own_rows)
+        for n in range(near_ref.shape[1]):
+            source = near_ref[0, n] * parts
+            image = group_ref[source, here, :]
+            for b in range(1, parts):
+                image = image + group_ref[source + b, here, :]
+            trace = take_trace(image, line(lines_ref, source + part, 1).astype(jnp.int32) - first_cell)
+            inflow = inflow + line(lines_ref, sub * parts + part, 2 + n) * trace
+        places = line(lines_ref, sub * parts + part, 1).astype(jnp.int32) - first_cell
+        inflows.append(spread(inflow, places, own_rows))
+    again = in_order(parts_ref, mine_ref[...], other_ref) + jnp.concatenate(inflows, 0)
     again_ref[...] = again
     sums = [down(vector_ref[...], again), down(image_ref[...], again), down(again, again)]
-    sums = jnp.concatenate([sums_ref[0:3, :], *sums, sums_ref[6:SUBL, :]], 0)
+    sums = jnp.concatenate([known_ref[0:3, :], *sums, jnp.zeros((SUBL - 6, LANES), jnp.float32)], 0)
     sums = jnp.sum(sums, axis=1, keepdims=True)
     sums = jnp.where(row_iota((SUBL, LANES)) == lane_iota((SUBL, LANES)), sums, 0.0)
     sums = jnp.sum(sums, axis=0, keepdims=True)
@@ -253,68 +268,73 @@
         ]
         return got[0] if parts == 2 else jnp.concatenate(got, 0)
 
-    others = from_others(start)
     block_rows, width = blocks.shape[1:]
     scratch = [
         pltpu.VMEM((block_rows, LANES), jnp.float32),
         pltpu.VMEM((block_rows * width // LANES, 2 * LANES), jnp.bfloat16),
     ]
+    in_parts = pltpu.VMEM((parts, rows, LANES), jnp.float32)
+    long = pl.CostEstimate(flops=1 << 32, bytes_accessed=1 << 20, transcendentals=0)
+
+    others = from_others(start)
     lines = pl.pallas_call(
         lines_kernel,
-        out_shape=rowed(SUBL),
+        out_shape=rowed(subs * parts, SUBL),
         in_specs=[vmem] * 4,
         out_specs=vmem,
         compiler_params=params,
-        cost_estimate=pl.CostEstimate(flops=1 << 32, bytes_accessed=1 << 20, transcendentals=0),
+        cost_estimate=long,
         name="group_lines",
     )(start, local_map, neighbours, coupling)
+    lines = lax.all_to_all(lines, ("sub", "blk"), 0, 0, tiled=True)
     wide = pl.pallas_call(
         widen_kernel,
         out_shape=jax.ShapeDtypeStruct(blocks.shape, jnp.float32),
         in_specs=[vmem],
         out_specs=vmem,
         compiler_params=params,
-        cost_estimate=pl.CostEstimate(flops=1 << 32, bytes_accessed=3 << 20, transcendentals=0),
+        cost_estimate=long,
         name="wide_blocks",
     )(blocks)
-    partial, vector = pl.pallas_call(
+    slots, partial, vector = pl.pallas_call(
         first_kernel,
-        out_shape=(rowed(subs * parts, rows + SUBL), rowed(rows)),
-        in_specs=[vmem] * 5,
-        out_specs=(vmem, vmem),
-        scratch_shapes=scratch,
+        out_shape=(rowed(subs * parts, rows), rowed(rows), rowed(rows)),
+        in_specs=[vmem] * 4,
+        out_specs=(vmem, vmem, vmem),
+        scratch_shapes=[pltpu.VMEM((parts, own_rows, LANES), jnp.float32), *scratch],
         compiler_params=params,
         name="first_image",
-    )(start, lines, others, wide, pattern)
-    group = lax.all_to_all(partial, ("sub", "blk"), 0, 0, tiled=True)
+    )(start, others, wide, pattern)
+    others = from_others(partial)
+    group = lax.all_to_all(slots, ("sub", "blk"), 0, 0, tiled=True)
     second, image = pl.pallas_call(
         functools.partial(second_kernel, coupling.shape[0]),
         out_shape=(rowed(rows), rowed(rows)),
-        in_specs=[vmem] * 3,
+        in_specs=[vmem] * 5,
         out_specs=(vmem, vmem),
-        scratch_shapes=scratch,
+        scratch_shapes=[in_parts, *scratch],
         compiler_params=params,
         name="second_image",
-    )(group, wide, pattern)
+    )(lines, partial, others, wide, pattern)
     others = from_others(second)
-    inflow, sums = pl.pallas_call(
-        inflow_kernel,
-        out_shape=(rowed(rows), rowed(SUBL)),
+    known = pl.pallas_call(
+        early_kernel,
+        out_shape=rowed(SUBL * pl.cdiv(3 + parts, SUBL)),
         in_specs=[vmem, vmem, vmem, smem],
-        out_specs=(vmem, vmem),
-        compiler_params=params,
-        cost_estimate=pl.CostEstimate(flops=1 << 32, bytes_accessed=1 << 20, transcendentals=0),
-        name="second_inflow",
-    )(vector, image, group, neighbours)
+        out_specs=vmem,
+        compiler_params=params,
+        cost_estimate=long,
+        name="known_sums",
+    )(vector, image, lines, neighbours)
     sums, again = pl.pallas_call(
         pair_kernel,
         out_shape=(rowed(reps * subs, 1), rowed(rows)),
-        in_specs=[vmem] * 6,
+        in_specs=[vmem] * 5 + [smem] + [vmem] * 2,
         out_specs=(vmem, vmem),
-        scratch_shapes=[pltpu.VMEM((parts, rows, LANES), jnp.float32)],
+        scratch_shapes=[in_parts],
         compiler_params=params,
         name="pair_sums",
-    )(vector, image, sums, inflow, second, others)
+    )(vector, image, known, lines, group, neighbours, second, others)
     sums = lax.all_to_all(sums, ("rep", "sub"), 0, 0, tiled=True)
     second, third, entries = pl.pallas_call(
         functools.partial(last_kernel, float(cells)),

time: 34 us -> 41.5 us (1.22)
  starting transfers between devices: 3.4 us -> 17.7 us
  blocking collectives: 21.5 us -> 9.9 us
  waiting for transfers between devices: 2.22 us -> 4.88 us
  Pallas kernels: 3.62 us -> 5.3 us
    all_to_all x1 -> x0, blocking collectives: 12.4 us -> none  [per_device(): group = lax.all_to_all(partial, ('sub', 'blk'), 0, 0, tiled=True)]
    all_to_all x0 -> x2, starting transfers between devices: none -> 11.8 us  [the longest x1 7.28 us: per_device(): lines = lax.all_to_all(lines, ('sub', 'blk'), 0, 0, tiled=True)]
    ppermute x2 -> x3, starting transfers between devices: 3.4 us -> 5.87 us  [from_others(): lax.ppermute(value[None], 'blk', [((i + step) % parts, i) for i in range(...]
    all_to_all x0 -> x2, waiting for transfers between devices: none -> 2.4 us  [the longest x1 2.39 us: per_device(): group = lax.all_to_all(slots, ('sub', 'blk'), 0, 0, tiled=True)]
    pallas_call x3, Pallas kernels: 1.86 us -> 2.8 us  [the longest x1 1.27 us: per_device(): pl.pallas_call(first_kernel, out_shape=(rowed(subs * parts, rows), rowed(...]
    all_to_all x1, blocking collectives: 9.03 us -> 9.9 us  [per_device(): sums = lax.all_to_all(sums, ('rep', 'sub'), 0, 0, tiled=True)]
    pallas_call x1, Pallas kernels: 0.11 us -> 0.86 us  [per_device(): pl.pallas_call(pair_kernel, out_shape=(rowed(reps * subs, 1), rowed(rows)...]
    unnamed x12 -> x16, local copies, waits for them, and re-layouts: 2.36 us -> 2.68 us
  transfers between devices with their start and end apart: 2 -> 5, of which waited for: 1 -> 3; matrix products, arithmetic and copies ran while one was open for 0% -> 0% of each run, Pallas kernels for 4% -> 7%
where the time goes in v8:
time: 41.5 us; the launch traced here: 41.1 us
  starting transfers between devices  17.7 us (43%)
  blocking collectives  9.9 us (24%)
  Pallas kernels  5.3 us (13%)
  waiting for transfers between devices  4.88 us (12%)
  local copies, waits for them, and re-layouts  2.68 us (6%)
  between operations  0.68 us (2%)
    all_to_all x1, blocking collectives, per_device(): sums = lax.all_to_all(sums, ('rep', 'sub'), 0, 0, tiled=True)  9.9 us
    all_to_all x1, starting transfers between devices, per_device(): lines = lax.all_to_all(lines, ('sub', 'blk'), 0, 0, tiled=True)  7.28 us
    ppermute x3, starting transfers between devices, from_others(): lax.ppermute(value[None], 'blk', [((i + step) % parts, i) for i in range(...  5.87 us
    all_to_all x1, starting transfers between devices, per_device(): group = lax.all_to_all(slots, ('sub', 'blk'), 0, 0, tiled=True)  4.54 us
    unnamed x16, local copies, waits for them, and re-layouts  2.68 us
    ppermute x3, waiting for transfers between devices, from_others(): lax.ppermute(value[None], 'blk', [((i + step) % parts, i) for i in range(...  2.49 us
    all_to_all x1, waiting for transfers between devices, per_device(): group = lax.all_to_all(slots, ('sub', 'blk'), 0, 0, tiled=True)  2.39 us
    pallas_call x1, Pallas kernels, per_device(): pl.pallas_call(first_kernel, out_shape=(rowed(subs * parts, rows), rowed(...  1.27 us
  transfers between devices with their start and end apart: 5, of which 3 were waited for; matrix products, arithmetic and copies ran while one was open for 0% of the time, Pallas kernels for 7%

profile of v8, /device:TPU:0, one launch (start us, length us, event | category | flops | bytes accessed | tf_op | source)
XLA Modules:
  0.0 41.1 jit_solution(8573142314909501392)
XLA Ops:
  0.6 0.0 copy-start.1
  0.6 0.7 %copy-done.1 = f32[1,1,1024]{2,1,0:T(1,128)S(1)} copy-done((f32[1,1,1024]{2,1,0:T(1,128)S(1)}, f32[1,1,1024]{2,1,0:T(1,128)}, u32[]{:S(2)}) %copy-start.1) | copy-done | bytes 4120
  1.3 0.0 copy-start.3
  1.3 0.7 %copy-done.3 = s32[1,1,2]{2,1,0:T(1,128)S(1)} copy-done((s32[1,1,2]{2,1,0:T(1,128)S(1)}, s32[1,1,2]{2,1,0:T(1,128)}, u32[]{:S(2)}) %copy-start.3) | copy-done | bytes 32
  2.0 0.0 copy-start.6
  2.0 0.7 %copy-done.6 = f32[1,1,2,128]{3,2,1,0:T(2,128)S(1)} copy-done((f32[1,1,2,128]{3,2,1,0:T(2,128)S(1)}, f32[1,1,2,128]{3,2,1,0:T(2,128)}, u32[]{:S(2)}) %copy-start.6) | copy-done | bytes 1048
  2.7 0.0 copy-start.7
  2.7 0.7 %copy-done.7 = s32[1,1,128]{2,1,0:T(1,128)S(1)} copy-done((s32[1,1,128]{2,1,0:T(1,128)S(1)}, s32[1,1,128]{2,1,0:T(1,128)}, u32[]{:S(2)}) %copy-start.7) | copy-done | bytes 536
  3.3 0.0 copy-start.2
  3.3 0.0 copy-start.5
  3.3 0.7 %group_lines.1 = f32[8,8,128]{2,1,0:T(8,128)} custom-call(f32[8,128]{1,0:T(8,128)S(1)} %bitcast.14, s32[1,128]{1,0:T(1,128)S(1)} %bitcast.25, s32[1,2]{1,0:T(1,128)S(1)} %bitcast.20, f32[2,128]{1,0:T(2,128)S(1)} %bitcast.24), custom_call_target="tpu_custom_call" | custom-call | flops 4294967296 | bytes 1048576 | tf_op jit(solution)/shard_map/group_lines/pallas_call | solution.py:280
  4.0 7.3 %all-to-all-start = ((f32[8,8,128]{2,1,0:T(8,128)}), f32[8,8,128]{2,1,0:T(8,128)S(1)}, u32[]{:S(2)}, u32[]{:S(2)}) async-start(f32[8,8,128]{2,1,0:T(8,128)} %group_lines.1), calls=%async_computation | async-start | bytes 65536 | tf_op jit(solution)/shard_map/all_to_all | solution.py:289
  11.3 0.0 copy-done.2
  11.3 2.0 %collective-permute-start = (f32[1,8,128]{2,1,0:T(8,128)S(1)}, f32[1,8,128]{2,1,0:T(8,128)S(1)}, u32[]{:S(2)}, u32[]{:S(2)}) collective-permute-start(f32[1,8,128]{2,1,0:T(8,128)S(1)} %bitcast.15), channel_id=1, source_target_pairs={{4,0},{0,4},{5,1},{1,5},{6,2},{2,6},{7,3},{3,7},{12,8},{8,12},{13,... | collective-permute-start | bytes 12296 | tf_op jit(solution)/shard_map/ppermute | solution.py:266
  13.3 0.0 copy-done.5
  13.3 0.0 copy-start
  13.3 0.1 wide_blocks.1.blocks_ref
  13.5 1.7 %collective-permute-done.other_ref = f32[1,8,128]{2,1,0:T(8,128)S(1)} collective-permute-done((f32[1,8,128]{2,1,0:T(8,128)S(1)}, f32[1,8,128]{2,1,0:T(8,128)S(1)}, u32[]{:S(2)}, u32[]{:S(2)}) %collective-permute-start) | collective-permute-done | bytes 4128 | tf_op jit(solution)/shard_map/ppermute | solution.py:266
  15.2 0.0 copy-done
  15.2 0.0 copy-start.4
  15.2 1.3 %first_image.1 = (f32[8,16,128]{2,1,0:T(8,128)}, f32[16,128]{1,0:T(8,128)S(1)}, f32[16,128]{1,0:T(8,128)S(1)}) custom-call(f32[8,128]{1,0:T(8,128)S(1)} %bitcast.16, f32[1,8,128]{2,1,0:T(8,128)S(1)} %collective-permute-done.other_ref, f32[4,32,4096]{2,1,0:T(8,128)S(1)} %wide_blocks.1.blocks_ref, s32[8,32]{1,0:T(8,128)S(1)} %bitcast.12), custom_call_target="tpu_custom_call" | custom-call | tf_op jit(solution)/shard_map/first_image/pallas_call | solution.py:299
  16.4 1.8 %collective-permute-start.1 = (f32[1,16,128]{2,1,0:T(8,128)S(1)}, f32[1,16,128]{2,1,0:T(8,128)S(1)}, u32[]{:S(2)}, u32[]{:S(2)}) collective-permute-start(f32[1,16,128]{2,1,0:T(8,128)S(1)} %bitcast.18), channel_id=1, source_target_pairs={{4,0},{0,4},{5,1},{1,5},{6,2},{2,6},{7,3},{3,7},{12,8},{8,12},{13,... | collective-permute-start | bytes 24584 | tf_op jit(solution)/shard_map/ppermute | solution.py:266
  18.2 0.0 all-to-all-done.lines_ref
  18.2 4.5 %all-to-all-start.1 = ((f32[8,16,128]{2,1,0:T(8,128)}), f32[8,16,128]{2,1,0:T(8,128)S(1)}, u32[]{:S(2)}, u32[]{:S(2)}) async-start(f32[8,16,128]{2,1,0:T(8,128)} %get-tuple-element.16), calls=%async_computation.1 | async-start | bytes 131072 | tf_op jit(solution)/shard_map/all_to_all | solution.py:309
  22.7 0.0 collective-permute-done.1.other_ref
  22.8 0.8 %second_image.1 = (f32[16,128]{1,0:T(8,128)S(1)}, f32[16,128]{1,0:T(8,128)S(1)}) custom-call(f32[8,8,128]{2,1,0:T(8,128)S(1)} %all-to-all-done.lines_ref, f32[16,128]{1,0:T(8,128)S(1)} %get-tuple-element.13.mine_ref, f32[1,16,128]{2,1,0:T(8,128)S(1)} %collective-permute-done.1.other_ref, f32[4,32,4096]{2,1,0:T(8,128)S(1)} %wide_blocks.1.blocks_ref, ...), custom_call_target="tpu_custom_call" | custom-call | tf_op jit(solution)/shard_map/second_image/pallas_call | solution.py:310
  23.5 2.1 %collective-permute-start.2 = (f32[1,16,128]{2,1,0:T(8,128)S(1)}, f32[1,16,128]{2,1,0:T(8,128)S(1)}, u32[]{:S(2)}, u32[]{:S(2)}) collective-permute-start(f32[1,16,128]{2,1,0:T(8,128)S(1)} %bitcast.19), channel_id=1, source_target_pairs={{4,0},{0,4},{5,1},{1,5},{6,2},{2,6},{7,3},{3,7},{12,8},{8,12},{13,... | collective-permute-start | bytes 24584 | tf_op jit(solution)/shard_map/ppermute | solution.py:266
  25.6 0.0 copy-done.4
  25.6 0.8 %known_sums.1.known_ref = f32[8,128]{1,0:T(8,128)S(1)} custom-call(f32[16,128]{1,0:T(8,128)S(1)} %get-tuple-element.15.vector_ref, f32[16,128]{1,0:T(8,128)S(1)} %get-tuple-element.14.image_ref, f32[8,8,128]{2,1,0:T(8,128)S(1)} %all-to-all-done.lines_ref, s32[1,2]{1,0:T(1,128)S(1)} %bitcast.21), custom_call_target="tpu_custom_call" | custom-call | flops 4294967296 | bytes 1048576 | tf_op jit(solution)/shard_map/known_sums/pallas_call | solution.py:320
  26.5 0.8 %collective-permute-done.2.other_ref = f32[1,16,128]{2,1,0:T(8,128)S(1)} collective-permute-done((f32[1,16,128]{2,1,0:T(8,128)S(1)}, f32[1,16,128]{2,1,0:T(8,128)S(1)}, u32[]{:S(2)}, u32[]{:S(2)}) %collective-permute-start.2) | collective-permute-done | bytes 8224 | tf_op jit(solution)/shard_map/ppermute | solution.py:266
  27.3 2.4 %all-to-all-done.1.group_ref = f32[8,16,128]{2,1,0:T(8,128)S(1)} async-done(((f32[8,16,128]{2,1,0:T(8,128)}), f32[8,16,128]{2,1,0:T(8,128)S(1)}, u32[]{:S(2)}, u32[]{:S(2)}) %all-to-all-start.1) | async-done | bytes 65568 | tf_op jit(solution)/shard_map/all_to_all | solution.py:309
  29.7 0.9 %pair_sums.1 = (f32[16,1,128]{2,1,0:T(1,128)S(1)}, f32[16,128]{1,0:T(8,128)S(1)}) custom-call(f32[16,128]{1,0:T(8,128)S(1)} %get-tuple-element.15.vector_ref, f32[16,128]{1,0:T(8,128)S(1)} %get-tuple-element.14.image_ref, f32[8,128]{1,0:T(8,128)S(1)} %known_sums.1.known_ref, f32[8,8,128]{2,1,0:T(8,128)S(1)} %all-to-all-done.lines_ref, ...), custom_call_target="tpu_custom_call" | custom-call | tf_op jit(solution)/shard_map/pair_sums/pallas_call | solution.py:329
  30.5 9.9 %all_to_all.15.sums_ref = f32[16,1,128]{2,1,0:T(1,128)S(1)} all-to-all(f32[16,1,128]{2,1,0:T(1,128)S(1)} %get-tuple-element.19), channel_id=1, replica_groups=mesh['sub'=4,'blk'=2,'rep'=4] {'rep','sub'}, dimensions={0} | all-to-all | bytes 16384 | tf_op jit(solution)/shard_map/all_to_all | solution.py:338
  40.4 0.7 %arnoldi_entries.1 = (f32[8,128]{1,0:T(8,128)}, f32[8,128]{1,0:T(8,128)}, f32[1,5]{1,0:T(1,128)}) custom-call(f32[8,128]{1,0:T(8,128)S(1)} %bitcast.17, f32[16,128]{1,0:T(8,128)S(1)} %get-tuple-element.14.image_ref, f32[16,128]{1,0:T(8,128)S(1)} %get-tuple-element.18.again_ref, f32[16,1,128]{2,1,0:T(1,128)S(1)} %all_to_all.15.sums_ref), custom_call_target="tpu_custom_call" | custom-call | tf_op jit(solution)/shard_map/arnoldi_entries/pallas_call | solution.py:339
Async XLA Ops:
  0.6 0.7 %copy-start.1 = (f32[1,1,1024]{2,1,0:T(1,128)S(1)}, f32[1,1,1024]{2,1,0:T(1,128)}, u32[]{:S(2)}) copy-start(f32[1,1,1024]{2,1,0:T(1,128)} %param.6) | copy-start | bytes 12292
  1.3 0.7 %copy-start.3 = (s32[1,1,2]{2,1,0:T(1,128)S(1)}, s32[1,1,2]{2,1,0:T(1,128)}, u32[]{:S(2)}) copy-start(s32[1,1,2]{2,1,0:T(1,128)} %param.10) | copy-start | bytes 28
  2.0 0.7 %copy-start.6 = (f32[1,1,2,128]{3,2,1,0:T(2,128)S(1)}, f32[1,1,2,128]{3,2,1,0:T(2,128)}, u32[]{:S(2)}) copy-start(f32[1,1,2,128]{3,2,1,0:T(2,128)} %param.11) | copy-start | bytes 3076
  2.7 0.7 %copy-start.7 = (s32[1,1,128]{2,1,0:T(1,128)S(1)}, s32[1,1,128]{2,1,0:T(1,128)}, u32[]{:S(2)}) copy-start(s32[1,1,128]{2,1,0:T(1,128)} %param.9) | copy-start | bytes 1540
  3.3 8.0 %copy-start.2 = (f32[1,1,1024]{2,1,0:T(1,128)S(1)}, f32[1,1,1024]{2,1,0:T(1,128)}, u32[]{:S(2)}) copy-start(f32[1,1,1024]{2,1,0:T(1,128)} %param.6) | copy-start | bytes 12292
  3.3 10.0 %copy-start.5 = (bf16[1,1,4,32,4096]{4,3,2,1,0:T(8,128)(2,1)S(1)}, bf16[1,1,4,32,4096]{4,3,2,1,0:T(8,128)(2,1)}, u32[]{:S(2)}) copy-start(bf16[1,1,4,32,4096]{4,3,2,1,0:T(8,128)(2,1)} %param.7) | copy-start | bytes 3145732
  4.0 14.2 %all-to-all-start = ((f32[8,8,128]{2,1,0:T(8,128)}), f32[8,8,128]{2,1,0:T(8,128)S(1)}, u32[]{:S(2)}, u32[]{:S(2)}) async-start(f32[8,8,128]{2,1,0:T(8,128)} %group_lines.1), calls=%async_computation | async-start | bytes 65536 | tf_op jit(solution)/shard_map/all_to_all | solution.py:289
  11.3 3.8 %collective-permute-start = (f32[1,8,128]{2,1,0:T(8,128)S(1)}, f32[1,8,128]{2,1,0:T(8,128)S(1)}, u32[]{:S(2)}, u32[]{:S(2)}) collective-permute-start(f32[1,8,128]{2,1,0:T(8,128)S(1)} %bitcast.15), channel_id=1, source_target_pairs={{4,0},{0,4},{5,1},{1,5},{6,2},{2,6},{7,3},{3,7},{12,8},{8,12},{13,... | collective-permute-start | bytes 12296 | tf_op jit(solution)/shard_map/ppermute | solution.py:266
  13.3 1.8 %copy-start = (s32[1,1,8,32]{3,2,1,0:T(8,128)S(1)}, s32[1,1,8,32]{3,2,1,0:T(8,128)}, u32[]{:S(2)}) copy-start(s32[1,1,8,32]{3,2,1,0:T(8,128)} %param.8) | copy-start | bytes 3076
  15.2 10.5 %copy-start.4 = (s32[1,1,2]{2,1,0:T(1,128)S(1)}, s32[1,1,2]{2,1,0:T(1,128)}, u32[]{:S(2)}) copy-start(s32[1,1,2]{2,1,0:T(1,128)} %param.10) | copy-start | bytes 28
  16.4 6.3 %collective-permute-start.1 = (f32[1,16,128]{2,1,0:T(8,128)S(1)}, f32[1,16,128]{2,1,0:T(8,128)S(1)}, u32[]{:S(2)}, u32[]{:S(2)}) collective-permute-start(f32[1,16,128]{2,1,0:T(8,128)S(1)} %bitcast.18), channel_id=1, source_target_pairs={{4,0},{0,4},{5,1},{1,5},{6,2},{2,6},{7,3},{3,7},{12,8},{8,12},{13,... | collective-permute-start | bytes 24584 | tf_op jit(solution)/shard_map/ppermute | solution.py:266
  18.2 11.4 %all-to-all-start.1 = ((f32[8,16,128]{2,1,0:T(8,128)}), f32[8,16,128]{2,1,0:T(8,128)S(1)}, u32[]{:S(2)}, u32[]{:S(2)}) async-start(f32[8,16,128]{2,1,0:T(8,128)} %get-tuple-element.16), calls=%async_computation.1 | async-start | bytes 131072 | tf_op jit(solution)/shard_map/all_to_all | solution.py:309
  23.5 3.7 %collective-permute-start.2 = (f32[1,16,128]{2,1,0:T(8,128)S(1)}, f32[1,16,128]{2,1,0:T(8,128)S(1)}, u32[]{:S(2)}, u32[]{:S(2)}) collective-permute-start(f32[1,16,128]{2,1,0:T(8,128)S(1)} %bitcast.19), channel_id=1, source_target_pairs={{4,0},{0,4},{5,1},{1,5},{6,2},{2,6},{7,3},{3,7},{12,8},{8,12},{13,... | collective-permute-start | bytes 24584 | tf_op jit(solution)/shard_map/ppermute | solution.py:266

commit v9 on v7

--- a/solution.py
+++ b/solution.py
@@ -193,7 +193,17 @@
         out_ref[device] = sums
 
 
-def last_kernel(cells, start_ref, image_ref, again_ref, sums_ref, second_ref, third_ref, entries_ref):
+def last_kernel(
+    cells, start_ref, image_ref, again_ref, sums_ref, second_ref, third_ref, entries_ref, hold_ref, line_ref, sems
+):
+    own_rows = start_ref.shape[0]
+    own = pl.ds(pl.multiple_of(lax.axis_index("blk") * own_rows, SUBL), own_rows)
+    vector, image = start_ref[...], image_ref[own, :]
+    copies = [
+        pltpu.make_async_copy(hold_ref.at[0], second_ref, sems.at[0]),
+        pltpu.make_async_copy(hold_ref.at[1], third_ref, sems.at[1]),
+        pltpu.make_async_copy(line_ref, entries_ref, sems.at[2]),
+    ]
     sums = jnp.sum(sums_ref[...], axis=0) / cells
 
     def whole(i):
@@ -208,6 +218,8 @@
     over_first = lax.rsqrt(first_square)
     h21 = first_square * over_first
     scale = lax.rsqrt(norm_square) * over_first
+    hold_ref[0] = (image - h11 * vector) * scale
+    copies[0].start()
     h12 = skew * inverse * over_first
     h22 = (wy - h11 * (ww + skew)) * scale * scale
     near = h11 + h22
@@ -217,16 +229,16 @@
     over_second = lax.rsqrt(second_square)
     h32 = second_square * over_second
 
-    own_rows = start_ref.shape[0]
-    own = pl.ds(pl.multiple_of(lax.axis_index("blk") * own_rows, SUBL), own_rows)
-    vector, image = start_ref[...], image_ref[own, :]
-    second_ref[...] = (image - h11 * vector) * scale
-    third_ref[...] = (again_ref[own, :] - near * image - far * vector) * (scale * over_second)
+    hold_ref[1] = (again_ref[own, :] - near * image - far * vector) * (scale * over_second)
+    copies[1].start()
     lane = lane_iota((1, LANES))
     entries = h32
     for i, value in enumerate((h11, h21, h12, h22)):
         entries = jnp.where(lane == i, value, entries)
-    entries_ref[...] = entries[:, 0:5]
+    line_ref[...] = entries[:, 0:5]
+    copies[2].start()
+    for copy in copies:
+        copy.wait()
 
 
 def per_device(start_vector, blocks, pattern, trace_map, neighbours, coupling):
@@ -245,6 +257,7 @@
         return jax.ShapeDtypeStruct((*shape, LANES), jnp.float32)
 
     smem = pl.BlockSpec(memory_space=pltpu.SMEM)
+    hbm = pl.BlockSpec(memory_space=pltpu.HBM)
 
     def from_others(value):
         got = [
@@ -320,7 +333,12 @@
         functools.partial(last_kernel, float(cells)),
         out_shape=(rowed(own_rows), rowed(own_rows), jax.ShapeDtypeStruct((1, 5), jnp.float32)),
         in_specs=[vmem] * 4,
-        out_specs=(vmem, vmem, vmem),
+        out_specs=(hbm, hbm, hbm),
+        scratch_shapes=[
+            pltpu.VMEM((2, own_rows, LANES), jnp.float32),
+            pltpu.VMEM((1, 5), jnp.float32),
+            pltpu.SemaphoreType.DMA((3,)),
+        ],
         compiler_params=params,
         name="arnoldi_entries",
     )(start, image, again, sums)

time: 34 us -> 34.1 us (level)
  no operation moved by 1% of the time
where the time goes in v9:
time: 34.1 us; the launch traced here: 33.8 us
  blocking collectives  21.5 us (63%)
  Pallas kernels  3.64 us (11%)
  starting transfers between devices  3.4 us (10%)
  local copies, waits for them, and re-layouts  2.36 us (7%)
  waiting for transfers between devices  2.22 us (7%)
  between operations  0.67 us (2%)
    all_to_all x1, blocking collectives, per_device(): group = lax.all_to_all(partial, ('sub', 'blk'), 0, 0, tiled=True)  12.4 us
    all_to_all x1, blocking collectives, per_device(): sums = lax.all_to_all(sums, ('rep', 'sub'), 0, 0, tiled=True)  9.03 us
    ppermute x2, starting transfers between devices, from_others(): lax.ppermute(value[None], 'blk', [((i + step) % parts, i) for i in range(...  3.4 us
    unnamed x12, local copies, waits for them, and re-layouts  2.36 us
    ppermute x2, waiting for transfers between devices, from_others(): lax.ppermute(value[None], 'blk', [((i + step) % parts, i) for i in range(...  2.22 us
    pallas_call x1, Pallas kernels, per_device(): pl.pallas_call(inflow_kernel, out_shape=(rowed(rows), rowed(SUBL)), in_sp...  1.13 us
    pallas_call x1, Pallas kernels, per_device(): pl.pallas_call(functools.partial(second_kernel, coupling.shape[0]), out_s...  0.78 us
    pallas_call x1, Pallas kernels, per_device(): pl.pallas_call(functools.partial(last_kernel, float(cells)), out_shape=(r...  0.75 us
  transfers between devices with their start and end apart: 2, of which 1 were waited for; matrix products, arithmetic and copies ran while one was open for 0% of the time, Pallas kernels for 4%

profile of v9, /device:TPU:0, one launch (start us, length us, event | category | flops | bytes accessed | tf_op | source)
XLA Modules:
  0.0 33.8 jit_solution(10174882198938321891)
XLA Ops:
  0.6 3.0 %collective-permute-start = (f32[1,8,128]{2,1,0:T(8,128)}, f32[1,8,128]{2,1,0:T(8,128)S(1)}, u32[]{:S(2)}, u32[]{:S(2)}) collective-permute-start(f32[1,8,128]{2,1,0:T(8,128)} %bitcast.13), channel_id=1, source_target_pairs={{4,0},{0,4},{5,1},{1,5},{6,2},{2,6},{7,3},{3,7},{12,8},{8,12},{13,... | collective-permute-start | bytes 12296 | tf_op jit(solution)/shard_map/ppermute | solution.py:264
  3.7 0.0 copy-start.2
  3.7 1.2 %copy-done.2 = bf16[1,1,4,32,4096]{4,3,2,1,0:T(8,128)(2,1)S(1)} copy-done((bf16[1,1,4,32,4096]{4,3,2,1,0:T(8,128)(2,1)S(1)}, bf16[1,1,4,32,4096]{4,3,2,1,0:T(8,128)(2,1)}, u32[]{:S(2)}) %copy-start.2) | copy-done | bytes 1048600
  4.9 0.0 copy-start.1
  4.9 0.0 copy-start.3
  4.9 0.0 copy-start.4
  4.9 0.0 copy-start.5
  4.9 0.1 wide_blocks.1.blocks_ref
  5.0 0.5 %copy-done.1 = f32[1,1,1024]{2,1,0:T(1,128)S(1)} copy-done((f32[1,1,1024]{2,1,0:T(1,128)S(1)}, f32[1,1,1024]{2,1,0:T(1,128)}, u32[]{:S(2)}) %copy-start.1) | copy-done | bytes 4120
  5.6 0.0 copy-done.3
  5.6 0.0 copy-done.4
  5.6 0.0 copy-done.5
  5.6 0.0 copy-start
  5.6 0.1 group_lines.1.lines_ref
  5.7 0.0 collective-permute-done.other_ref
  5.7 0.6 %copy-done = s32[1,1,8,32]{3,2,1,0:T(8,128)S(1)} copy-done((s32[1,1,8,32]{3,2,1,0:T(8,128)S(1)}, s32[1,1,8,32]{3,2,1,0:T(8,128)}, u32[]{:S(2)}) %copy-start) | copy-done | bytes 1048
  6.3 0.6 %first_image.1 = (f32[8,24,128]{2,1,0:T(8,128)S(1)}, f32[16,128]{1,0:T(8,128)S(1)}) custom-call(f32[8,128]{1,0:T(8,128)S(1)} %bitcast.15, f32[8,128]{1,0:T(8,128)S(1)} %group_lines.1.lines_ref, f32[1,8,128]{2,1,0:T(8,128)S(1)} %collective-permute-done.other_ref, f32[4,32,4096]{2,1,0:T(8,128)S(1)} %wide_blocks.1.blocks_ref, s32[8,32]{1,0:T(8,128)S(1)} %bitcast.11), custom_call_target="tpu_custom_call" | custom-call | tf_op jit(solution)/shard_map/first_image/pallas_call | solution.py:293
  6.9 12.4 %all_to_all.10.group_ref = f32[8,24,128]{2,1,0:T(8,128)S(1)} all-to-all(f32[8,24,128]{2,1,0:T(8,128)S(1)} %get-tuple-element.14), channel_id=1, replica_groups=mesh['sub'=4,'blk'=2,'rep'=4] {'sub','blk'}, dimensions={0} | all-to-all | bytes 196608 | tf_op jit(solution)/shard_map/all_to_all | solution.py:302
  19.4 0.8 %second_image.1 = (f32[16,128]{1,0:T(8,128)S(1)}, f32[16,128]{1,0:T(8,128)S(1)}) custom-call(f32[8,24,128]{2,1,0:T(8,128)S(1)} %all_to_all.10.group_ref, f32[4,32,4096]{2,1,0:T(8,128)S(1)} %wide_blocks.1.blocks_ref, s32[8,32]{1,0:T(8,128)S(1)} %bitcast.12), custom_call_target="tpu_custom_call" | custom-call | tf_op jit(solution)/shard_map/second_image/pallas_call | solution.py:303
  20.1 0.4 %collective-permute-start.1 = (f32[1,16,128]{2,1,0:T(8,128)S(1)}, f32[1,16,128]{2,1,0:T(8,128)S(1)}, u32[]{:S(2)}, u32[]{:S(2)}) collective-permute-start(f32[1,16,128]{2,1,0:T(8,128)S(1)} %bitcast.17), channel_id=1, source_target_pairs={{4,0},{0,4},{5,1},{1,5},{6,2},{2,6},{7,3},{3,7},{12,8},{8,12},{13,... | collective-permute-start | bytes 24584 | tf_op jit(solution)/shard_map/ppermute | solution.py:264
  20.5 1.1 %second_inflow.1 = (f32[16,128]{1,0:T(8,128)S(1)}, f32[8,128]{1,0:T(8,128)S(1)}) custom-call(f32[16,128]{1,0:T(8,128)S(1)} %get-tuple-element.16.vector_ref, f32[16,128]{1,0:T(8,128)S(1)} %get-tuple-element.15.image_ref, f32[8,24,128]{2,1,0:T(8,128)S(1)} %all_to_all.10.group_ref, s32[1,2]{1,0:T(1,128)S(1)} %bitcast.22), custom_call_target="tpu_custom_call" | custom-call | flops 4294967296 | bytes 1048576 | tf_op jit(solution)/shard_map/second_inflow/pallas_call | solution.py:313
  21.6 2.2 %collective-permute-done.1.other_ref = f32[1,16,128]{2,1,0:T(8,128)S(1)} collective-permute-done((f32[1,16,128]{2,1,0:T(8,128)S(1)}, f32[1,16,128]{2,1,0:T(8,128)S(1)}, u32[]{:S(2)}, u32[]{:S(2)}) %collective-permute-start.1) | collective-permute-done | bytes 8224 | tf_op jit(solution)/shard_map/ppermute | solution.py:264
  23.9 0.1 pair_sums.1
  24.0 9.0 %all_to_all.11.sums_ref = f32[16,1,128]{2,1,0:T(1,128)S(1)} all-to-all(f32[16,1,128]{2,1,0:T(1,128)S(1)} %get-tuple-element.21), channel_id=1, replica_groups=mesh['sub'=4,'blk'=2,'rep'=4] {'rep','sub'}, dimensions={0} | all-to-all | bytes 16384 | tf_op jit(solution)/shard_map/all_to_all | solution.py:331
  33.0 0.8 %arnoldi_entries.1 = (f32[8,128]{1,0:T(8,128)}, f32[8,128]{1,0:T(8,128)}, f32[1,5]{1,0:T(1,128)}) custom-call(f32[8,128]{1,0:T(8,128)S(1)} %bitcast.16, f32[16,128]{1,0:T(8,128)S(1)} %get-tuple-element.15.image_ref, f32[16,128]{1,0:T(8,128)S(1)} %get-tuple-element.20.again_ref, f32[16,1,128]{2,1,0:T(1,128)S(1)} %all_to_all.11.sums_ref), custom_call_target="tpu_custom_call" | custom-call | tf_op jit(solution)/shard_map/arnoldi_entries/pallas_call | solution.py:332
Async XLA Ops:
  0.6 5.1 %collective-permute-start = (f32[1,8,128]{2,1,0:T(8,128)}, f32[1,8,128]{2,1,0:T(8,128)S(1)}, u32[]{:S(2)}, u32[]{:S(2)}) collective-permute-start(f32[1,8,128]{2,1,0:T(8,128)} %bitcast.13), channel_id=1, source_target_pairs={{4,0},{0,4},{5,1},{1,5},{6,2},{2,6},{7,3},{3,7},{12,8},{8,12},{13,... | collective-permute-start | bytes 12296 | tf_op jit(solution)/shard_map/ppermute | solution.py:264
  3.7 1.2 %copy-start.2 = (bf16[1,1,4,32,4096]{4,3,2,1,0:T(8,128)(2,1)S(1)}, bf16[1,1,4,32,4096]{4,3,2,1,0:T(8,128)(2,1)}, u32[]{:S(2)}) copy-start(bf16[1,1,4,32,4096]{4,3,2,1,0:T(8,128)(2,1)} %param.7) | copy-start | bytes 3145732
  4.9 0.7 %copy-start.1 = (f32[1,1,1024]{2,1,0:T(1,128)S(1)}, f32[1,1,1024]{2,1,0:T(1,128)}, u32[]{:S(2)}) copy-start(f32[1,1,1024]{2,1,0:T(1,128)} %param.6) | copy-start | bytes 12292
  4.9 0.7 %copy-start.3 = (f32[1,1,2,128]{3,2,1,0:T(2,128)S(1)}, f32[1,1,2,128]{3,2,1,0:T(2,128)}, u32[]{:S(2)}) copy-start(f32[1,1,2,128]{3,2,1,0:T(2,128)} %param.11) | copy-start | bytes 3076
  4.9 0.7 %copy-start.4 = (s32[1,1,128]{2,1,0:T(1,128)S(1)}, s32[1,1,128]{2,1,0:T(1,128)}, u32[]{:S(2)}) copy-start(s32[1,1,128]{2,1,0:T(1,128)} %param.9) | copy-start | bytes 1540
  4.9 0.7 %copy-start.5 = (s32[1,1,2]{2,1,0:T(1,128)S(1)}, s32[1,1,2]{2,1,0:T(1,128)}, u32[]{:S(2)}) copy-start(s32[1,1,2]{2,1,0:T(1,128)} %param.10) | copy-start | bytes 28
  5.6 0.7 %copy-start = (s32[1,1,8,32]{3,2,1,0:T(8,128)S(1)}, s32[1,1,8,32]{3,2,1,0:T(8,128)}, u32[]{:S(2)}) copy-start(s32[1,1,8,32]{3,2,1,0:T(8,128)} %param.8) | copy-start | bytes 3076
  20.1 3.7 %collective-permute-start.1 = (f32[1,16,128]{2,1,0:T(8,128)S(1)}, f32[1,16,128]{2,1,0:T(8,128)S(1)}, u32[]{:S(2)}, u32[]{:S(2)}) collective-permute-start(f32[1,16,128]{2,1,0:T(8,128)S(1)} %bitcast.17), channel_id=1, source_target_pairs={{4,0},{0,4},{5,1},{1,5},{6,2},{2,6},{7,3},{3,7},{12,8},{8,12},{13,... | collective-permute-start | bytes 24584 | tf_op jit(solution)/shard_map/ppermute | solution.py:264

commit v10 on v7

--- a/solution.py
+++ b/solution.py
@@ -29,40 +29,57 @@
     return lax.broadcasted_iota(jnp.int32, shape, 0)
 
 
-def block_product(vector, blocks_ref, pattern_ref, first_slot, fold_ref, halves_ref):
+def choices(pattern_ref, first_slot, slots):
+    block_rows = pattern_ref.shape[1]
+    half = block_rows // 2
+    place = row_iota((block_rows, block_rows))
+    place = jnp.where(place < half, 2 * place, 2 * (place - half) + 1)
+    thrice = (block_rows, 3 * block_rows)
+    copies = (lane_iota(thrice) % block_rows == row_iota(thrice)).astype(jnp.float32).astype(jnp.bfloat16)
+    rows = []
+    for k in range(slots):
+        chosen = place == pattern_ref[pl.ds(first_slot + k, 1), :]
+        chosen = chosen.astype(jnp.float32).astype(jnp.bfloat16)
+        rows.append(
+            lax.dot_general(chosen, copies, (((0,), (0,)), ((), ())), preferred_element_type=jnp.float32)
+        )
+    return jnp.concatenate(rows, 0).astype(jnp.bfloat16)
+
+
+def block_product(vector, blocks_ref, choices_ref, fold_ref, halves_ref):
     slots, block_rows, width = blocks_ref.shape
     half = block_rows // 2
     lower = lane_iota(vector.shape) < BS
     turned = pltpu.roll(vector, BS, 1)
     table = jnp.concatenate([jnp.where(lower, vector, turned), jnp.where(lower, turned, vector)], 0)
     table = jnp.concatenate(pieces(table), 0)
-    place = row_iota((block_rows, block_rows))
-    place = jnp.where(place < half, 2 * place, 2 * (place - half) + 1)
-    picked = []
-    for k in range(slots):
-        names = pattern_ref[pl.ds(first_slot + k, 1), :]
-        chosen = (place == names).astype(jnp.float32).astype(jnp.bfloat16)
-        chosen = jnp.concatenate([chosen] * 3, 0)
-        picked.append(
-            lax.dot_general(chosen, table, (((0,), (0,)), ((), ())), preferred_element_type=jnp.float32)
-        )
+    picked = lax.dot_general(
+        choices_ref[...], table, (((1,), (0,)), ((), ())), preferred_element_type=jnp.float32
+    )
     ones = (row_iota((2 * LANES, LANES)) % LANES) // BS == lane_iota((2 * LANES, LANES)) % 2
     ones = ones.astype(jnp.float32).astype(jnp.bfloat16)
     pair = (lane_iota((block_rows, LANES)) % BS) // 2
     chunks = width // LANES
-    for c in range(chunks):
-        total = None
-        for k in range(slots):
-            term = blocks_ref[k, :, pl.ds(c * LANES, LANES)] * picked[k]
-            total = term if total is None else total + term
-        high = total.astype(jnp.bfloat16)
-        here = pl.ds(c * block_rows, block_rows)
-        halves_ref[here, 0:LANES] = high
-        halves_ref[here, LANES : 2 * LANES] = (total - high.astype(jnp.float32)).astype(jnp.bfloat16)
-    sums = lax.dot_general(halves_ref[...], ones, (((1,), (0,)), ((), ())), preferred_element_type=jnp.float32)
-    result = sums[0:block_rows]
-    for c in range(1, chunks):
-        result = jnp.where(pair == c, sums[c * block_rows : (c + 1) * block_rows], result)
+    together = chunks // 4
+    result = jnp.zeros((block_rows, LANES), jnp.float32)
+    for first in range(0, chunks, together):
+        for c in range(first, first + together):
+            total = None
+            for k in range(slots):
+                term = blocks_ref[k, :, pl.ds(c * LANES, LANES)] * picked[k * block_rows : (k + 1) * block_rows]
+                total = term if total is None else total + term
+            high = total.astype(jnp.bfloat16)
+            here = pl.ds(c * block_rows, block_rows)
+            halves_ref[here, 0:LANES] = high
+            halves_ref[here, LANES : 2 * LANES] = (total - high.astype(jnp.float32)).astype(jnp.bfloat16)
+        sums = lax.dot_general(
+            halves_ref[pl.ds(first * block_rows, together * block_rows), :],
+            ones,
+            (((1,), (0,)), ((), ())),
+            preferred_element_type=jnp.float32,
+        )
+        for i in range(together):
+            result = jnp.where(pair == first + i, sums[i * block_rows : (i + 1) * block_rows], result)
     fold_ref[...] = result
     even = fold_ref[pl.ds(0, half, stride=2), :]
     odd = fold_ref[pl.ds(1, half, stride=2), :]
@@ -87,7 +104,7 @@
     return landed[0:count] + landed[count : 2 * count] + landed[2 * count : 3 * count]
 
 
-def lines_kernel(start_ref, map_ref, near_ref, coupling_ref, out_ref):
+def lines_kernel(start_ref, map_ref, near_ref, coupling_ref, pattern_ref, out_ref, choices_ref):
     places = map_ref[...]
     count = coupling_ref.shape[0]
     first_cell = lax.axis_index("blk") * start_ref.shape[0] * LANES
@@ -97,20 +114,22 @@
     lines += [jnp.broadcast_to(near[:, n : n + 1], (1, LANES)) for n in range(count)]
     lines += [jnp.zeros((SUBL - len(lines), LANES), jnp.float32)]
     out_ref[...] = jnp.concatenate(lines, 0)
+    slots = choices_ref.shape[0] // pattern_ref.shape[1]
+    choices_ref[...] = choices(pattern_ref, lax.axis_index("blk") * slots, slots)
 
 
 def widen_kernel(blocks_ref, out_ref):
     out_ref[...] = blocks_ref[...].astype(jnp.float32)
 
 
-def first_kernel(start_ref, lines_ref, other_ref, blocks_ref, pattern_ref, out_ref, vector_ref, fold_ref, halves_ref):
+def first_kernel(start_ref, lines_ref, other_ref, blocks_ref, choices_ref, out_ref, vector_ref, fold_ref, halves_ref):
     own_rows, rows = start_ref.shape[0], vector_ref.shape[0]
     blk, parts = lax.axis_index("blk"), lax.axis_size("blk")
     for step in range(parts):
         place = lax.rem(blk + step, parts)
         place = pl.ds(pl.multiple_of(place * own_rows, SUBL), own_rows)
         vector_ref[place, :] = other_ref[step - 1] if step else start_ref[...]
-    partial = block_product(vector_ref[...], blocks_ref, pattern_ref, blk * blocks_ref.shape[0], fold_ref, halves_ref)
+    partial = block_product(vector_ref[...], blocks_ref, choices_ref, fold_ref, halves_ref)
     for device in range(out_ref.shape[0]):
         out_ref[device, 0:rows, :] = partial
         out_ref[device, rows : rows + SUBL, :] = lines_ref[...]
@@ -143,13 +162,13 @@
     return total
 
 
-def second_kernel(count, group_ref, blocks_ref, pattern_ref, out_ref, image_ref, fold_ref, halves_ref):
+def second_kernel(count, group_ref, blocks_ref, choices_ref, out_ref, image_ref, fold_ref, halves_ref):
     rows = image_ref.shape[0]
-    sub, blk, parts = lax.axis_index("sub"), lax.axis_index("blk"), lax.axis_size("blk")
+    sub, parts = lax.axis_index("sub"), lax.axis_size("blk")
     added = [landed(group_ref, sub, part, rows // parts, count)[0] for part in range(parts)]
     image = summed(group_ref, sub, 0, rows) + jnp.concatenate(added, 0)
     image_ref[...] = image
-    out_ref[...] = block_product(image, blocks_ref, pattern_ref, blk * blocks_ref.shape[0], fold_ref, halves_ref)
+    out_ref[...] = block_product(image, blocks_ref, choices_ref, fold_ref, halves_ref)
 
 
 def down(left, right):
@@ -254,20 +273,20 @@
         return got[0] if parts == 2 else jnp.concatenate(got, 0)
 
     others = from_others(start)
-    block_rows, width = blocks.shape[1:]
+    slots, block_rows, width = blocks.shape
     scratch = [
         pltpu.VMEM((block_rows, LANES), jnp.float32),
         pltpu.VMEM((block_rows * width // LANES, 2 * LANES), jnp.bfloat16),
     ]
-    lines = pl.pallas_call(
+    lines, chosen = pl.pallas_call(
         lines_kernel,
-        out_shape=rowed(SUBL),
-        in_specs=[vmem] * 4,
-        out_specs=vmem,
+        out_shape=(rowed(SUBL), jax.ShapeDtypeStruct((slots * block_rows, 3 * block_rows), jnp.bfloat16)),
+        in_specs=[vmem] * 5,
+        out_specs=(vmem, vmem),
         compiler_params=params,
         cost_estimate=pl.CostEstimate(flops=1 << 32, bytes_accessed=1 << 20, transcendentals=0),
         name="group_lines",
-    )(start, local_map, neighbours, coupling)
+    )(start, local_map, neighbours, coupling, pattern)
     wide = pl.pallas_call(
         widen_kernel,
         out_shape=jax.ShapeDtypeStruct(blocks.shape, jnp.float32),
@@ -285,7 +304,7 @@
         scratch_shapes=scratch,
         compiler_params=params,
         name="first_image",
-    )(start, lines, others, wide, pattern)
+    )(start, lines, others, wide, chosen)
     group = lax.all_to_all(partial, ("sub", "blk"), 0, 0, tiled=True)
     second, image = pl.pallas_call(
         functools.partial(second_kernel, coupling.shape[0]),
@@ -295,7 +314,7 @@
         scratch_shapes=scratch,
         compiler_params=params,
         name="second_image",
-    )(group, wide, pattern)
+    )(group, wide, chosen)
     others = from_others(second)
     inflow, sums = pl.pallas_call(
         inflow_kernel,

time: 34 us -> 34 us (level)
  local copies, waits for them, and re-layouts: 2.36 us -> 1.78 us
  blocking collectives: 21.5 us -> 21.9 us
    unnamed x12, local copies, waits for them, and re-layouts: 2.36 us -> 1.78 us
    all_to_all x1, blocking collectives: 12.4 us -> 12.9 us  [per_device(): group = lax.all_to_all(partial, ('sub', 'blk'), 0, 0, tiled=True)]
where the time goes in v10:
time: 34 us; the launch traced here: 33.7 us
  blocking collectives  21.9 us (64%)
  Pallas kernels  3.73 us (11%)
  starting transfers between devices  3.4 us (10%)
  waiting for transfers between devices  2.22 us (7%)
  local copies, waits for them, and re-layouts  1.78 us (5%)
  between operations  0.68 us (2%)
    all_to_all x1, blocking collectives, per_device(): group = lax.all_to_all(partial, ('sub', 'blk'), 0, 0, tiled=True)  12.9 us
    all_to_all x1, blocking collectives, per_device(): sums = lax.all_to_all(sums, ('rep', 'sub'), 0, 0, tiled=True)  9.03 us
    ppermute x2, starting transfers between devices, from_others(): lax.ppermute(value[None], 'blk', [((i + step) % parts, i) for i in range(...  3.4 us
    ppermute x2, waiting for transfers between devices, from_others(): lax.ppermute(value[None], 'blk', [((i + step) % parts, i) for i in range(...  2.22 us
    unnamed x12, local copies, waits for them, and re-layouts  1.78 us
    pallas_call x1, Pallas kernels, per_device(): pl.pallas_call(inflow_kernel, out_shape=(rowed(rows), rowed(SUBL)), in_sp...  1.13 us
    pallas_call x1, Pallas kernels, per_device(): pl.pallas_call(functools.partial(second_kernel, coupling.shape[0]), out_s...  0.79 us
    pallas_call x1, Pallas kernels, per_device(): pl.pallas_call(functools.partial(last_kernel, float(cells)), out_shape=(r...  0.72 us
  transfers between devices with their start and end apart: 2, of which 1 were waited for; matrix products, arithmetic and copies ran while one was open for 0% of the time, Pallas kernels for 4%

profile of v10, /device:TPU:0, one launch (start us, length us, event | category | flops | bytes accessed | tf_op | source)
XLA Modules:
  0.0 33.7 jit_solution(15180150996609228141)
XLA Ops:
  0.6 3.0 %collective-permute-start = (f32[1,8,128]{2,1,0:T(8,128)}, f32[1,8,128]{2,1,0:T(8,128)S(1)}, u32[]{:S(2)}, u32[]{:S(2)}) collective-permute-start(f32[1,8,128]{2,1,0:T(8,128)} %bitcast.11), channel_id=1, source_target_pairs={{4,0},{0,4},{5,1},{1,5},{6,2},{2,6},{7,3},{3,7},{12,8},{8,12},{13,... | collective-permute-start | bytes 12296 | tf_op jit(solution)/shard_map/ppermute | solution.py:270
  3.7 0.0 copy-start.1
  3.7 1.2 %copy-done.1 = bf16[1,1,4,32,4096]{4,3,2,1,0:T(8,128)(2,1)S(1)} copy-done((bf16[1,1,4,32,4096]{4,3,2,1,0:T(8,128)(2,1)S(1)}, bf16[1,1,4,32,4096]{4,3,2,1,0:T(8,128)(2,1)}, u32[]{:S(2)}) %copy-start.1) | copy-done | bytes 1048600
  4.9 0.0 copy-start
  4.9 0.0 copy-start.2
  4.9 0.0 copy-start.3
  4.9 0.0 copy-start.4
  4.9 0.0 copy-start.5
  4.9 0.1 wide_blocks.1.blocks_ref
  5.1 0.5 %copy-done = f32[1,1,1024]{2,1,0:T(1,128)S(1)} copy-done((f32[1,1,1024]{2,1,0:T(1,128)S(1)}, f32[1,1,1024]{2,1,0:T(1,128)}, u32[]{:S(2)}) %copy-start) | copy-done | bytes 4120
  5.6 0.0 copy-done.2
  5.6 0.0 copy-done.3
  5.6 0.0 copy-done.4
  5.6 0.0 copy-done.5
  5.6 0.2 group_lines.1
  5.8 0.0 collective-permute-done.other_ref
  5.8 0.6 %first_image.1 = (f32[8,24,128]{2,1,0:T(8,128)S(1)}, f32[16,128]{1,0:T(8,128)S(1)}) custom-call(f32[8,128]{1,0:T(8,128)S(1)} %bitcast.13, f32[8,128]{1,0:T(8,128)S(1)} %get-tuple-element.16.lines_ref, f32[1,8,128]{2,1,0:T(8,128)S(1)} %collective-permute-done.other_ref, f32[4,32,4096]{2,1,0:T(8,128)S(1)} %wide_blocks.1.blocks_ref, ...), custom_call_target="tpu_custom_call" | custom-call | tf_op jit(solution)/shard_map/first_image/pallas_call | solution.py:299
  6.5 12.9 %all_to_all.10.group_ref = f32[8,24,128]{2,1,0:T(8,128)S(1)} all-to-all(f32[8,24,128]{2,1,0:T(8,128)S(1)} %get-tuple-element.18), channel_id=1, replica_groups=mesh['sub'=4,'blk'=2,'rep'=4] {'sub','blk'}, dimensions={0} | all-to-all | bytes 196608 | tf_op jit(solution)/shard_map/all_to_all | solution.py:308
  19.4 0.8 %second_image.1 = (f32[16,128]{1,0:T(8,128)S(1)}, f32[16,128]{1,0:T(8,128)S(1)}) custom-call(f32[8,24,128]{2,1,0:T(8,128)S(1)} %all_to_all.10.group_ref, f32[4,32,4096]{2,1,0:T(8,128)S(1)} %wide_blocks.1.blocks_ref, bf16[128,96]{1,0:T(8,128)(2,1)S(1)} %get-tuple-element.17.choices_ref), custom_call_target="tpu_custom_call" | custom-call | tf_op jit(solution)/shard_map/second_image/pallas_call | solution.py:309
  20.2 0.4 %collective-permute-start.1 = (f32[1,16,128]{2,1,0:T(8,128)S(1)}, f32[1,16,128]{2,1,0:T(8,128)S(1)}, u32[]{:S(2)}, u32[]{:S(2)}) collective-permute-start(f32[1,16,128]{2,1,0:T(8,128)S(1)} %bitcast.15), channel_id=1, source_target_pairs={{4,0},{0,4},{5,1},{1,5},{6,2},{2,6},{7,3},{3,7},{12,8},{8,12},{13,... | collective-permute-start | bytes 24584 | tf_op jit(solution)/shard_map/ppermute | solution.py:270
  20.5 1.1 %second_inflow.1 = (f32[16,128]{1,0:T(8,128)S(1)}, f32[8,128]{1,0:T(8,128)S(1)}) custom-call(f32[16,128]{1,0:T(8,128)S(1)} %get-tuple-element.20.vector_ref, f32[16,128]{1,0:T(8,128)S(1)} %get-tuple-element.19.image_ref, f32[8,24,128]{2,1,0:T(8,128)S(1)} %all_to_all.10.group_ref, s32[1,2]{1,0:T(1,128)S(1)} %bitcast.21), custom_call_target="tpu_custom_call" | custom-call | flops 4294967296 | bytes 1048576 | tf_op jit(solution)/shard_map/second_inflow/pallas_call | solution.py:319
  21.7 2.2 %collective-permute-done.1.other_ref = f32[1,16,128]{2,1,0:T(8,128)S(1)} collective-permute-done((f32[1,16,128]{2,1,0:T(8,128)S(1)}, f32[1,16,128]{2,1,0:T(8,128)S(1)}, u32[]{:S(2)}, u32[]{:S(2)}) %collective-permute-start.1) | collective-permute-done | bytes 8224 | tf_op jit(solution)/shard_map/ppermute | solution.py:270
  23.9 0.1 pair_sums.1
  24.0 9.0 %all_to_all.11.sums_ref = f32[16,1,128]{2,1,0:T(1,128)S(1)} all-to-all(f32[16,1,128]{2,1,0:T(1,128)S(1)} %get-tuple-element.25), channel_id=1, replica_groups=mesh['sub'=4,'blk'=2,'rep'=4] {'rep','sub'}, dimensions={0} | all-to-all | bytes 16384 | tf_op jit(solution)/shard_map/all_to_all | solution.py:337
  33.0 0.7 %arnoldi_entries.1 = (f32[8,128]{1,0:T(8,128)}, f32[8,128]{1,0:T(8,128)}, f32[1,5]{1,0:T(1,128)}) custom-call(f32[8,128]{1,0:T(8,128)S(1)} %bitcast.14, f32[16,128]{1,0:T(8,128)S(1)} %get-tuple-element.19.image_ref, f32[16,128]{1,0:T(8,128)S(1)} %get-tuple-element.24.again_ref, f32[16,1,128]{2,1,0:T(1,128)S(1)} %all_to_all.11.sums_ref), custom_call_target="tpu_custom_call" | custom-call | tf_op jit(solution)/shard_map/arnoldi_entries/pallas_call | solution.py:338
Async XLA Ops:
  0.6 5.2 %collective-permute-start = (f32[1,8,128]{2,1,0:T(8,128)}, f32[1,8,128]{2,1,0:T(8,128)S(1)}, u32[]{:S(2)}, u32[]{:S(2)}) collective-permute-start(f32[1,8,128]{2,1,0:T(8,128)} %bitcast.11), channel_id=1, source_target_pairs={{4,0},{0,4},{5,1},{1,5},{6,2},{2,6},{7,3},{3,7},{12,8},{8,12},{13,... | collective-permute-start | bytes 12296 | tf_op jit(solution)/shard_map/ppermute | solution.py:270
  3.7 1.2 %copy-start.1 = (bf16[1,1,4,32,4096]{4,3,2,1,0:T(8,128)(2,1)S(1)}, bf16[1,1,4,32,4096]{4,3,2,1,0:T(8,128)(2,1)}, u32[]{:S(2)}) copy-start(bf16[1,1,4,32,4096]{4,3,2,1,0:T(8,128)(2,1)} %param.7) | copy-start | bytes 3145732
  4.9 0.7 %copy-start = (f32[1,1,1024]{2,1,0:T(1,128)S(1)}, f32[1,1,1024]{2,1,0:T(1,128)}, u32[]{:S(2)}) copy-start(f32[1,1,1024]{2,1,0:T(1,128)} %param.6) | copy-start | bytes 12292
  4.9 0.7 %copy-start.2 = (s32[1,1,8,32]{3,2,1,0:T(8,128)S(1)}, s32[1,1,8,32]{3,2,1,0:T(8,128)}, u32[]{:S(2)}) copy-start(s32[1,1,8,32]{3,2,1,0:T(8,128)} %param.8) | copy-start | bytes 3076
  4.9 0.7 %copy-start.3 = (f32[1,1,2,128]{3,2,1,0:T(2,128)S(1)}, f32[1,1,2,128]{3,2,1,0:T(2,128)}, u32[]{:S(2)}) copy-start(f32[1,1,2,128]{3,2,1,0:T(2,128)} %param.11) | copy-start | bytes 3076
  4.9 0.7 %copy-start.4 = (s32[1,1,128]{2,1,0:T(1,128)S(1)}, s32[1,1,128]{2,1,0:T(1,128)}, u32[]{:S(2)}) copy-start(s32[1,1,128]{2,1,0:T(1,128)} %param.9) | copy-start | bytes 1540
  4.9 0.7 %copy-start.5 = (s32[1,1,2]{2,1,0:T(1,128)S(1)}, s32[1,1,2]{2,1,0:T(1,128)}, u32[]{:S(2)}) copy-start(s32[1,1,2]{2,1,0:T(1,128)} %param.10) | copy-start | bytes 28
  20.2 3.7 %collective-permute-start.1 = (f32[1,16,128]{2,1,0:T(8,128)S(1)}, f32[1,16,128]{2,1,0:T(8,128)S(1)}, u32[]{:S(2)}, u32[]{:S(2)}) collective-permute-start(f32[1,16,128]{2,1,0:T(8,128)S(1)} %bitcast.15), channel_id=1, source_target_pairs={{4,0},{0,4},{5,1},{1,5},{6,2},{2,6},{7,3},{3,7},{12,8},{8,12},{13,... | collective-permute-start | bytes 24584 | tf_op jit(solution)/shard_map/ppermute | solution.py:270

commit v11 on v10

--- a/solution.py
+++ b/solution.py
@@ -135,17 +135,20 @@
         out_ref[device, rows : rows + SUBL, :] = lines_ref[...]
 
 
+def member(sub_at, part):
+    return part * lax.axis_size("sub") + sub_at
+
+
 def line(group_ref, device, i):
     first = group_ref.shape[1] - SUBL + i
     return group_ref[device, first : first + 1, :]
 
 
 def landed(group_ref, sub_at, part, own_rows, count):
-    parts = lax.axis_size("blk")
-    traces = [line(group_ref, other * parts + part, 0) for other in range(lax.axis_size("sub"))]
+    traces = [line(group_ref, member(other, part), 0) for other in range(lax.axis_size("sub"))]
     traces = jnp.concatenate(traces, 0)
     names = row_iota(traces.shape).astype(jnp.float32)
-    device = sub_at * parts + part
+    device = member(sub_at, part)
     inflow = jnp.zeros((1, LANES), jnp.float32)
     for n in range(count):
         chosen = jnp.where(names == line(group_ref, device, 2 + count + n), traces, 0.0)
@@ -156,9 +159,9 @@
 
 def summed(group_ref, sub_at, first, count):
     parts = lax.axis_size("blk")
-    total = group_ref[sub_at * parts, first : first + count, :]
+    total = group_ref[member(sub_at, 0), first : first + count, :]
     for b in range(1, parts):
-        total = total + group_ref[sub_at * parts + b, first : first + count, :]
+        total = total + group_ref[member(sub_at, b), first : first + count, :]
     return total
 
 
@@ -181,7 +184,7 @@
     sub, parts = lax.axis_index("sub"), lax.axis_size("blk")
     own_rows = rows // parts
     for part in range(parts):
-        device = sub * parts + part
+        device = member(sub, part)
         inflow = jnp.zeros((1, LANES), jnp.float32)
         for n in range(count):
             source = near_ref[0, n]
@@ -305,7 +308,7 @@
         compiler_params=params,
         name="first_image",
     )(start, lines, others, wide, chosen)
-    group = lax.all_to_all(partial, ("sub", "blk"), 0, 0, tiled=True)
+    group = lax.all_to_all(partial, ("blk", "sub"), 0, 0, tiled=True)
     second, image = pl.pallas_call(
         functools.partial(second_kernel, coupling.shape[0]),
         out_shape=(rowed(rows), rowed(rows)),
@@ -334,7 +337,7 @@
         compiler_params=params,
         name="pair_sums",
     )(vector, image, sums, inflow, second, others)
-    sums = lax.all_to_all(sums, ("rep", "sub"), 0, 0, tiled=True)
+    sums = lax.all_to_all(sums, ("sub", "rep"), 0, 0, tiled=True)
     second, third, entries = pl.pallas_call(
         functools.partial(last_kernel, float(cells)),
         out_shape=(rowed(own_rows), rowed(own_rows), jax.ShapeDtypeStruct((1, 5), jnp.float32)),

time: 34 us -> 34.2 us (level)
  no operation moved by 1% of the time
where the time goes in v11:
time: 34.2 us; the launch traced here: 33.9 us
  blocking collectives  22.1 us (65%)
  Pallas kernels  3.73 us (11%)
  starting transfers between devices  3.66 us (11%)
  waiting for transfers between devices  1.96 us (6%)
  local copies, waits for them, and re-layouts  1.78 us (5%)
  between operations  0.68 us (2%)
    all_to_all x1, blocking collectives, per_device(): group = lax.all_to_all(partial, ('blk', 'sub'), 0, 0, tiled=True)  13 us
    all_to_all x1, blocking collectives, per_device(): sums = lax.all_to_all(sums, ('sub', 'rep'), 0, 0, tiled=True)  9.07 us
    ppermute x2, starting transfers between devices, from_others(): lax.ppermute(value[None], 'blk', [((i + step) % parts, i) for i in range(...  3.66 us
    ppermute x2, waiting for transfers between devices, from_others(): lax.ppermute(value[None], 'blk', [((i + step) % parts, i) for i in range(...  1.96 us
    unnamed x12, local copies, waits for them, and re-layouts  1.78 us
    pallas_call x1, Pallas kernels, per_device(): pl.pallas_call(inflow_kernel, out_shape=(rowed(rows), rowed(SUBL)), in_sp...  1.13 us
    pallas_call x1, Pallas kernels, per_device(): pl.pallas_call(functools.partial(second_kernel, coupling.shape[0]), out_s...  0.79 us
    pallas_call x1, Pallas kernels, per_device(): pl.pallas_call(functools.partial(last_kernel, float(cells)), out_shape=(r...  0.72 us
  transfers between devices with their start and end apart: 2, of which 1 were waited for; matrix products, arithmetic and copies ran while one was open for 0% of the time, Pallas kernels for 4%

profile of v11, /device:TPU:0, one launch (start us, length us, event | category | flops | bytes accessed | tf_op | source)
XLA Modules:
  0.0 33.9 jit_solution(10196655104503276552)
XLA Ops:
  0.6 3.0 %collective-permute-start = (f32[1,8,128]{2,1,0:T(8,128)}, f32[1,8,128]{2,1,0:T(8,128)S(1)}, u32[]{:S(2)}, u32[]{:S(2)}) collective-permute-start(f32[1,8,128]{2,1,0:T(8,128)} %bitcast.11), channel_id=1, source_target_pairs={{4,0},{0,4},{5,1},{1,5},{6,2},{2,6},{7,3},{3,7},{12,8},{8,12},{13,... | collective-permute-start | bytes 12296 | tf_op jit(solution)/shard_map/ppermute | solution.py:273
  3.7 0.0 copy-start.1
  3.7 1.2 %copy-done.1 = bf16[1,1,4,32,4096]{4,3,2,1,0:T(8,128)(2,1)S(1)} copy-done((bf16[1,1,4,32,4096]{4,3,2,1,0:T(8,128)(2,1)S(1)}, bf16[1,1,4,32,4096]{4,3,2,1,0:T(8,128)(2,1)}, u32[]{:S(2)}) %copy-start.1) | copy-done | bytes 1048600
  4.9 0.0 copy-start
  4.9 0.0 copy-start.2
  4.9 0.0 copy-start.3
  4.9 0.0 copy-start.4
  4.9 0.0 copy-start.5
  4.9 0.1 wide_blocks.1.blocks_ref
  5.1 0.5 %copy-done = f32[1,1,1024]{2,1,0:T(1,128)S(1)} copy-done((f32[1,1,1024]{2,1,0:T(1,128)S(1)}, f32[1,1,1024]{2,1,0:T(1,128)}, u32[]{:S(2)}) %copy-start) | copy-done | bytes 4120
  5.6 0.0 copy-done.2
  5.6 0.0 copy-done.3
  5.6 0.0 copy-done.4
  5.6 0.0 copy-done.5
  5.6 0.2 group_lines.1
  5.8 0.0 collective-permute-done.other_ref
  5.8 0.6 %first_image.1 = (f32[8,24,128]{2,1,0:T(8,128)S(1)}, f32[16,128]{1,0:T(8,128)S(1)}) custom-call(f32[8,128]{1,0:T(8,128)S(1)} %bitcast.13, f32[8,128]{1,0:T(8,128)S(1)} %get-tuple-element.16.lines_ref, f32[1,8,128]{2,1,0:T(8,128)S(1)} %collective-permute-done.other_ref, f32[4,32,4096]{2,1,0:T(8,128)S(1)} %wide_blocks.1.blocks_ref, ...), custom_call_target="tpu_custom_call" | custom-call | tf_op jit(solution)/shard_map/first_image/pallas_call | solution.py:302
  6.5 13.0 %all_to_all.10.group_ref = f32[8,24,128]{2,1,0:T(8,128)S(1)} all-to-all(f32[8,24,128]{2,1,0:T(8,128)S(1)} %get-tuple-element.18), channel_id=1, replica_groups=mesh['sub'=4,'blk'=2,'rep'=4] {'blk','sub'}, dimensions={0} | all-to-all | bytes 196608 | tf_op jit(solution)/shard_map/all_to_all | solution.py:311
  19.5 0.8 %second_image.1 = (f32[16,128]{1,0:T(8,128)S(1)}, f32[16,128]{1,0:T(8,128)S(1)}) custom-call(f32[8,24,128]{2,1,0:T(8,128)S(1)} %all_to_all.10.group_ref, f32[4,32,4096]{2,1,0:T(8,128)S(1)} %wide_blocks.1.blocks_ref, bf16[128,96]{1,0:T(8,128)(2,1)S(1)} %get-tuple-element.17.choices_ref), custom_call_target="tpu_custom_call" | custom-call | tf_op jit(solution)/shard_map/second_image/pallas_call | solution.py:312
  20.3 0.6 %collective-permute-start.1 = (f32[1,16,128]{2,1,0:T(8,128)S(1)}, f32[1,16,128]{2,1,0:T(8,128)S(1)}, u32[]{:S(2)}, u32[]{:S(2)}) collective-permute-start(f32[1,16,128]{2,1,0:T(8,128)S(1)} %bitcast.15), channel_id=1, source_target_pairs={{4,0},{0,4},{5,1},{1,5},{6,2},{2,6},{7,3},{3,7},{12,8},{8,12},{13,... | collective-permute-start | bytes 24584 | tf_op jit(solution)/shard_map/ppermute | solution.py:273
  20.9 1.1 %second_inflow.1 = (f32[16,128]{1,0:T(8,128)S(1)}, f32[8,128]{1,0:T(8,128)S(1)}) custom-call(f32[16,128]{1,0:T(8,128)S(1)} %get-tuple-element.20.vector_ref, f32[16,128]{1,0:T(8,128)S(1)} %get-tuple-element.19.image_ref, f32[8,24,128]{2,1,0:T(8,128)S(1)} %all_to_all.10.group_ref, s32[1,2]{1,0:T(1,128)S(1)} %bitcast.21), custom_call_target="tpu_custom_call" | custom-call | flops 4294967296 | bytes 1048576 | tf_op jit(solution)/shard_map/second_inflow/pallas_call | solution.py:322
  22.1 2.0 %collective-permute-done.1.other_ref = f32[1,16,128]{2,1,0:T(8,128)S(1)} collective-permute-done((f32[1,16,128]{2,1,0:T(8,128)S(1)}, f32[1,16,128]{2,1,0:T(8,128)S(1)}, u32[]{:S(2)}, u32[]{:S(2)}) %collective-permute-start.1) | collective-permute-done | bytes 8224 | tf_op jit(solution)/shard_map/ppermute | solution.py:273
  24.0 0.1 pair_sums.1
  24.1 9.1 %all_to_all.11.sums_ref = f32[16,1,128]{2,1,0:T(1,128)S(1)} all-to-all(f32[16,1,128]{2,1,0:T(1,128)S(1)} %get-tuple-element.25), channel_id=1, replica_groups=mesh['sub'=4,'blk'=2,'rep'=4] {'sub','rep'}, dimensions={0} | all-to-all | bytes 16384 | tf_op jit(solution)/shard_map/all_to_all | solution.py:340
  33.2 0.7 %arnoldi_entries.1 = (f32[8,128]{1,0:T(8,128)}, f32[8,128]{1,0:T(8,128)}, f32[1,5]{1,0:T(1,128)}) custom-call(f32[8,128]{1,0:T(8,128)S(1)} %bitcast.14, f32[16,128]{1,0:T(8,128)S(1)} %get-tuple-element.19.image_ref, f32[16,128]{1,0:T(8,128)S(1)} %get-tuple-element.24.again_ref, f32[16,1,128]{2,1,0:T(1,128)S(1)} %all_to_all.11.sums_ref), custom_call_target="tpu_custom_call" | custom-call | tf_op jit(solution)/shard_map/arnoldi_entries/pallas_call | solution.py:341
Async XLA Ops:
  0.6 5.2 %collective-permute-start = (f32[1,8,128]{2,1,0:T(8,128)}, f32[1,8,128]{2,1,0:T(8,128)S(1)}, u32[]{:S(2)}, u32[]{:S(2)}) collective-permute-start(f32[1,8,128]{2,1,0:T(8,128)} %bitcast.11), channel_id=1, source_target_pairs={{4,0},{0,4},{5,1},{1,5},{6,2},{2,6},{7,3},{3,7},{12,8},{8,12},{13,... | collective-permute-start | bytes 12296 | tf_op jit(solution)/shard_map/ppermute | solution.py:273
  3.7 1.2 %copy-start.1 = (bf16[1,1,4,32,4096]{4,3,2,1,0:T(8,128)(2,1)S(1)}, bf16[1,1,4,32,4096]{4,3,2,1,0:T(8,128)(2,1)}, u32[]{:S(2)}) copy-start(bf16[1,1,4,32,4096]{4,3,2,1,0:T(8,128)(2,1)} %param.7) | copy-start | bytes 3145732
  4.9 0.7 %copy-start = (f32[1,1,1024]{2,1,0:T(1,128)S(1)}, f32[1,1,1024]{2,1,0:T(1,128)}, u32[]{:S(2)}) copy-start(f32[1,1,1024]{2,1,0:T(1,128)} %param.6) | copy-start | bytes 12292
  4.9 0.7 %copy-start.2 = (s32[1,1,8,32]{3,2,1,0:T(8,128)S(1)}, s32[1,1,8,32]{3,2,1,0:T(8,128)}, u32[]{:S(2)}) copy-start(s32[1,1,8,32]{3,2,1,0:T(8,128)} %param.8) | copy-start | bytes 3076
  4.9 0.7 %copy-start.3 = (f32[1,1,2,128]{3,2,1,0:T(2,128)S(1)}, f32[1,1,2,128]{3,2,1,0:T(2,128)}, u32[]{:S(2)}) copy-start(f32[1,1,2,128]{3,2,1,0:T(2,128)} %param.11) | copy-start | bytes 3076
  4.9 0.7 %copy-start.4 = (s32[1,1,128]{2,1,0:T(1,128)S(1)}, s32[1,1,128]{2,1,0:T(1,128)}, u32[]{:S(2)}) copy-start(s32[1,1,128]{2,1,0:T(1,128)} %param.9) | copy-start | bytes 1540
  4.9 0.7 %copy-start.5 = (s32[1,1,2]{2,1,0:T(1,128)S(1)}, s32[1,1,2]{2,1,0:T(1,128)}, u32[]{:S(2)}) copy-start(s32[1,1,2]{2,1,0:T(1,128)} %param.10) | copy-start | bytes 28
  20.3 3.7 %collective-permute-start.1 = (f32[1,16,128]{2,1,0:T(8,128)S(1)}, f32[1,16,128]{2,1,0:T(8,128)S(1)}, u32[]{:S(2)}, u32[]{:S(2)}) collective-permute-start(f32[1,16,128]{2,1,0:T(8,128)S(1)} %bitcast.15), channel_id=1, source_target_pairs={{4,0},{0,4},{5,1},{1,5},{6,2},{2,6},{7,3},{3,7},{12,8},{8,12},{13,... | collective-permute-start | bytes 24584 | tf_op jit(solution)/shard_map/ppermute | solution.py:273

commit v12 on v10

--- a/solution.py
+++ b/solution.py
@@ -46,7 +46,7 @@
     return jnp.concatenate(rows, 0).astype(jnp.bfloat16)
 
 
-def block_product(vector, blocks_ref, choices_ref, fold_ref, halves_ref):
+def block_product(vector, blocks_ref, choices_ref, fold_ref):
     slots, block_rows, width = blocks_ref.shape
     half = block_rows // 2
     lower = lane_iota(vector.shape) < BS
@@ -56,30 +56,30 @@
     picked = lax.dot_general(
         choices_ref[...], table, (((1,), (0,)), ((), ())), preferred_element_type=jnp.float32
     )
-    ones = (row_iota((2 * LANES, LANES)) % LANES) // BS == lane_iota((2 * LANES, LANES)) % 2
-    ones = ones.astype(jnp.float32).astype(jnp.bfloat16)
-    pair = (lane_iota((block_rows, LANES)) % BS) // 2
-    chunks = width // LANES
-    together = chunks // 4
-    result = jnp.zeros((block_rows, LANES), jnp.float32)
-    for first in range(0, chunks, together):
-        for c in range(first, first + together):
-            total = None
-            for k in range(slots):
-                term = blocks_ref[k, :, pl.ds(c * LANES, LANES)] * picked[k * block_rows : (k + 1) * block_rows]
-                total = term if total is None else total + term
-            high = total.astype(jnp.bfloat16)
-            here = pl.ds(c * block_rows, block_rows)
-            halves_ref[here, 0:LANES] = high
-            halves_ref[here, LANES : 2 * LANES] = (total - high.astype(jnp.float32)).astype(jnp.bfloat16)
-        sums = lax.dot_general(
-            halves_ref[pl.ds(first * block_rows, together * block_rows), :],
-            ones,
-            (((1,), (0,)), ((), ())),
-            preferred_element_type=jnp.float32,
-        )
-        for i in range(together):
-            result = jnp.where(pair == first + i, sums[i * block_rows : (i + 1) * block_rows], result)
+    lane = lane_iota((block_rows, LANES))
+
+    def exchanged(value, distance):
+        up = (lane // distance) % 2 == 1
+        return jnp.where(up, pltpu.roll(value, distance, 1), pltpu.roll(value, LANES - distance, 1))
+
+    def merged(left, right, distance):
+        up = (lane // distance) % 2 == 1
+        return jnp.where(up, right, left) + exchanged(jnp.where(up, left, right), distance)
+
+    waiting = []
+    for c in range(width // LANES):
+        total = None
+        for k in range(slots):
+            term = blocks_ref[k, :, pl.ds(c * LANES, LANES)] * picked[k * block_rows : (k + 1) * block_rows]
+            total = term if total is None else total + term
+        distance, rest = 2, c
+        while rest % 2:
+            total = merged(waiting.pop(), total, distance)
+            distance, rest = distance * 2, rest // 2
+        waiting.append(total)
+    result = waiting.pop()
+    result = result + exchanged(result, 1)
+    result = jnp.where((lane % 2 == 1) != (lane >= BS), pltpu.roll(result, BS, 1), result)
     fold_ref[...] = result
     even = fold_ref[pl.ds(0, half, stride=2), :]
     odd = fold_ref[pl.ds(1, half, stride=2), :]
@@ -122,14 +122,14 @@
     out_ref[...] = blocks_ref[...].astype(jnp.float32)
 
 
-def first_kernel(start_ref, lines_ref, other_ref, blocks_ref, choices_ref, out_ref, vector_ref, fold_ref, halves_ref):
+def first_kernel(start_ref, lines_ref, other_ref, blocks_ref, choices_ref, out_ref, vector_ref, fold_ref):
     own_rows, rows = start_ref.shape[0], vector_ref.shape[0]
     blk, parts = lax.axis_index("blk"), lax.axis_size("blk")
     for step in range(parts):
         place = lax.rem(blk + step, parts)
         place = pl.ds(pl.multiple_of(place * own_rows, SUBL), own_rows)
         vector_ref[place, :] = other_ref[step - 1] if step else start_ref[...]
-    partial = block_product(vector_ref[...], blocks_ref, choices_ref, fold_ref, halves_ref)
+    partial = block_product(vector_ref[...], blocks_ref, choices_ref, fold_ref)
     for device in range(out_ref.shape[0]):
         out_ref[device, 0:rows, :] = partial
         out_ref[device, rows : rows + SUBL, :] = lines_ref[...]
@@ -162,13 +162,13 @@
     return total
 
 
-def second_kernel(count, group_ref, blocks_ref, choices_ref, out_ref, image_ref, fold_ref, halves_ref):
+def second_kernel(count, group_ref, blocks_ref, choices_ref, out_ref, image_ref, fold_ref):
     rows = image_ref.shape[0]
     sub, parts = lax.axis_index("sub"), lax.axis_size("blk")
     added = [landed(group_ref, sub, part, rows // parts, count)[0] for part in range(parts)]
     image = summed(group_ref, sub, 0, rows) + jnp.concatenate(added, 0)
     image_ref[...] = image
-    out_ref[...] = block_product(image, blocks_ref, choices_ref, fold_ref, halves_ref)
+    out_ref[...] = block_product(image, blocks_ref, choices_ref, fold_ref)
 
 
 def down(left, right):
@@ -273,11 +273,8 @@
         return got[0] if parts == 2 else jnp.concatenate(got, 0)
 
     others = from_others(start)
-    slots, block_rows, width = blocks.shape
-    scratch = [
-        pltpu.VMEM((block_rows, LANES), jnp.float32),
-        pltpu.VMEM((block_rows * width // LANES, 2 * LANES), jnp.bfloat16),
-    ]
+    slots, block_rows = blocks.shape[:2]
+    scratch = [pltpu.VMEM((block_rows, LANES), jnp.float32)]
     lines, chosen = pl.pallas_call(
         lines_kernel,
         out_shape=(rowed(SUBL), jax.ShapeDtypeStruct((slots * block_rows, 3 * block_rows), jnp.bfloat16)),

time: 34 us -> 34.5 us (1.015)
  Pallas kernels: 3.73 us -> 4.31 us
where the time goes in v12:
time: 34.5 us; the launch traced here: 34.3 us
  blocking collectives  22 us (64%)
  Pallas kernels  4.31 us (12%)
  starting transfers between devices  3.36 us (10%)
  waiting for transfers between devices  2.22 us (6%)
  local copies, waits for them, and re-layouts  1.78 us (5%)
  between operations  0.67 us (2%)
    all_to_all x1, blocking collectives, per_device(): group = lax.all_to_all(partial, ('sub', 'blk'), 0, 0, tiled=True)  12.9 us
    all_to_all x1, blocking collectives, per_device(): sums = lax.all_to_all(sums, ('rep', 'sub'), 0, 0, tiled=True)  9.03 us
    ppermute x2, starting transfers between devices, from_others(): lax.ppermute(value[None], 'blk', [((i + step) % parts, i) for i in range(...  3.36 us
    ppermute x2, waiting for transfers between devices, from_others(): lax.ppermute(value[None], 'blk', [((i + step) % parts, i) for i in range(...  2.22 us
    unnamed x12, local copies, waits for them, and re-layouts  1.78 us
    pallas_call x1, Pallas kernels, per_device(): pl.pallas_call(inflow_kernel, out_shape=(rowed(rows), rowed(SUBL)), in_sp...  1.13 us
    pallas_call x1, Pallas kernels, per_device(): pl.pallas_call(functools.partial(second_kernel, coupling.shape[0]), out_s...  1.08 us
    pallas_call x1, Pallas kernels, per_device(): pl.pallas_call(first_kernel, out_shape=(rowed(subs * parts, rows + SUBL),...  0.94 us
  transfers between devices with their start and end apart: 2, of which 1 were waited for; matrix products, arithmetic and copies ran while one was open for 0% of the time, Pallas kernels for 4%

profile of v12, /device:TPU:0, one launch (start us, length us, event | category | flops | bytes accessed | tf_op | source)
XLA Modules:
  0.0 34.3 jit_solution(16945094046840737951)
XLA Ops:
  0.6 3.0 %collective-permute-start = (f32[1,8,128]{2,1,0:T(8,128)}, f32[1,8,128]{2,1,0:T(8,128)S(1)}, u32[]{:S(2)}, u32[]{:S(2)}) collective-permute-start(f32[1,8,128]{2,1,0:T(8,128)} %bitcast.11), channel_id=1, source_target_pairs={{4,0},{0,4},{5,1},{1,5},{6,2},{2,6},{7,3},{3,7},{12,8},{8,12},{13,... | collective-permute-start | bytes 12296 | tf_op jit(solution)/shard_map/ppermute | solution.py:270
  3.7 0.0 copy-start.1
  3.7 1.2 %copy-done.1 = bf16[1,1,4,32,4096]{4,3,2,1,0:T(8,128)(2,1)S(1)} copy-done((bf16[1,1,4,32,4096]{4,3,2,1,0:T(8,128)(2,1)S(1)}, bf16[1,1,4,32,4096]{4,3,2,1,0:T(8,128)(2,1)}, u32[]{:S(2)}) %copy-start.1) | copy-done | bytes 1048600
  4.9 0.0 copy-start
  4.9 0.0 copy-start.2
  4.9 0.0 copy-start.3
  4.9 0.0 copy-start.4
  4.9 0.0 copy-start.5
  4.9 0.1 wide_blocks.1.blocks_ref
  5.1 0.5 %copy-done = f32[1,1,1024]{2,1,0:T(1,128)S(1)} copy-done((f32[1,1,1024]{2,1,0:T(1,128)S(1)}, f32[1,1,1024]{2,1,0:T(1,128)}, u32[]{:S(2)}) %copy-start) | copy-done | bytes 4120
  5.6 0.0 copy-done.2
  5.6 0.0 copy-done.3
  5.6 0.0 copy-done.4
  5.6 0.0 copy-done.5
  5.6 0.2 group_lines.1
  5.8 0.0 collective-permute-done.other_ref
  5.8 0.9 %first_image.1 = (f32[8,24,128]{2,1,0:T(8,128)S(1)}, f32[16,128]{1,0:T(8,128)S(1)}) custom-call(f32[8,128]{1,0:T(8,128)S(1)} %bitcast.13, f32[8,128]{1,0:T(8,128)S(1)} %get-tuple-element.16.lines_ref, f32[1,8,128]{2,1,0:T(8,128)S(1)} %collective-permute-done.other_ref, f32[4,32,4096]{2,1,0:T(8,128)S(1)} %wide_blocks.1.blocks_ref, ...), custom_call_target="tpu_custom_call" | custom-call | tf_op jit(solution)/shard_map/first_image/pallas_call | solution.py:296
  6.7 12.9 %all_to_all.10.group_ref = f32[8,24,128]{2,1,0:T(8,128)S(1)} all-to-all(f32[8,24,128]{2,1,0:T(8,128)S(1)} %get-tuple-element.18), channel_id=1, replica_groups=mesh['sub'=4,'blk'=2,'rep'=4] {'sub','blk'}, dimensions={0} | all-to-all | bytes 196608 | tf_op jit(solution)/shard_map/all_to_all | solution.py:305
  19.7 1.1 %second_image.1 = (f32[16,128]{1,0:T(8,128)S(1)}, f32[16,128]{1,0:T(8,128)S(1)}) custom-call(f32[8,24,128]{2,1,0:T(8,128)S(1)} %all_to_all.10.group_ref, f32[4,32,4096]{2,1,0:T(8,128)S(1)} %wide_blocks.1.blocks_ref, bf16[128,96]{1,0:T(8,128)(2,1)S(1)} %get-tuple-element.17.choices_ref), custom_call_target="tpu_custom_call" | custom-call | tf_op jit(solution)/shard_map/second_image/pallas_call | solution.py:306
  20.7 0.3 collective-permute-start.1
  21.1 1.1 %second_inflow.1 = (f32[16,128]{1,0:T(8,128)S(1)}, f32[8,128]{1,0:T(8,128)S(1)}) custom-call(f32[16,128]{1,0:T(8,128)S(1)} %get-tuple-element.20.vector_ref, f32[16,128]{1,0:T(8,128)S(1)} %get-tuple-element.19.image_ref, f32[8,24,128]{2,1,0:T(8,128)S(1)} %all_to_all.10.group_ref, s32[1,2]{1,0:T(1,128)S(1)} %bitcast.21), custom_call_target="tpu_custom_call" | custom-call | flops 4294967296 | bytes 1048576 | tf_op jit(solution)/shard_map/second_inflow/pallas_call | solution.py:316
  22.2 2.2 %collective-permute-done.1.other_ref = f32[1,16,128]{2,1,0:T(8,128)S(1)} collective-permute-done((f32[1,16,128]{2,1,0:T(8,128)S(1)}, f32[1,16,128]{2,1,0:T(8,128)S(1)}, u32[]{:S(2)}, u32[]{:S(2)}) %collective-permute-start.1) | collective-permute-done | bytes 8224 | tf_op jit(solution)/shard_map/ppermute | solution.py:270
  24.4 0.1 pair_sums.1
  24.5 9.0 %all_to_all.11.sums_ref = f32[16,1,128]{2,1,0:T(1,128)S(1)} all-to-all(f32[16,1,128]{2,1,0:T(1,128)S(1)} %get-tuple-element.25), channel_id=1, replica_groups=mesh['sub'=4,'blk'=2,'rep'=4] {'rep','sub'}, dimensions={0} | all-to-all | bytes 16384 | tf_op jit(solution)/shard_map/all_to_all | solution.py:334
  33.6 0.7 %arnoldi_entries.1 = (f32[8,128]{1,0:T(8,128)}, f32[8,128]{1,0:T(8,128)}, f32[1,5]{1,0:T(1,128)}) custom-call(f32[8,128]{1,0:T(8,128)S(1)} %bitcast.14, f32[16,128]{1,0:T(8,128)S(1)} %get-tuple-element.19.image_ref, f32[16,128]{1,0:T(8,128)S(1)} %get-tuple-element.24.again_ref, f32[16,1,128]{2,1,0:T(1,128)S(1)} %all_to_all.11.sums_ref), custom_call_target="tpu_custom_call" | custom-call | tf_op jit(solution)/shard_map/arnoldi_entries/pallas_call | solution.py:335
Async XLA Ops:
  0.6 5.2 %collective-permute-start = (f32[1,8,128]{2,1,0:T(8,128)}, f32[1,8,128]{2,1,0:T(8,128)S(1)}, u32[]{:S(2)}, u32[]{:S(2)}) collective-permute-start(f32[1,8,128]{2,1,0:T(8,128)} %bitcast.11), channel_id=1, source_target_pairs={{4,0},{0,4},{5,1},{1,5},{6,2},{2,6},{7,3},{3,7},{12,8},{8,12},{13,... | collective-permute-start | bytes 12296 | tf_op jit(solution)/shard_map/ppermute | solution.py:270
  3.7 1.2 %copy-start.1 = (bf16[1,1,4,32,4096]{4,3,2,1,0:T(8,128)(2,1)S(1)}, bf16[1,1,4,32,4096]{4,3,2,1,0:T(8,128)(2,1)}, u32[]{:S(2)}) copy-start(bf16[1,1,4,32,4096]{4,3,2,1,0:T(8,128)(2,1)} %param.7) | copy-start | bytes 3145732
  4.9 0.7 %copy-start = (f32[1,1,1024]{2,1,0:T(1,128)S(1)}, f32[1,1,1024]{2,1,0:T(1,128)}, u32[]{:S(2)}) copy-start(f32[1,1,1024]{2,1,0:T(1,128)} %param.6) | copy-start | bytes 12292
  4.9 0.7 %copy-start.2 = (s32[1,1,8,32]{3,2,1,0:T(8,128)S(1)}, s32[1,1,8,32]{3,2,1,0:T(8,128)}, u32[]{:S(2)}) copy-start(s32[1,1,8,32]{3,2,1,0:T(8,128)} %param.8) | copy-start | bytes 3076
  4.9 0.7 %copy-start.3 = (f32[1,1,2,128]{3,2,1,0:T(2,128)S(1)}, f32[1,1,2,128]{3,2,1,0:T(2,128)}, u32[]{:S(2)}) copy-start(f32[1,1,2,128]{3,2,1,0:T(2,128)} %param.11) | copy-start | bytes 3076
  4.9 0.7 %copy-start.4 = (s32[1,1,128]{2,1,0:T(1,128)S(1)}, s32[1,1,128]{2,1,0:T(1,128)}, u32[]{:S(2)}) copy-start(s32[1,1,128]{2,1,0:T(1,128)} %param.9) | copy-start | bytes 1540
  4.9 0.7 %copy-start.5 = (s32[1,1,2]{2,1,0:T(1,128)S(1)}, s32[1,1,2]{2,1,0:T(1,128)}, u32[]{:S(2)}) copy-start(s32[1,1,2]{2,1,0:T(1,128)} %param.10) | copy-start | bytes 28
  20.7 3.7 %collective-permute-start.1 = (f32[1,16,128]{2,1,0:T(8,128)S(1)}, f32[1,16,128]{2,1,0:T(8,128)S(1)}, u32[]{:S(2)}, u32[]{:S(2)}) collective-permute-start(f32[1,16,128]{2,1,0:T(8,128)S(1)} %bitcast.15), channel_id=1, source_target_pairs={{4,0},{0,4},{5,1},{1,5},{6,2},{2,6},{7,3},{3,7},{12,8},{8,12},{13,... | collective-permute-start | bytes 24584 | tf_op jit(solution)/shard_map/ppermute | solution.py:270

commit v13 on v10

v13 whole, which is shorter than its diff:
```python
import functools

import jax
import jax.numpy as jnp
from jax import lax
from jax.experimental import pallas as pl
from jax.experimental.pallas import tpu as pltpu
from jax.sharding import PartitionSpec as P

BS = 64
LANES = 128
SUBL = 8
epsilon = 1e-06


def pieces(value):
    high = value.astype(jnp.bfloat16)
    rest = value - high.astype(jnp.float32)
    middle = rest.astype(jnp.bfloat16)
    low = (rest - middle.astype(jnp.float32)).astype(jnp.bfloat16)
    return high, middle, low


def lane_iota(shape):
    return lax.broadcasted_iota(jnp.int32, shape, len(shape) - 1)


def row_iota(shape):
    return lax.broadcasted_iota(jnp.int32, shape, 0)


def choices(pattern_ref, slot):
    block_rows = pattern_ref.shape[1]
    half = block_rows // 2
    place = row_iota((block_rows, block_rows))
    place = jnp.where(place < half, 2 * place, 2 * (place - half) + 1)
    thrice = (block_rows, 3 * block_rows)
    copies = (lane_iota(thrice) % block_rows == row_iota(thrice)).astype(jnp.float32).astype(jnp.bfloat16)
    chosen = (place == pattern_ref[pl.ds(slot, 1), :]).astype(jnp.float32).astype(jnp.bfloat16)
    return lax.dot_general(chosen, copies, (((0,), (0,)), ((), ())), preferred_element_type=jnp.float32)


def block_product(vector, fetch, width, chosen, fold_ref, halves_ref):
    block_rows = fold_ref.shape[0]
    slots = chosen.shape[0] // block_rows
    half = block_rows // 2
    lower = lane_iota(vector.shape) < BS
    turned = pltpu.roll(vector, BS, 1)
    table = jnp.concatenate([jnp.where(lower, vector, turned), jnp.where(lower, turned, vector)], 0)
    table = jnp.concatenate(pieces(table), 0)
    picked = lax.dot_general(chosen, table, (((1,), (0,)), ((), ())), preferred_element_type=jnp.float32)
    ones = (row_iota((2 * LANES, LANES)) % LANES) // BS == lane_iota((2 * LANES, LANES)) % 2
    ones = ones.astype(jnp.float32).astype(jnp.bfloat16)
    pair = (lane_iota((block_rows, LANES)) % BS) // 2
    chunks = width // LANES
    together = chunks // 4
    result = jnp.zeros((block_rows, LANES), jnp.float32)
    for first in range(0, chunks, together):
        for c in range(first, first + together):
            total = None
            for k in range(slots):
                term = fetch(k, pl.ds(c * LANES, LANES)) * picked[k * block_rows : (k + 1) * block_rows]
                total = term if total is None else total + term
            high = total.astype(jnp.bfloat16)
            here = pl.ds(c * block_rows, block_rows)
            halves_ref[here, 0:LANES] = high
            halves_ref[here, LANES : 2 * LANES] = (total - high.astype(jnp.float32)).astype(jnp.bfloat16)
        sums = lax.dot_general(
            halves_ref[pl.ds(first * block_rows, together * block_rows), :],
            ones,
            (((1,), (0,)), ((), ())),
            preferred_element_type=jnp.float32,
        )
        for i in range(together):
            result = jnp.where(pair == first + i, sums[i * block_rows : (i + 1) * block_rows], result)
    fold_ref[...] = result
    even = fold_ref[pl.ds(0, half, stride=2), :]
    odd = fold_ref[pl.ds(1, half, stride=2), :]
    return jnp.where(lane_iota((half, LANES)) < BS, even, odd)


def take_trace(rows, places):
    count = rows.shape[0]
    low = jnp.broadcast_to(places % LANES, (count, LANES))
    picked = jnp.take_along_axis(rows, low, axis=1)
    return jnp.sum(jnp.where(row_iota((count, LANES)) == places // LANES, picked, 0.0), axis=0, keepdims=True)


def spread(values, places, count):
    aimed = jnp.where(row_iota((count, LANES)) == places // LANES, values, 0.0)
    high = aimed.astype(jnp.bfloat16).astype(jnp.float32)
    rest = aimed - high
    middle = rest.astype(jnp.bfloat16).astype(jnp.float32)
    stack = jnp.concatenate([high, middle, rest - middle], 0).astype(jnp.bfloat16)
    target = (row_iota((LANES, LANES)) == places % LANES).astype(jnp.float32).astype(jnp.bfloat16)
    landed = lax.dot_general(stack, target, (((1,), (1,)), ((), ())), preferred_element_type=jnp.float32)
    return landed[0:count] + landed[count : 2 * count] + landed[2 * count : 3 * count]


def lines_kernel(
    start_ref, map_ref, near_ref, coupling_ref, pattern_ref, out_ref, first_ref, second_ref, rows_ref
):
    places = map_ref[...]
    count = coupling_ref.shape[0]
    blk, parts = lax.axis_index("blk"), lax.axis_size("blk")
    lines = [take_trace(start_ref[...], places - blk * start_ref.shape[0] * LANES), places.astype(jnp.float32)]
    lines += [coupling_ref[n : n + 1, :] for n in range(count)]
    near = near_ref[...].astype(jnp.float32)
    lines += [jnp.broadcast_to(near[:, n : n + 1], (1, LANES)) for n in range(count)]
    lines += [jnp.zeros((SUBL - len(lines), LANES), jnp.float32)]
    out_ref[...] = jnp.concatenate(lines, 0)
    all_slots, block_rows = pattern_ref.shape
    slots = all_slots // parts
    own_rows = block_rows // parts
    for step in range(parts):
        for k in range(slots):
            at = step * slots + k
            chosen = choices(pattern_ref, lax.rem(blk + step, parts) * slots + k)
            if step == 0:
                first_ref[k * block_rows : (k + 1) * block_rows, :] = chosen.astype(jnp.bfloat16)
            rows_ref[...] = chosen
            own = rows_ref[pl.ds(pl.multiple_of(blk * own_rows, SUBL), own_rows), :]
            second_ref[at * own_rows : (at + 1) * own_rows, :] = own.astype(jnp.bfloat16)


def widen_kernel(blocks_ref, out_ref, send_ref):
    out_ref[...] = blocks_ref[...].astype(jnp.float32)
    others, _, own_rows, _ = send_ref.shape
    blk, parts = lax.axis_index("blk"), lax.axis_size("blk")
    for step in range(1, others + 1):
        part = lax.rem(blk + parts - step, parts)
        send_ref[step - 1] = blocks_ref[:, pl.ds(pl.multiple_of(part * own_rows, 16), own_rows), :]


def first_kernel(
    start_ref, lines_ref, other_ref, blocks_ref, choices_ref, out_ref, vector_ref, fold_ref, halves_ref
):
    own_rows, rows = start_ref.shape[0], vector_ref.shape[0]
    blk, parts = lax.axis_index("blk"), lax.axis_size("blk")
    for step in range(parts):
        place = lax.rem(blk + step, parts)
        place = pl.ds(pl.multiple_of(place * own_rows, SUBL), own_rows)
        vector_ref[place, :] = other_ref[step - 1] if step else start_ref[...]

    def fetch(k, lanes):
        return blocks_ref[k, :, lanes]

    partial = block_product(
        vector_ref[...], fetch, blocks_ref.shape[2], choices_ref[...], fold_ref, halves_ref
    )
    for device in range(out_ref.shape[0]):
        out_ref[device, 0:rows, :] = partial
        out_ref[device, rows : rows + SUBL, :] = lines_ref[...]


def line(group_ref, device, i):
    first = group_ref.shape[1] - SUBL + i
    return group_ref[device, first : first + 1, :]


def landed(group_ref, sub_at, part, own_rows, count):
    parts = lax.axis_size("blk")
    traces = [line(group_ref, other * parts + part, 0) for other in range(lax.axis_size("sub"))]
    traces = jnp.concatenate(traces, 0)
    names = row_iota(traces.shape).astype(jnp.float32)
    device = sub_at * parts + part
    inflow = jnp.zeros((1, LANES), jnp.float32)
    for n in range(count):
        chosen = jnp.where(names == line(group_ref, device, 2 + count + n), traces, 0.0)
        inflow = inflow + line(group_ref, device, 2 + n) * jnp.sum(chosen, axis=0, keepdims=True)
    places = line(group_ref, device, 1).astype(jnp.int32) - part * own_rows * LANES
    return spread(inflow, places, own_rows), places


def summed(group_ref, sub_at, where):
    parts = lax.axis_size("blk")
    total = group_ref[sub_at * parts, where, :]
    for b in range(1, parts):
        total = total + group_ref[sub_at * parts + b, where, :]
    return total


def down(left, right):
    return jnp.sum(left * right, axis=0, keepdims=True)


def second_kernel(
    start_ref,
    group_ref,
    blocks_ref,
    other_ref,
    choices_ref,
    near_ref,
    out_ref,
    image_ref,
    again_ref,
    whole_ref,
    fold_ref,
    halves_ref,
):
    own_rows = start_ref.shape[0]
    slots, block_rows, width = blocks_ref.shape
    count = near_ref.shape[1]
    sub, blk, parts = lax.axis_index("sub"), lax.axis_index("blk"), lax.axis_size("blk")
    own_blocks = block_rows // parts
    here = pl.ds(pl.multiple_of(blk * own_blocks, 16), own_blocks)
    own = pl.ds(pl.multiple_of(blk * own_rows, SUBL), own_rows)
    added = [landed(group_ref, sub, part, own_rows, count)[0] for part in range(parts)]
    image = summed(group_ref, sub, pl.ds(0, own_rows * parts)) + jnp.concatenate(added, 0)
    whole_ref[...] = image

    def fetch(k, lanes):
        if k < slots:
            return blocks_ref[k, here, lanes]
        return other_ref[k // slots - 1, k % slots, :, lanes].astype(jnp.float32)

    again = block_product(image, fetch, width, choices_ref[...], fold_ref, halves_ref)
    inflow = jnp.zeros((1, LANES), jnp.float32)
    for n in range(count):
        source = near_ref[0, n]
        added, places = landed(group_ref, source, blk, own_rows, count)
        trace = take_trace(summed(group_ref, source, own) + added, places)
        inflow = inflow + line(group_ref, sub * parts + blk, 2 + n) * trace
    places = line(group_ref, sub * parts + blk, 1).astype(jnp.int32) - blk * own_rows * LANES
    again = again + spread(inflow, places, own_rows)
    again_ref[...] = again
    vector, image = start_ref[...], whole_ref[own, :]
    image_ref[...] = image
    sums = [down(vector, vector), down(vector, image), down(image, image)]
    sums += [down(vector, again), down(image, again), down(again, again)]
    sums = jnp.concatenate([*sums, jnp.zeros((SUBL - 6, LANES), jnp.float32)], 0)
    sums = jnp.sum(sums, axis=1, keepdims=True)
    sums = jnp.where(row_iota((SUBL, LANES)) == lane_iota((SUBL, LANES)), sums, 0.0)
    sums = jnp.sum(sums, axis=0, keepdims=True)
    for device in range(out_ref.shape[0]):
        out_ref[device] = sums


def last_kernel(cells, start_ref, image_ref, again_ref, sums_ref, second_ref, third_ref, entries_ref):
    sums = jnp.sum(sums_ref[...], axis=0) / cells

    def whole(i):
        return jnp.broadcast_to(sums[:, i : i + 1], (1, LANES))

    vv, vw, ww, vy, wy, yy = (whole(i) for i in range(6))
    norm_square = vv + epsilon
    inverse = 1.0 / norm_square
    h11 = vw * inverse
    skew = vy - h11 * vw
    first_square = jnp.maximum(ww - 2.0 * h11 * vw + h11 * h11 * vv, 0.0) * inverse + epsilon
    over_first = lax.rsqrt(first_square)
    h21 = first_square * over_first
    scale = lax.rsqrt(norm_square) * over_first
    h12 = skew * inverse * over_first
    h22 = (wy - h11 * (ww + skew)) * scale * scale
    near = h11 + h22
    far = skew * inverse - h11 * h22
    second_square = yy + near * near * ww + far * far * vv + 2.0 * (near * far * vw - near * wy - far * vy)
    second_square = jnp.maximum(second_square, 0.0) * scale * scale + epsilon
    over_second = lax.rsqrt(second_square)
    h32 = second_square * over_second

    vector, image = start_ref[...], image_ref[...]
    second_ref[...] = (image - h11 * vector) * scale
    third_ref[...] = (again_ref[...] - near * image - far * vector) * (scale * over_second)
    lane = lane_iota((1, LANES))
    entries = h32
    for i, value in enumerate((h11, h21, h12, h22)):
        entries = jnp.where(lane == i, value, entries)
    entries_ref[...] = entries[:, 0:5]


def per_device(start_vector, blocks, pattern, trace_map, neighbours, coupling):
    own_cells = start_vector.shape[2]
    own_rows = own_cells // LANES
    parts, subs, reps = lax.axis_size("blk"), lax.axis_size("sub"), lax.axis_size("rep")
    rows = own_rows * parts
    cells = own_cells * parts * subs * reps
    start = start_vector.reshape(own_rows, LANES)
    local_map = trace_map[0]
    blocks, pattern, neighbours, coupling = blocks[0, 0], pattern[0, 0], neighbours[0], coupling[0, 0]
    vmem = pl.BlockSpec(memory_space=pltpu.VMEM)
    params = pltpu.CompilerParams(vmem_limit_bytes=32 * 1024 * 1024)

    def rowed(*shape):
        return jax.ShapeDtypeStruct((*shape, LANES), jnp.float32)

    smem = pl.BlockSpec(memory_space=pltpu.SMEM)

    def from_others(pick):
        got = [
            lax.ppermute(pick(step), "blk", [((i + step) % parts, i) for i in range(parts)])
            for step in range(1, parts)
        ]
        return got[0] if parts == 2 else jnp.concatenate(got, 0)

    slots, block_rows, width = blocks.shape
    own_blocks = block_rows // parts

    def scratch(count):
        return [
            pltpu.VMEM((count, LANES), jnp.float32),
            pltpu.VMEM((count * width // LANES, 2 * LANES), jnp.bfloat16),
        ]

    def shaped(dtype, *shape):
        return jax.ShapeDtypeStruct(shape, dtype)

    long = pl.CostEstimate(flops=1 << 32, bytes_accessed=1 << 20, transcendentals=0)
    others = from_others(lambda step: start[None])
    wide, send = pl.pallas_call(
        widen_kernel,
        out_shape=(
            shaped(jnp.float32, *blocks.shape),
            shaped(jnp.bfloat16, parts - 1, slots, own_blocks, width),
        ),
        in_specs=[vmem],
        out_specs=(vmem, vmem),
        compiler_params=params,
        cost_estimate=long,
        name="wide_blocks",
    )(blocks)
    other_blocks = from_others(lambda step: send if parts == 2 else send[step - 1 : step])
    lines, chosen, chosen_own = pl.pallas_call(
        lines_kernel,
        out_shape=(
            rowed(SUBL),
            shaped(jnp.bfloat16, slots * block_rows, 3 * block_rows),
            shaped(jnp.bfloat16, slots * block_rows, 3 * block_rows),
        ),
        in_specs=[vmem] * 5,
        out_specs=(vmem, vmem, vmem),
        scratch_shapes=[pltpu.VMEM((block_rows, 3 * block_rows), jnp.float32)],
        compiler_params=params,
        cost_estimate=long,
        name="group_lines",
    )(start, local_map, neighbours, coupling, pattern)
    partial, vector = pl.pallas_call(
        first_kernel,
        out_shape=(rowed(subs * parts, rows + SUBL), rowed(rows)),
        in_specs=[vmem] * 5,
        out_specs=(vmem, vmem),
        scratch_shapes=scratch(block_rows),
        compiler_params=params,
        name="first_image",
    )(start, lines, others, wide, chosen)
    group = lax.all_to_all(partial, ("sub", "blk"), 0, 0, tiled=True)
    sums, image, again = pl.pallas_call(
        second_kernel,
        out_shape=(rowed(reps * subs * parts, 1), rowed(own_rows), rowed(own_rows)),
        in_specs=[vmem] * 5 + [smem],
        out_specs=(vmem, vmem, vmem),
        scratch_shapes=[pltpu.VMEM((rows, LANES), jnp.float32), *scratch(own_blocks)],
        compiler_params=params,
        name="second_image",
    )(start, group, wide, other_blocks, chosen_own, neighbours)
    sums = lax.all_to_all(sums, ("rep", "sub", "blk"), 0, 0, tiled=True)
    second, third, entries = pl.pallas_call(
        functools.partial(last_kernel, float(cells)),
        out_shape=(rowed(own_rows), rowed(own_rows), jax.ShapeDtypeStruct((1, 5), jnp.float32)),
        in_specs=[vmem] * 4,
        out_specs=(vmem, vmem, vmem),
        compiler_params=params,
        name="arnoldi_entries",
    )(start, image, again, sums)
    return second.reshape(start_vector.shape), third.reshape(start_vector.shape), entries.reshape(5)


def solution(mesh):
    return jax.shard_map(
        per_device,
        mesh=mesh,
        in_specs=(
            P("rep", "sub", "blk"),
            P("rep", "sub", "blk", None, None),
            P("rep", "sub", None, None),
            P("rep", "sub", "blk"),
            P("rep", "sub", None),
            P("rep", "sub", None, "blk"),
        ),
        out_specs=(P("rep", "sub", "blk"), P("rep", "sub", "blk"), P()),
        check_vma=False,
    )
```

time: 34 us -> 34 us (level)
  blocking collectives: 21.9 us -> 24.9 us
  waiting for transfers between devices: 2.22 us -> 0.01 us
    all_to_all x1, blocking collectives: 9.03 us -> 11.8 us  [per_device(): sums = lax.all_to_all(sums, ('rep', 'sub', 'blk'), 0, 0, tiled=True)]
    ppermute x2, waiting for transfers between devices: 2.22 us -> 0.01 us  [from_others(): lax.ppermute(pick(step), 'blk', [((i + step) % parts, i) for i in range(p...]
    pallas_call x5 -> x3, Pallas kernels: 2.36 us -> 2.02 us  [the longest x1 1.61 us: per_device(): pl.pallas_call(second_kernel, out_shape=(rowed(reps * subs * parts, 1), r...]
  transfers between devices with their start and end apart: 2 -> 2, of which waited for: 1 -> 0; matrix products, arithmetic and copies ran while one was open for 0% -> 0% of each run, Pallas kernels for 4% -> 3%
where the time goes in v13:
time: 34 us; the launch traced here: 33.8 us
  blocking collectives  24.9 us (73%)
  Pallas kernels  3.4 us (10%)
  starting transfers between devices  3.11 us (9%)
  local copies, waits for them, and re-layouts  1.68 us (5%)
  between operations  0.68 us (2%)
    all_to_all x1, blocking collectives, per_device(): group = lax.all_to_all(partial, ('sub', 'blk'), 0, 0, tiled=True)  13.1 us
    all_to_all x1, blocking collectives, per_device(): sums = lax.all_to_all(sums, ('rep', 'sub', 'blk'), 0, 0, tiled=True)  11.8 us
    ppermute x2, starting transfers between devices, from_others(): lax.ppermute(pick(step), 'blk', [((i + step) % parts, i) for i in range(p...  3.11 us
    unnamed x12, local copies, waits for them, and re-layouts  1.68 us
    pallas_call x1, Pallas kernels, per_device(): pl.pallas_call(second_kernel, out_shape=(rowed(reps * subs * parts, 1), r...  1.61 us
    pallas_call x1, Pallas kernels, per_device(): pl.pallas_call(functools.partial(last_kernel, float(cells)), out_shape=(r...  0.74 us
  transfers between devices with their start and end apart: 2, of which 0 were waited for; matrix products, arithmetic and copies ran while one was open for 0% of the time, Pallas kernels for 3%

profile of v13, /device:TPU:0, one launch (start us, length us, event | category | flops | bytes accessed | tf_op | source)
XLA Modules:
  0.0 33.8 jit_solution(5751822408174803339)
XLA Ops:
  0.6 3.0 %collective-permute-start = (f32[1,8,128]{2,1,0:T(8,128)}, f32[1,8,128]{2,1,0:T(8,128)S(1)}, u32[]{:S(2)}, u32[]{:S(2)}) collective-permute-start(f32[1,8,128]{2,1,0:T(8,128)} %bitcast.10), channel_id=1, source_target_pairs={{4,0},{0,4},{5,1},{1,5},{6,2},{2,6},{7,3},{3,7},{12,8},{8,12},{13,... | collective-permute-start | bytes 12296 | tf_op jit(solution)/shard_map/ppermute | solution.py:292
  3.7 0.0 copy-start.2
  3.7 1.2 %copy-done.2 = bf16[1,1,4,32,4096]{4,3,2,1,0:T(8,128)(2,1)S(1)} copy-done((bf16[1,1,4,32,4096]{4,3,2,1,0:T(8,128)(2,1)S(1)}, bf16[1,1,4,32,4096]{4,3,2,1,0:T(8,128)(2,1)}, u32[]{:S(2)}) %copy-start.2) | copy-done | bytes 1048600
  4.9 0.0 copy-start
  4.9 0.0 copy-start.1
  4.9 0.0 copy-start.3
  4.9 0.0 copy-start.4
  4.9 0.0 copy-start.5
  4.9 0.2 wide_blocks.1
  5.1 0.1 collective-permute-start.1
  5.2 0.4 %copy-done = f32[1,1,1024]{2,1,0:T(1,128)S(1)} copy-done((f32[1,1,1024]{2,1,0:T(1,128)S(1)}, f32[1,1,1024]{2,1,0:T(1,128)}, u32[]{:S(2)}) %copy-start) | copy-done | bytes 4120
  5.6 0.0 copy-done.1
  5.6 0.0 copy-done.3
  5.6 0.0 copy-done.4
  5.6 0.0 copy-done.5
  5.6 0.2 group_lines.1
  5.9 0.0 collective-permute-done.other_ref
  5.9 0.6 %first_image.1 = (f32[8,24,128]{2,1,0:T(8,128)S(1)}, f32[16,128]{1,0:T(8,128)}) custom-call(f32[8,128]{1,0:T(8,128)S(1)} %bitcast.12, f32[8,128]{1,0:T(8,128)S(1)} %get-tuple-element.15.lines_ref, f32[1,8,128]{2,1,0:T(8,128)S(1)} %collective-permute-done.other_ref, f32[4,32,4096]{2,1,0:T(8,128)S(1)} %get-tuple-element.16.blocks_ref, ...), custom_call_target="tpu_custom_call" | custom-call | tf_op jit(solution)/shard_map/first_image/pallas_call | solution.py:338
  6.5 13.1 %all_to_all.10.group_ref = f32[8,24,128]{2,1,0:T(8,128)S(1)} all-to-all(f32[8,24,128]{2,1,0:T(8,128)S(1)} %get-tuple-element.18), channel_id=1, replica_groups=mesh['sub'=4,'blk'=2,'rep'=4] {'sub','blk'}, dimensions={0} | all-to-all | bytes 196608 | tf_op jit(solution)/shard_map/all_to_all | solution.py:347
  19.6 0.0 collective-permute-done.1.other_ref
  19.6 1.6 %second_image.1 = (f32[32,1,128]{2,1,0:T(1,128)S(1)}, f32[8,128]{1,0:T(8,128)S(1)}, f32[8,128]{1,0:T(8,128)S(1)}) custom-call(f32[8,128]{1,0:T(8,128)S(1)} %bitcast.13, f32[8,24,128]{2,1,0:T(8,128)S(1)} %all_to_all.10.group_ref, f32[4,32,4096]{2,1,0:T(8,128)S(1)} %get-tuple-element.16.blocks_ref, ...), custom_call_target="tpu_custom_call" | custom-call | tf_op jit(solution)/shard_map/second_image/pallas_call | solution.py:348
  21.2 11.8 %all_to_all.11.sums_ref = f32[32,1,128]{2,1,0:T(1,128)S(1)} all-to-all(f32[32,1,128]{2,1,0:T(1,128)S(1)} %get-tuple-element.23), channel_id=1, replica_groups=mesh['sub'=4,'blk'=2,'rep'=4] {'rep','sub','blk'}, dimensions={0} | all-to-all | bytes 32768 | tf_op jit(solution)/shard_map/all_to_all | solution.py:357
  33.0 0.7 %arnoldi_entries.1 = (f32[8,128]{1,0:T(8,128)}, f32[8,128]{1,0:T(8,128)}, f32[1,5]{1,0:T(1,128)}) custom-call(f32[8,128]{1,0:T(8,128)S(1)} %bitcast.14, f32[8,128]{1,0:T(8,128)S(1)} %get-tuple-element.21.image_ref, f32[8,128]{1,0:T(8,128)S(1)} %get-tuple-element.22.again_ref, f32[32,1,128]{2,1,0:T(1,128)S(1)} %all_to_all.11.sums_ref), custom_call_target="tpu_custom_call" | custom-call | tf_op jit(solution)/shard_map/arnoldi_entries/pallas_call | solution.py:358
Async XLA Ops:
  0.6 5.2 %collective-permute-start = (f32[1,8,128]{2,1,0:T(8,128)}, f32[1,8,128]{2,1,0:T(8,128)S(1)}, u32[]{:S(2)}, u32[]{:S(2)}) collective-permute-start(f32[1,8,128]{2,1,0:T(8,128)} %bitcast.10), channel_id=1, source_target_pairs={{4,0},{0,4},{5,1},{1,5},{6,2},{2,6},{7,3},{3,7},{12,8},{8,12},{13,... | collective-permute-start | bytes 12296 | tf_op jit(solution)/shard_map/ppermute | solution.py:292
  3.7 1.2 %copy-start.2 = (bf16[1,1,4,32,4096]{4,3,2,1,0:T(8,128)(2,1)S(1)}, bf16[1,1,4,32,4096]{4,3,2,1,0:T(8,128)(2,1)}, u32[]{:S(2)}) copy-start(bf16[1,1,4,32,4096]{4,3,2,1,0:T(8,128)(2,1)} %param.7) | copy-start | bytes 3145732
  4.9 0.7 %copy-start = (f32[1,1,1024]{2,1,0:T(1,128)S(1)}, f32[1,1,1024]{2,1,0:T(1,128)}, u32[]{:S(2)}) copy-start(f32[1,1,1024]{2,1,0:T(1,128)} %param.6) | copy-start | bytes 12292
  4.9 0.7 %copy-start.1 = (s32[1,1,2]{2,1,0:T(1,128)S(1)}, s32[1,1,2]{2,1,0:T(1,128)}, u32[]{:S(2)}) copy-start(s32[1,1,2]{2,1,0:T(1,128)} %param.10) | copy-start | bytes 28
  4.9 0.7 %copy-start.3 = (s32[1,1,8,32]{3,2,1,0:T(8,128)S(1)}, s32[1,1,8,32]{3,2,1,0:T(8,128)}, u32[]{:S(2)}) copy-start(s32[1,1,8,32]{3,2,1,0:T(8,128)} %param.8) | copy-start | bytes 3076
  4.9 0.7 %copy-start.4 = (f32[1,1,2,128]{3,2,1,0:T(2,128)S(1)}, f32[1,1,2,128]{3,2,1,0:T(2,128)}, u32[]{:S(2)}) copy-start(f32[1,1,2,128]{3,2,1,0:T(2,128)} %param.11) | copy-start | bytes 3076
  4.9 0.7 %copy-start.5 = (s32[1,1,128]{2,1,0:T(1,128)S(1)}, s32[1,1,128]{2,1,0:T(1,128)}, u32[]{:S(2)}) copy-start(s32[1,1,128]{2,1,0:T(1,128)} %param.9) | copy-start | bytes 1540
  5.1 14.5 %collective-permute-start.1 = (bf16[1,4,16,4096]{3,2,1,0:T(8,128)(2,1)S(1)}, bf16[1,4,16,4096]{3,2,1,0:T(8,128)(2,1)S(1)}, u32[]{:S(2)}, u32[]{:S(2)}) collective-permute-start(bf16[1,4,16,4096]{3,2,1,0:T(8,128)(2,1)S(1)} %get-tuple-element.19), channel_id=1, source_target_pairs={{4,0},{0,4},{5,1},{1,5},{6,2},{2,6},{7,3},{3,7},{12,8},{8,12},{13,... | collective-permute-start | bytes 1572872 | tf_op jit(solution)/shard_map/ppermute | solution.py:292

commit v14 on v13

--- a/solution.py
+++ b/solution.py
@@ -123,13 +123,8 @@
             second_ref[at * own_rows : (at + 1) * own_rows, :] = own.astype(jnp.bfloat16)
 
 
-def widen_kernel(blocks_ref, out_ref, send_ref):
+def widen_kernel(blocks_ref, out_ref):
     out_ref[...] = blocks_ref[...].astype(jnp.float32)
-    others, _, own_rows, _ = send_ref.shape
-    blk, parts = lax.axis_index("blk"), lax.axis_size("blk")
-    for step in range(1, others + 1):
-        part = lax.rem(blk + parts - step, parts)
-        send_ref[step - 1] = blocks_ref[:, pl.ds(pl.multiple_of(part * own_rows, 16), own_rows), :]
 
 
 def first_kernel(
@@ -308,19 +303,21 @@
 
     long = pl.CostEstimate(flops=1 << 32, bytes_accessed=1 << 20, transcendentals=0)
     others = from_others(lambda step: start[None])
-    wide, send = pl.pallas_call(
+
+    def rows_of_other(step):
+        part = lax.rem(lax.axis_index("blk") + parts - step, parts)
+        return lax.dynamic_slice_in_dim(blocks, part * own_blocks, own_blocks, 1)[None]
+
+    other_blocks = from_others(rows_of_other)
+    wide = pl.pallas_call(
         widen_kernel,
-        out_shape=(
-            shaped(jnp.float32, *blocks.shape),
-            shaped(jnp.bfloat16, parts - 1, slots, own_blocks, width),
-        ),
+        out_shape=shaped(jnp.float32, *blocks.shape),
         in_specs=[vmem],
-        out_specs=(vmem, vmem),
+        out_specs=vmem,
         compiler_params=params,
         cost_estimate=long,
         name="wide_blocks",
     )(blocks)
-    other_blocks = from_others(lambda step: send if parts == 2 else send[step - 1 : step])
     lines, chosen, chosen_own = pl.pallas_call(
         lines_kernel,
         out_shape=(

time: 34 us -> 33.7 us (level)
  blocking collectives: 24.9 us -> 23.4 us
  local copies, waits for them, and re-layouts: 1.68 us -> 2.87 us
    all_to_all x1, blocking collectives: 11.8 us -> 10.1 us  [per_device(): sums = lax.all_to_all(sums, ('rep', 'sub', 'blk'), 0, 0, tiled=True)]
    broadcast_in_dim x0 -> x1, local copies, waits for them, and re-layouts: none -> 1.08 us  [rows_of_other(): lax.dynamic_slice_in_dim(blocks, part * own_blocks, own_blocks, 1)[None]]
  transfers between devices with their start and end apart: 2 -> 2, of which waited for: 0 -> 0; matrix products, arithmetic and copies ran while one was open for 0% -> 3% of each run, Pallas kernels for 3% -> 3%
where the time goes in v14:
time: 33.7 us; the launch traced here: 33.4 us
  blocking collectives  23.4 us (69%)
  Pallas kernels  3.36 us (10%)
  starting transfers between devices  3.13 us (9%)
  local copies, waits for them, and re-layouts  2.87 us (9%)
  between operations  0.68 us (2%)
    all_to_all x1, blocking collectives, per_device(): group = lax.all_to_all(partial, ('sub', 'blk'), 0, 0, tiled=True)  13.2 us
    all_to_all x1, blocking collectives, per_device(): sums = lax.all_to_all(sums, ('rep', 'sub', 'blk'), 0, 0, tiled=True)  10.1 us
    ppermute x2, starting transfers between devices, from_others(): lax.ppermute(pick(step), 'blk', [((i + step) % parts, i) for i in range(p...  3.13 us
    unnamed x12, local copies, waits for them, and re-layouts  1.79 us
    pallas_call x1, Pallas kernels, per_device(): pl.pallas_call(second_kernel, out_shape=(rowed(reps * subs * parts, 1), r...  1.61 us
    broadcast_in_dim x1, local copies, waits for them, and re-layouts, rows_of_other(): lax.dynamic_slice_in_dim(blocks, part * own_blocks, own_blocks, 1)[None]  1.08 us
    pallas_call x1, Pallas kernels, per_device(): pl.pallas_call(functools.partial(last_kernel, float(cells)), out_shape=(r...  0.74 us
  transfers between devices with their start and end apart: 2, of which 0 were waited for; matrix products, arithmetic and copies ran while one was open for 3% of the time, Pallas kernels for 3%

profile of v14, /device:TPU:0, one launch (start us, length us, event | category | flops | bytes accessed | tf_op | source)
XLA Modules:
  0.0 33.4 jit_solution(9034553568105139046)
XLA Ops:
  0.6 3.0 %collective-permute-start = (f32[1,8,128]{2,1,0:T(8,128)}, f32[1,8,128]{2,1,0:T(8,128)S(1)}, u32[]{:S(2)}, u32[]{:S(2)}) collective-permute-start(f32[1,8,128]{2,1,0:T(8,128)} %bitcast.13), channel_id=1, source_target_pairs={{4,0},{0,4},{5,1},{1,5},{6,2},{2,6},{7,3},{3,7},{12,8},{8,12},{13,... | collective-permute-start | bytes 12296 | tf_op jit(solution)/shard_map/ppermute | solution.py:287
  3.7 1.1 %dynamic-slice_bitcast_fusion = bf16[1,4,16,4096]{3,2,1,0:T(8,128)(2,1)S(1)} fusion(bf16[1,1,4,32,4096]{4,3,2,1,0:T(8,128)(2,1)} %param.7, s32[]{:T(128)S(6)} %select_n.3), kind=kLoop, calls=%fused_computation | loop fusion | bytes 1048580 | tf_op jit(solution)/shard_map/broadcast_in_dim | solution.py:309
  4.7 0.1 collective-permute-start.1
  4.8 0.0 copy-start
  4.8 1.2 %copy-done = bf16[1,1,4,32,4096]{4,3,2,1,0:T(8,128)(2,1)S(1)} copy-done((bf16[1,1,4,32,4096]{4,3,2,1,0:T(8,128)(2,1)S(1)}, bf16[1,1,4,32,4096]{4,3,2,1,0:T(8,128)(2,1)}, u32[]{:S(2)}) %copy-start) | copy-done | bytes 1048600
  6.1 0.0 copy-start.1
  6.1 0.0 copy-start.2
  6.1 0.0 copy-start.3
  6.1 0.0 copy-start.4
  6.1 0.0 copy-start.5
  6.1 0.1 wide_blocks.1.blocks_ref
  6.2 0.5 %copy-done.1 = f32[1,1,1024]{2,1,0:T(1,128)S(1)} copy-done((f32[1,1,1024]{2,1,0:T(1,128)S(1)}, f32[1,1,1024]{2,1,0:T(1,128)}, u32[]{:S(2)}) %copy-start.1) | copy-done | bytes 4120
  6.8 0.0 copy-done.2
  6.8 0.0 copy-done.3
  6.8 0.0 copy-done.4
  6.8 0.0 copy-done.5
  6.8 0.2 group_lines.1
  7.0 0.0 collective-permute-done.other_ref
  7.0 0.6 %first_image.1 = (f32[8,24,128]{2,1,0:T(8,128)S(1)}, f32[16,128]{1,0:T(8,128)}) custom-call(f32[8,128]{1,0:T(8,128)S(1)} %bitcast.15, f32[8,128]{1,0:T(8,128)S(1)} %get-tuple-element.13.lines_ref, f32[1,8,128]{2,1,0:T(8,128)S(1)} %collective-permute-done.other_ref, f32[4,32,4096]{2,1,0:T(8,128)S(1)} %wide_blocks.1.blocks_ref, ...), custom_call_target="tpu_custom_call" | custom-call | tf_op jit(solution)/shard_map/first_image/pallas_call | solution.py:335
  7.7 13.2 %all_to_all.10.group_ref = f32[8,24,128]{2,1,0:T(8,128)S(1)} all-to-all(f32[8,24,128]{2,1,0:T(8,128)S(1)} %get-tuple-element.15), channel_id=1, replica_groups=mesh['sub'=4,'blk'=2,'rep'=4] {'sub','blk'}, dimensions={0} | all-to-all | bytes 196608 | tf_op jit(solution)/shard_map/all_to_all | solution.py:344
  20.9 0.0 collective-permute-done.1.other_ref
  20.9 1.6 %second_image.1 = (f32[32,1,128]{2,1,0:T(1,128)S(1)}, f32[8,128]{1,0:T(8,128)S(1)}, f32[8,128]{1,0:T(8,128)S(1)}) custom-call(f32[8,128]{1,0:T(8,128)S(1)} %bitcast.16, f32[8,24,128]{2,1,0:T(8,128)S(1)} %all_to_all.10.group_ref, f32[4,32,4096]{2,1,0:T(8,128)S(1)} %wide_blocks.1.blocks_ref, bf16[1,4,16,4096]{3,2,1,0:T(8,128)(2,1)S(1)} %collective-permute-done.1.other_ref, ...), custom_call_target="tpu_custom_call" | custom-call | tf_op jit(solution)/shard_map/second_image/pallas_call | solution.py:345
  22.5 10.1 %all_to_all.11.sums_ref = f32[32,1,128]{2,1,0:T(1,128)S(1)} all-to-all(f32[32,1,128]{2,1,0:T(1,128)S(1)} %get-tuple-element.19), channel_id=1, replica_groups=mesh['sub'=4,'blk'=2,'rep'=4] {'rep','sub','blk'}, dimensions={0} | all-to-all | bytes 32768 | tf_op jit(solution)/shard_map/all_to_all | solution.py:354
  32.7 0.7 %arnoldi_entries.1 = (f32[8,128]{1,0:T(8,128)}, f32[8,128]{1,0:T(8,128)}, f32[1,5]{1,0:T(1,128)}) custom-call(f32[8,128]{1,0:T(8,128)S(1)} %bitcast.17, f32[8,128]{1,0:T(8,128)S(1)} %get-tuple-element.17.image_ref, f32[8,128]{1,0:T(8,128)S(1)} %get-tuple-element.18.again_ref, f32[32,1,128]{2,1,0:T(1,128)S(1)} %all_to_all.11.sums_ref), custom_call_target="tpu_custom_call" | custom-call | tf_op jit(solution)/shard_map/arnoldi_entries/pallas_call | solution.py:355
Async XLA Ops:
  0.6 6.4 %collective-permute-start = (f32[1,8,128]{2,1,0:T(8,128)}, f32[1,8,128]{2,1,0:T(8,128)S(1)}, u32[]{:S(2)}, u32[]{:S(2)}) collective-permute-start(f32[1,8,128]{2,1,0:T(8,128)} %bitcast.13), channel_id=1, source_target_pairs={{4,0},{0,4},{5,1},{1,5},{6,2},{2,6},{7,3},{3,7},{12,8},{8,12},{13,... | collective-permute-start | bytes 12296 | tf_op jit(solution)/shard_map/ppermute | solution.py:287
  4.7 16.2 %collective-permute-start.1 = (bf16[1,4,16,4096]{3,2,1,0:T(8,128)(2,1)S(1)}, bf16[1,4,16,4096]{3,2,1,0:T(8,128)(2,1)S(1)}, u32[]{:S(2)}, u32[]{:S(2)}) collective-permute-start(bf16[1,4,16,4096]{3,2,1,0:T(8,128)(2,1)S(1)} %dynamic-slice_bitcast_fusion), channel_id=1, source_target_pairs={{4,0},{0,4},{5,1},{1,5},{6,2},{2,6},{7,3},{3,7},{12,8},{8,12},{13,... | collective-permute-start | bytes 1572872 | tf_op jit(solution)/shard_map/ppermute | solution.py:287
  4.8 1.2 %copy-start = (bf16[1,1,4,32,4096]{4,3,2,1,0:T(8,128)(2,1)S(1)}, bf16[1,1,4,32,4096]{4,3,2,1,0:T(8,128)(2,1)}, u32[]{:S(2)}) copy-start(bf16[1,1,4,32,4096]{4,3,2,1,0:T(8,128)(2,1)} %param.7) | copy-start | bytes 3145732
  6.1 0.7 %copy-start.1 = (f32[1,1,1024]{2,1,0:T(1,128)S(1)}, f32[1,1,1024]{2,1,0:T(1,128)}, u32[]{:S(2)}) copy-start(f32[1,1,1024]{2,1,0:T(1,128)} %param.6) | copy-start | bytes 12292
  6.1 0.7 %copy-start.2 = (s32[1,1,2]{2,1,0:T(1,128)S(1)}, s32[1,1,2]{2,1,0:T(1,128)}, u32[]{:S(2)}) copy-start(s32[1,1,2]{2,1,0:T(1,128)} %param.10) | copy-start | bytes 28
  6.1 0.7 %copy-start.3 = (s32[1,1,8,32]{3,2,1,0:T(8,128)S(1)}, s32[1,1,8,32]{3,2,1,0:T(8,128)}, u32[]{:S(2)}) copy-start(s32[1,1,8,32]{3,2,1,0:T(8,128)} %param.8) | copy-start | bytes 3076
  6.1 0.7 %copy-start.4 = (f32[1,1,2,128]{3,2,1,0:T(2,128)S(1)}, f32[1,1,2,128]{3,2,1,0:T(2,128)}, u32[]{:S(2)}) copy-start(f32[1,1,2,128]{3,2,1,0:T(2,128)} %param.11) | copy-start | bytes 3076
  6.1 0.7 %copy-start.5 = (s32[1,1,128]{2,1,0:T(1,128)S(1)}, s32[1,1,128]{2,1,0:T(1,128)}, u32[]{:S(2)}) copy-start(s32[1,1,128]{2,1,0:T(1,128)} %param.9) | copy-start | bytes 1540

commit v15 on v14

--- a/solution.py
+++ b/solution.py
@@ -123,6 +123,14 @@
             second_ref[at * own_rows : (at + 1) * own_rows, :] = own.astype(jnp.bfloat16)
 
 
+def send_kernel(blocks_ref, out_ref):
+    others, _, own_rows, _ = out_ref.shape
+    blk, parts = lax.axis_index("blk"), lax.axis_size("blk")
+    for step in range(1, others + 1):
+        part = lax.rem(blk + parts - step, parts)
+        out_ref[step - 1] = blocks_ref[:, pl.ds(pl.multiple_of(part * own_rows, 16), own_rows), :]
+
+
 def widen_kernel(blocks_ref, out_ref):
     out_ref[...] = blocks_ref[...].astype(jnp.float32)
 
@@ -200,16 +208,6 @@
     own_blocks = block_rows // parts
     here = pl.ds(pl.multiple_of(blk * own_blocks, 16), own_blocks)
     own = pl.ds(pl.multiple_of(blk * own_rows, SUBL), own_rows)
-    added = [landed(group_ref, sub, part, own_rows, count)[0] for part in range(parts)]
-    image = summed(group_ref, sub, pl.ds(0, own_rows * parts)) + jnp.concatenate(added, 0)
-    whole_ref[...] = image
-
-    def fetch(k, lanes):
-        if k < slots:
-            return blocks_ref[k, here, lanes]
-        return other_ref[k // slots - 1, k % slots, :, lanes].astype(jnp.float32)
-
-    again = block_product(image, fetch, width, choices_ref[...], fold_ref, halves_ref)
     inflow = jnp.zeros((1, LANES), jnp.float32)
     for n in range(count):
         source = near_ref[0, n]
@@ -217,7 +215,17 @@
         trace = take_trace(summed(group_ref, source, own) + added, places)
         inflow = inflow + line(group_ref, sub * parts + blk, 2 + n) * trace
     places = line(group_ref, sub * parts + blk, 1).astype(jnp.int32) - blk * own_rows * LANES
-    again = again + spread(inflow, places, own_rows)
+    inflow = spread(inflow, places, own_rows)
+    added = [landed(group_ref, sub, part, own_rows, count)[0] for part in range(parts)]
+    image = summed(group_ref, sub, pl.ds(0, own_rows * parts)) + jnp.concatenate(added, 0)
+    whole_ref[...] = image
+
+    def fetch(k, lanes):
+        if k < slots:
+            return blocks_ref[k, here, lanes]
+        return other_ref[k // slots - 1, k % slots, :, lanes].astype(jnp.float32)
+
+    again = block_product(image, fetch, width, choices_ref[...], fold_ref, halves_ref) + inflow
     again_ref[...] = again
     vector, image = start_ref[...], whole_ref[own, :]
     image_ref[...] = image
@@ -304,11 +312,15 @@
     long = pl.CostEstimate(flops=1 << 32, bytes_accessed=1 << 20, transcendentals=0)
     others = from_others(lambda step: start[None])
 
-    def rows_of_other(step):
-        part = lax.rem(lax.axis_index("blk") + parts - step, parts)
-        return lax.dynamic_slice_in_dim(blocks, part * own_blocks, own_blocks, 1)[None]
-
-    other_blocks = from_others(rows_of_other)
+    send = pl.pallas_call(
+        send_kernel,
+        out_shape=shaped(jnp.bfloat16, parts - 1, slots, own_blocks, width),
+        in_specs=[vmem],
+        out_specs=vmem,
+        compiler_params=params,
+        name="send_blocks",
+    )(blocks)
+    other_blocks = from_others(lambda step: send if parts == 2 else send[step - 1 : step])
     wide = pl.pallas_call(
         widen_kernel,
         out_shape=shaped(jnp.float32, *blocks.shape),

time: 33.7 us -> 33.9 us (level)
  blocking collectives: 23.4 us -> 24.8 us
  local copies, waits for them, and re-layouts: 2.87 us -> 1.69 us
    all_to_all x1, blocking collectives: 10.1 us -> 11.8 us  [per_device(): sums = lax.all_to_all(sums, ('rep', 'sub', 'blk'), 0, 0, tiled=True)]
    broadcast_in_dim x1 -> x0, local copies, waits for them, and re-layouts: 1.08 us -> none  [rows_of_other(): lax.dynamic_slice_in_dim(blocks, part * own_blocks, own_blocks, 1)[None]]
  transfers between devices with their start and end apart: 2 -> 2, of which waited for: 0 -> 0; matrix products, arithmetic and copies ran while one was open for 3% -> 0% of each run, Pallas kernels for 3% -> 3%
where the time goes in v15:
time: 33.9 us; the launch traced here: 33.7 us
  blocking collectives  24.8 us (73%)
  Pallas kernels  3.42 us (10%)
  starting transfers between devices  3.11 us (9%)
  local copies, waits for them, and re-layouts  1.69 us (5%)
  between operations  0.71 us (2%)
    all_to_all x1, blocking collectives, per_device(): group = lax.all_to_all(partial, ('sub', 'blk'), 0, 0, tiled=True)  12.9 us
    all_to_all x1, blocking collectives, per_device(): sums = lax.all_to_all(sums, ('rep', 'sub', 'blk'), 0, 0, tiled=True)  11.8 us
    ppermute x2, starting transfers between devices, from_others(): lax.ppermute(pick(step), 'blk', [((i + step) % parts, i) for i in range(p...  3.11 us
    unnamed x12, local copies, waits for them, and re-layouts  1.69 us
    pallas_call x1, Pallas kernels, per_device(): pl.pallas_call(second_kernel, out_shape=(rowed(reps * subs * parts, 1), r...  1.63 us
    pallas_call x1, Pallas kernels, per_device(): pl.pallas_call(functools.partial(last_kernel, float(cells)), out_shape=(r...  0.74 us
  transfers between devices with their start and end apart: 2, of which 0 were waited for; matrix products, arithmetic and copies ran while one was open for 0% of the time, Pallas kernels for 3%

profile of v15, /device:TPU:0, one launch (start us, length us, event | category | flops | bytes accessed | tf_op | source)
XLA Modules:
  0.0 33.7 jit_solution(3900631148632521435)
XLA Ops:
  0.6 3.0 %collective-permute-start = (f32[1,8,128]{2,1,0:T(8,128)}, f32[1,8,128]{2,1,0:T(8,128)S(1)}, u32[]{:S(2)}, u32[]{:S(2)}) collective-permute-start(f32[1,8,128]{2,1,0:T(8,128)} %bitcast.12), channel_id=1, source_target_pairs={{4,0},{0,4},{5,1},{1,5},{6,2},{2,6},{7,3},{3,7},{12,8},{8,12},{13,... | collective-permute-start | bytes 12296 | tf_op jit(solution)/shard_map/ppermute | solution.py:295
  3.7 0.0 copy-start
  3.7 1.2 %copy-done = bf16[1,1,4,32,4096]{4,3,2,1,0:T(8,128)(2,1)S(1)} copy-done((bf16[1,1,4,32,4096]{4,3,2,1,0:T(8,128)(2,1)S(1)}, bf16[1,1,4,32,4096]{4,3,2,1,0:T(8,128)(2,1)}, u32[]{:S(2)}) %copy-start) | copy-done | bytes 1048600
  4.9 0.0 copy-start.1
  4.9 0.0 copy-start.2
  4.9 0.0 copy-start.3
  5.0 0.0 copy-start.4
  5.0 0.0 copy-start.5
  5.0 0.1 collective-permute-start.1
  5.1 0.1 wide_blocks.1.blocks_ref
  5.2 0.4 %copy-done.1 = f32[1,1,1024]{2,1,0:T(1,128)S(1)} copy-done((f32[1,1,1024]{2,1,0:T(1,128)S(1)}, f32[1,1,1024]{2,1,0:T(1,128)}, u32[]{:S(2)}) %copy-start.1) | copy-done | bytes 4120
  5.6 0.0 copy-done.2
  5.6 0.0 copy-done.3
  5.6 0.0 copy-done.4
  5.7 0.0 copy-done.5
  5.7 0.2 group_lines.1
  5.9 0.0 collective-permute-done.other_ref
  5.9 0.6 %first_image.1 = (f32[8,24,128]{2,1,0:T(8,128)S(1)}, f32[16,128]{1,0:T(8,128)}) custom-call(f32[8,128]{1,0:T(8,128)S(1)} %bitcast.14, f32[8,128]{1,0:T(8,128)S(1)} %get-tuple-element.13.lines_ref, f32[1,8,128]{2,1,0:T(8,128)S(1)} %collective-permute-done.other_ref, f32[4,32,4096]{2,1,0:T(8,128)S(1)} %wide_blocks.1.blocks_ref, ...), custom_call_target="tpu_custom_call" | custom-call | tf_op jit(solution)/shard_map/first_image/pallas_call | solution.py:347
  6.5 12.9 %all_to_all.10.group_ref = f32[8,24,128]{2,1,0:T(8,128)S(1)} all-to-all(f32[8,24,128]{2,1,0:T(8,128)S(1)} %get-tuple-element.15), channel_id=1, replica_groups=mesh['sub'=4,'blk'=2,'rep'=4] {'sub','blk'}, dimensions={0} | all-to-all | bytes 196608 | tf_op jit(solution)/shard_map/all_to_all | solution.py:356
  19.5 0.0 collective-permute-done.1.other_ref
  19.5 1.6 %second_image.1 = (f32[32,1,128]{2,1,0:T(1,128)S(1)}, f32[8,128]{1,0:T(8,128)S(1)}, f32[8,128]{1,0:T(8,128)S(1)}) custom-call(f32[8,128]{1,0:T(8,128)S(1)} %bitcast.15, f32[8,24,128]{2,1,0:T(8,128)S(1)} %all_to_all.10.group_ref, f32[4,32,4096]{2,1,0:T(8,128)S(1)} %wide_blocks.1.blocks_ref, bf16[1,4,16,4096]{3,2,1,0:T(8,128)(2,1)S(1)} %collective-permute-done.1.other_ref, ...), custom_call_target="tpu_custom_call" | custom-call | tf_op jit(solution)/shard_map/second_image/pallas_call | solution.py:357
  21.1 11.8 %all_to_all.11.sums_ref = f32[32,1,128]{2,1,0:T(1,128)S(1)} all-to-all(f32[32,1,128]{2,1,0:T(1,128)S(1)} %get-tuple-element.19), channel_id=1, replica_groups=mesh['sub'=4,'blk'=2,'rep'=4] {'rep','sub','blk'}, dimensions={0} | all-to-all | bytes 32768 | tf_op jit(solution)/shard_map/all_to_all | solution.py:366
  33.0 0.7 %arnoldi_entries.1 = (f32[8,128]{1,0:T(8,128)}, f32[8,128]{1,0:T(8,128)}, f32[1,5]{1,0:T(1,128)}) custom-call(f32[8,128]{1,0:T(8,128)S(1)} %bitcast.16, f32[8,128]{1,0:T(8,128)S(1)} %get-tuple-element.17.image_ref, f32[8,128]{1,0:T(8,128)S(1)} %get-tuple-element.18.again_ref, f32[32,1,128]{2,1,0:T(1,128)S(1)} %all_to_all.11.sums_ref), custom_call_target="tpu_custom_call" | custom-call | tf_op jit(solution)/shard_map/arnoldi_entries/pallas_call | solution.py:367
  (1 shorter events, 0.0 us)
Async XLA Ops:
  0.6 5.3 %collective-permute-start = (f32[1,8,128]{2,1,0:T(8,128)}, f32[1,8,128]{2,1,0:T(8,128)S(1)}, u32[]{:S(2)}, u32[]{:S(2)}) collective-permute-start(f32[1,8,128]{2,1,0:T(8,128)} %bitcast.12), channel_id=1, source_target_pairs={{4,0},{0,4},{5,1},{1,5},{6,2},{2,6},{7,3},{3,7},{12,8},{8,12},{13,... | collective-permute-start | bytes 12296 | tf_op jit(solution)/shard_map/ppermute | solution.py:295
  3.7 1.2 %copy-start = (bf16[1,1,4,32,4096]{4,3,2,1,0:T(8,128)(2,1)S(1)}, bf16[1,1,4,32,4096]{4,3,2,1,0:T(8,128)(2,1)}, u32[]{:S(2)}) copy-start(bf16[1,1,4,32,4096]{4,3,2,1,0:T(8,128)(2,1)} %param.7) | copy-start | bytes 3145732
  4.9 0.7 %copy-start.1 = (f32[1,1,1024]{2,1,0:T(1,128)S(1)}, f32[1,1,1024]{2,1,0:T(1,128)}, u32[]{:S(2)}) copy-start(f32[1,1,1024]{2,1,0:T(1,128)} %param.6) | copy-start | bytes 12292
  4.9 0.7 %copy-start.2 = (s32[1,1,2]{2,1,0:T(1,128)S(1)}, s32[1,1,2]{2,1,0:T(1,128)}, u32[]{:S(2)}) copy-start(s32[1,1,2]{2,1,0:T(1,128)} %param.10) | copy-start | bytes 28
  4.9 0.7 %copy-start.3 = (s32[1,1,8,32]{3,2,1,0:T(8,128)S(1)}, s32[1,1,8,32]{3,2,1,0:T(8,128)}, u32[]{:S(2)}) copy-start(s32[1,1,8,32]{3,2,1,0:T(8,128)} %param.8) | copy-start | bytes 3076
  5.0 0.7 %copy-start.4 = (f32[1,1,2,128]{3,2,1,0:T(2,128)S(1)}, f32[1,1,2,128]{3,2,1,0:T(2,128)}, u32[]{:S(2)}) copy-start(f32[1,1,2,128]{3,2,1,0:T(2,128)} %param.11) | copy-start | bytes 3076
  5.0 0.7 %copy-start.5 = (s32[1,1,128]{2,1,0:T(1,128)S(1)}, s32[1,1,128]{2,1,0:T(1,128)}, u32[]{:S(2)}) copy-start(s32[1,1,128]{2,1,0:T(1,128)} %param.9) | copy-start | bytes 1540
  5.0 14.5 %collective-permute-start.1 = (bf16[1,4,16,4096]{3,2,1,0:T(8,128)(2,1)S(1)}, bf16[1,4,16,4096]{3,2,1,0:T(8,128)(2,1)S(1)}, u32[]{:S(2)}, u32[]{:S(2)}) collective-permute-start(bf16[1,4,16,4096]{3,2,1,0:T(8,128)(2,1)S(1)} %send_blocks.1), channel_id=1, source_target_pairs={{4,0},{0,4},{5,1},{1,5},{6,2},{2,6},{7,3},{3,7},{12,8},{8,12},{13,... | collective-permute-start | bytes 1572872 | tf_op jit(solution)/shard_map/ppermute | solution.py:295

commit v16 on v15

--- a/solution.py
+++ b/solution.py
@@ -192,19 +192,23 @@
     group_ref,
     blocks_ref,
     other_ref,
-    choices_ref,
+    first_ref,
+    second_ref,
     near_ref,
-    out_ref,
+    base_ref,
+    give_ref,
     image_ref,
-    again_ref,
     whole_ref,
     fold_ref,
     halves_ref,
+    own_fold_ref,
+    own_halves_ref,
 ):
     own_rows = start_ref.shape[0]
     slots, block_rows, width = blocks_ref.shape
     count = near_ref.shape[1]
     sub, blk, parts = lax.axis_index("sub"), lax.axis_index("blk"), lax.axis_size("blk")
+    odd = lax.rem(lax.axis_index("rep"), 2)
     own_blocks = block_rows // parts
     here = pl.ds(pl.multiple_of(blk * own_blocks, 16), own_blocks)
     own = pl.ds(pl.multiple_of(blk * own_rows, SUBL), own_rows)
@@ -215,20 +219,41 @@
         trace = take_trace(summed(group_ref, source, own) + added, places)
         inflow = inflow + line(group_ref, sub * parts + blk, 2 + n) * trace
     places = line(group_ref, sub * parts + blk, 1).astype(jnp.int32) - blk * own_rows * LANES
-    inflow = spread(inflow, places, own_rows)
+    base_ref[...] = spread(inflow, places, own_rows)
     added = [landed(group_ref, sub, part, own_rows, count)[0] for part in range(parts)]
-    image = summed(group_ref, sub, pl.ds(0, own_rows * parts)) + jnp.concatenate(added, 0)
-    whole_ref[...] = image
-
-    def fetch(k, lanes):
+    whole_ref[...] = summed(group_ref, sub, pl.ds(0, own_rows * parts)) + jnp.concatenate(added, 0)
+    image_ref[...] = whole_ref[own, :]
+
+    def fetch_own(k, lanes):
         if k < slots:
             return blocks_ref[k, here, lanes]
         return other_ref[k // slots - 1, k % slots, :, lanes].astype(jnp.float32)
 
-    again = block_product(image, fetch, width, choices_ref[...], fold_ref, halves_ref) + inflow
+    def fetch(k, lanes):
+        return blocks_ref[k, :, lanes]
+
+    @pl.when(odd == 0)
+    def _():
+        product = block_product(whole_ref[...], fetch_own, width, second_ref[...], own_fold_ref, own_halves_ref)
+        base_ref[...] = base_ref[...] + product
+        give_ref[...] = jnp.zeros(give_ref.shape, jnp.float32)
+
+    @pl.when(odd == 1)
+    def _():
+        product = block_product(whole_ref[...], fetch, width, first_ref[...], fold_ref, halves_ref)
+        whole_ref[...] = product
+        base_ref[...] = base_ref[...] + whole_ref[own, :]
+        for step in range(1, parts):
+            part = lax.rem(blk + parts - step, parts)
+            give_ref[step - 1] = whole_ref[pl.ds(pl.multiple_of(part * own_rows, SUBL), own_rows), :]
+
+
+def sums_kernel(start_ref, image_ref, base_ref, other_ref, out_ref, again_ref):
+    again = base_ref[...]
+    for step in range(other_ref.shape[0]):
+        again = again + other_ref[step]
     again_ref[...] = again
-    vector, image = start_ref[...], whole_ref[own, :]
-    image_ref[...] = image
+    vector, image = start_ref[...], image_ref[...]
     sums = [down(vector, vector), down(vector, image), down(image, image)]
     sums += [down(vector, again), down(image, again), down(again, again)]
     sums = jnp.concatenate([*sums, jnp.zeros((SUBL - 6, LANES), jnp.float32)], 0)
@@ -290,11 +315,11 @@
 
     smem = pl.BlockSpec(memory_space=pltpu.SMEM)
 
-    def from_others(pick):
-        got = [
-            lax.ppermute(pick(step), "blk", [((i + step) % parts, i) for i in range(parts)])
-            for step in range(1, parts)
-        ]
+    def from_others(pick, members=range(reps)):
+        got = []
+        for step in range(1, parts):
+            route = [((i + step) % parts * reps + r, i * reps + r) for r in members for i in range(parts)]
+            got.append(lax.ppermute(pick(step), ("blk", "rep"), route))
         return got[0] if parts == 2 else jnp.concatenate(got, 0)
 
     slots, block_rows, width = blocks.shape
@@ -320,7 +345,7 @@
         compiler_params=params,
         name="send_blocks",
     )(blocks)
-    other_blocks = from_others(lambda step: send if parts == 2 else send[step - 1 : step])
+    other_blocks = from_others(lambda step: send if parts == 2 else send[step - 1 : step], range(0, reps, 2))
     wide = pl.pallas_call(
         widen_kernel,
         out_shape=shaped(jnp.float32, *blocks.shape),
@@ -354,15 +379,24 @@
         name="first_image",
     )(start, lines, others, wide, chosen)
     group = lax.all_to_all(partial, ("sub", "blk"), 0, 0, tiled=True)
-    sums, image, again = pl.pallas_call(
+    base, give, image = pl.pallas_call(
         second_kernel,
-        out_shape=(rowed(reps * subs * parts, 1), rowed(own_rows), rowed(own_rows)),
-        in_specs=[vmem] * 5 + [smem],
+        out_shape=(rowed(own_rows), rowed(parts - 1, own_rows), rowed(own_rows)),
+        in_specs=[vmem] * 6 + [smem],
         out_specs=(vmem, vmem, vmem),
-        scratch_shapes=[pltpu.VMEM((rows, LANES), jnp.float32), *scratch(own_blocks)],
+        scratch_shapes=[pltpu.VMEM((rows, LANES), jnp.float32), *scratch(block_rows), *scratch(own_blocks)],
         compiler_params=params,
         name="second_image",
-    )(start, group, wide, other_blocks, chosen_own, neighbours)
+    )(start, group, wide, other_blocks, chosen, chosen_own, neighbours)
+    given = from_others(lambda step: give if parts == 2 else give[step - 1 : step], range(1, reps, 2))
+    sums, again = pl.pallas_call(
+        sums_kernel,
+        out_shape=(rowed(reps * subs * parts, 1), rowed(own_rows)),
+        in_specs=[vmem] * 4,
+        out_specs=(vmem, vmem),
+        compiler_params=params,
+        name="own_sums",
+    )(start, image, base, given)
     sums = lax.all_to_all(sums, ("rep", "sub", "blk"), 0, 0, tiled=True)
     second, third, entries = pl.pallas_call(
         functools.partial(last_kernel, float(cells)),

time: 33.9 us -> 33.9 us (level)
  starting transfers between devices: 3.11 us -> 5.75 us
  blocking collectives: 24.8 us -> 22.4 us
  local copies, waits for them, and re-layouts: 1.69 us -> 1.26 us
    all_to_all x1, blocking collectives: 11.8 us -> 9.17 us  [per_device(): sums = lax.all_to_all(sums, ('rep', 'sub', 'blk'), 0, 0, tiled=True)]
    ppermute x2 -> x3, starting transfers between devices: 3.11 us -> 5.75 us  [from_others(): got.append(lax.ppermute(pick(step), ('blk', 'rep'), route))]
    unnamed x12, local copies, waits for them, and re-layouts: 1.69 us -> 1.26 us
    pallas_call x1 -> x2, Pallas kernels: 1.63 us -> 1.66 us  [the longest x1 1.55 us: per_device(): pl.pallas_call(second_kernel, out_shape=(rowed(own_rows), rowed(parts - 1...]
  transfers between devices with their start and end apart: 2 -> 3, of which waited for: 0 -> 0; matrix products, arithmetic and copies ran while one was open for 0% -> 0% of each run, Pallas kernels for 3% -> 3%
where the time goes in v16:
time: 33.9 us; the launch traced here: 33.7 us
  blocking collectives  22.4 us (66%)
  starting transfers between devices  5.75 us (17%)
  Pallas kernels  3.46 us (10%)
  local copies, waits for them, and re-layouts  1.26 us (4%)
  between operations  0.77 us (2%)
    all_to_all x1, blocking collectives, per_device(): group = lax.all_to_all(partial, ('sub', 'blk'), 0, 0, tiled=True)  13.2 us
    all_to_all x1, blocking collectives, per_device(): sums = lax.all_to_all(sums, ('rep', 'sub', 'blk'), 0, 0, tiled=True)  9.17 us
    ppermute x3, starting transfers between devices, from_others(): got.append(lax.ppermute(pick(step), ('blk', 'rep'), route))  5.75 us
    pallas_call x1, Pallas kernels, per_device(): pl.pallas_call(second_kernel, out_shape=(rowed(own_rows), rowed(parts - 1...  1.55 us
    unnamed x12, local copies, waits for them, and re-layouts  1.26 us
    pallas_call x1, Pallas kernels, per_device(): pl.pallas_call(functools.partial(last_kernel, float(cells)), out_shape=(r...  0.74 us
  transfers between devices with their start and end apart: 3, of which 0 were waited for; matrix products, arithmetic and copies ran while one was open for 0% of the time, Pallas kernels for 3%

profile of v16, /device:TPU:0, one launch (start us, length us, event | category | flops | bytes accessed | tf_op | source)
XLA Modules:
  0.0 33.7 jit_solution(9320491254314089830)
XLA Ops:
  0.6 3.0 %collective-permute-start = (f32[1,8,128]{2,1,0:T(8,128)}, f32[1,8,128]{2,1,0:T(8,128)S(1)}, u32[]{:S(2)}, u32[]{:S(2)}) collective-permute-start(f32[1,8,128]{2,1,0:T(8,128)} %bitcast.12), channel_id=1, source_target_pairs={{4,0},{0,4},{5,1},{1,5},{6,2},{2,6},{7,3},{3,7},{12,8},{8,12},{13,... | collective-permute-start | bytes 12296 | tf_op jit(solution)/shard_map/ppermute | solution.py:322
  3.7 0.0 copy-start
  3.7 1.2 %copy-done = bf16[1,1,4,32,4096]{4,3,2,1,0:T(8,128)(2,1)S(1)} copy-done((bf16[1,1,4,32,4096]{4,3,2,1,0:T(8,128)(2,1)S(1)}, bf16[1,1,4,32,4096]{4,3,2,1,0:T(8,128)(2,1)}, u32[]{:S(2)}) %copy-start) | copy-done | bytes 1048600
  4.9 0.0 copy-start.1
  4.9 0.0 copy-start.2
  4.9 0.0 copy-start.3
  5.0 0.0 copy-start.4
  5.0 0.0 copy-start.5
  5.0 2.1 %collective-permute-start.1 = (bf16[1,4,16,4096]{3,2,1,0:T(8,128)(2,1)S(1)}, bf16[1,4,16,4096]{3,2,1,0:T(8,128)(2,1)S(1)}, u32[]{:S(2)}, u32[]{:S(2)}) collective-permute-start(bf16[1,4,16,4096]{3,2,1,0:T(8,128)(2,1)S(1)} %send_blocks.1), channel_id=1, source_target_pairs={{4,0},{0,4},{6,2},{2,6},{12,8},{8,12},{14,10},{10,14},{20,16},{16,... | collective-permute-start | bytes 1572872 | tf_op jit(solution)/shard_map/ppermute | solution.py:322
  7.0 0.1 wide_blocks.1.blocks_ref
  7.2 0.0 copy-done.1
  7.2 0.0 copy-done.2
  7.2 0.0 copy-done.3
  7.2 0.0 copy-done.4
  7.2 0.0 copy-done.5
  7.2 0.2 group_lines.1
  7.5 0.0 collective-permute-done.other_ref
  7.5 0.6 %first_image.1 = (f32[8,24,128]{2,1,0:T(8,128)S(1)}, f32[16,128]{1,0:T(8,128)}) custom-call(f32[8,128]{1,0:T(8,128)S(1)} %bitcast.14, f32[8,128]{1,0:T(8,128)S(1)} %get-tuple-element.15.lines_ref, f32[1,8,128]{2,1,0:T(8,128)S(1)} %collective-permute-done.other_ref, f32[4,32,4096]{2,1,0:T(8,128)S(1)} %wide_blocks.1.blocks_ref, ...), custom_call_target="tpu_custom_call" | custom-call | tf_op jit(solution)/shard_map/first_image/pallas_call | solution.py:372
  8.2 13.2 %all_to_all.10.group_ref = f32[8,24,128]{2,1,0:T(8,128)S(1)} all-to-all(f32[8,24,128]{2,1,0:T(8,128)S(1)} %get-tuple-element.17), channel_id=1, replica_groups=mesh['sub'=4,'blk'=2,'rep'=4] {'sub','blk'}, dimensions={0} | all-to-all | bytes 196608 | tf_op jit(solution)/shard_map/all_to_all | solution.py:381
  21.4 0.0 collective-permute-done.1.other_ref
  21.4 1.6 %second_image.1 = (f32[8,128]{1,0:T(8,128)S(1)}, f32[1,8,128]{2,1,0:T(8,128)S(1)}, f32[8,128]{1,0:T(8,128)S(1)}) custom-call(f32[8,128]{1,0:T(8,128)S(1)} %bitcast.15, f32[8,24,128]{2,1,0:T(8,128)S(1)} %all_to_all.10.group_ref, f32[4,32,4096]{2,1,0:T(8,128)S(1)} %wide_blocks.1.blocks_ref, bf16[1,4,16,4096]{3,2,1,0:T(8,128)(2,1)S(1)} %collective-permute-done.1.other_ref, ...), custom_call_target="tpu_custom_call" | custom-call | tf_op jit(solution)/shard_map/second_image/pallas_call | solution.py:382
  23.0 0.7 %collective-permute-start.2 = (f32[1,8,128]{2,1,0:T(8,128)S(1)}, f32[1,8,128]{2,1,0:T(8,128)S(1)}, u32[]{:S(2)}, u32[]{:S(2)}) collective-permute-start(f32[1,8,128]{2,1,0:T(8,128)S(1)} %get-tuple-element.21), channel_id=1, source_target_pairs={{5,1},{1,5},{7,3},{3,7},{13,9},{9,13},{15,11},{11,15},{21,17},{17,... | collective-permute-start | bytes 12296 | tf_op jit(solution)/shard_map/ppermute | solution.py:322
  23.6 0.0 collective-permute-done.2.other_ref
  23.6 0.1 own_sums.1
  23.7 9.2 %all_to_all.11.sums_ref = f32[32,1,128]{2,1,0:T(1,128)S(1)} all-to-all(f32[32,1,128]{2,1,0:T(1,128)S(1)} %get-tuple-element.23), channel_id=1, replica_groups=mesh['sub'=4,'blk'=2,'rep'=4] {'rep','sub','blk'}, dimensions={0} | all-to-all | bytes 32768 | tf_op jit(solution)/shard_map/all_to_all | solution.py:400
  32.9 0.7 %arnoldi_entries.1 = (f32[8,128]{1,0:T(8,128)}, f32[8,128]{1,0:T(8,128)}, f32[1,5]{1,0:T(1,128)}) custom-call(f32[8,128]{1,0:T(8,128)S(1)} %bitcast.17, f32[8,128]{1,0:T(8,128)S(1)} %get-tuple-element.19.image_ref, f32[8,128]{1,0:T(8,128)S(1)} %get-tuple-element.22.again_ref, f32[32,1,128]{2,1,0:T(1,128)S(1)} %all_to_all.11.sums_ref), custom_call_target="tpu_custom_call" | custom-call | tf_op jit(solution)/shard_map/arnoldi_entries/pallas_call | solution.py:401
  (1 shorter events, 0.0 us)
Async XLA Ops:
  0.6 6.9 %collective-permute-start = (f32[1,8,128]{2,1,0:T(8,128)}, f32[1,8,128]{2,1,0:T(8,128)S(1)}, u32[]{:S(2)}, u32[]{:S(2)}) collective-permute-start(f32[1,8,128]{2,1,0:T(8,128)} %bitcast.12), channel_id=1, source_target_pairs={{4,0},{0,4},{5,1},{1,5},{6,2},{2,6},{7,3},{3,7},{12,8},{8,12},{13,... | collective-permute-start | bytes 12296 | tf_op jit(solution)/shard_map/ppermute | solution.py:322
  3.7 1.2 %copy-start = (bf16[1,1,4,32,4096]{4,3,2,1,0:T(8,128)(2,1)S(1)}, bf16[1,1,4,32,4096]{4,3,2,1,0:T(8,128)(2,1)}, u32[]{:S(2)}) copy-start(bf16[1,1,4,32,4096]{4,3,2,1,0:T(8,128)(2,1)} %param.7) | copy-start | bytes 3145732
  4.9 2.3 %copy-start.1 = (f32[1,1,1024]{2,1,0:T(1,128)S(1)}, f32[1,1,1024]{2,1,0:T(1,128)}, u32[]{:S(2)}) copy-start(f32[1,1,1024]{2,1,0:T(1,128)} %param.6) | copy-start | bytes 12292
  4.9 2.3 %copy-start.2 = (s32[1,1,2]{2,1,0:T(1,128)S(1)}, s32[1,1,2]{2,1,0:T(1,128)}, u32[]{:S(2)}) copy-start(s32[1,1,2]{2,1,0:T(1,128)} %param.10) | copy-start | bytes 28
  4.9 2.3 %copy-start.3 = (s32[1,1,8,32]{3,2,1,0:T(8,128)S(1)}, s32[1,1,8,32]{3,2,1,0:T(8,128)}, u32[]{:S(2)}) copy-start(s32[1,1,8,32]{3,2,1,0:T(8,128)} %param.8) | copy-start | bytes 3076
  5.0 2.3 %copy-start.4 = (f32[1,1,2,128]{3,2,1,0:T(2,128)S(1)}, f32[1,1,2,128]{3,2,1,0:T(2,128)}, u32[]{:S(2)}) copy-start(f32[1,1,2,128]{3,2,1,0:T(2,128)} %param.11) | copy-start | bytes 3076
  5.0 2.3 %copy-start.5 = (s32[1,1,128]{2,1,0:T(1,128)S(1)}, s32[1,1,128]{2,1,0:T(1,128)}, u32[]{:S(2)}) copy-start(s32[1,1,128]{2,1,0:T(1,128)} %param.9) | copy-start | bytes 1540
  5.0 16.4 %collective-permute-start.1 = (bf16[1,4,16,4096]{3,2,1,0:T(8,128)(2,1)S(1)}, bf16[1,4,16,4096]{3,2,1,0:T(8,128)(2,1)S(1)}, u32[]{:S(2)}, u32[]{:S(2)}) collective-permute-start(bf16[1,4,16,4096]{3,2,1,0:T(8,128)(2,1)S(1)} %send_blocks.1), channel_id=1, source_target_pairs={{4,0},{0,4},{6,2},{2,6},{12,8},{8,12},{14,10},{10,14},{20,16},{16,... | collective-permute-start | bytes 1572872 | tf_op jit(solution)/shard_map/ppermute | solution.py:322
  23.0 0.7 %collective-permute-start.2 = (f32[1,8,128]{2,1,0:T(8,128)S(1)}, f32[1,8,128]{2,1,0:T(8,128)S(1)}, u32[]{:S(2)}, u32[]{:S(2)}) collective-permute-start(f32[1,8,128]{2,1,0:T(8,128)S(1)} %get-tuple-element.21), channel_id=1, source_target_pairs={{5,1},{1,5},{7,3},{3,7},{13,9},{9,13},{15,11},{11,15},{21,17},{17,... | collective-permute-start | bytes 12296 | tf_op jit(solution)/shard_map/ppermute | solution.py:322

commit v17 on v16

--- a/solution.py
+++ b/solution.py
@@ -318,7 +318,9 @@
     def from_others(pick, members=range(reps)):
         got = []
         for step in range(1, parts):
-            route = [((i + step) % parts * reps + r, i * reps + r) for r in members for i in range(parts)]
+            route = [
+                ((i + step * (r in members)) % parts * reps + r, i * reps + r) for r in range(reps) for i in range(parts)
+            ]
             got.append(lax.ppermute(pick(step), ("blk", "rep"), route))
         return got[0] if parts == 2 else jnp.concatenate(got, 0)
 

time: 33.9 us -> 33.9 us (level)
  no operation moved by 1% of the time
where the time goes in v17:
time: 33.9 us; the launch traced here: 33.7 us
  blocking collectives  22.4 us (66%)
  starting transfers between devices  5.75 us (17%)
  Pallas kernels  3.46 us (10%)
  local copies, waits for them, and re-layouts  1.26 us (4%)
  between operations  0.77 us (2%)
    all_to_all x1, blocking collectives, per_device(): group = lax.all_to_all(partial, ('sub', 'blk'), 0, 0, tiled=True)  13.2 us
    all_to_all x1, blocking collectives, per_device(): sums = lax.all_to_all(sums, ('rep', 'sub', 'blk'), 0, 0, tiled=True)  9.17 us
    ppermute x3, starting transfers between devices, from_others(): got.append(lax.ppermute(pick(step), ('blk', 'rep'), route))  5.75 us
    pallas_call x1, Pallas kernels, per_device(): pl.pallas_call(second_kernel, out_shape=(rowed(own_rows), rowed(parts - 1...  1.55 us
    unnamed x12, local copies, waits for them, and re-layouts  1.26 us
    pallas_call x1, Pallas kernels, per_device(): pl.pallas_call(functools.partial(last_kernel, float(cells)), out_shape=(r...  0.74 us
  transfers between devices with their start and end apart: 3, of which 0 were waited for; matrix products, arithmetic and copies ran while one was open for 0% of the time, Pallas kernels for 3%

profile of v17, /device:TPU:0, one launch (start us, length us, event | category | flops | bytes accessed | tf_op | source)
XLA Modules:
  0.0 33.7 jit_solution(8669809935319397946)
XLA Ops:
  0.6 3.0 %collective-permute-start = (f32[1,8,128]{2,1,0:T(8,128)}, f32[1,8,128]{2,1,0:T(8,128)S(1)}, u32[]{:S(2)}, u32[]{:S(2)}) collective-permute-start(f32[1,8,128]{2,1,0:T(8,128)} %bitcast.12), channel_id=1, source_target_pairs={{4,0},{0,4},{5,1},{1,5},{6,2},{2,6},{7,3},{3,7},{12,8},{8,12},{13,... | collective-permute-start | bytes 12296 | tf_op jit(solution)/shard_map/ppermute | solution.py:324
  3.7 0.0 copy-start
  3.7 1.2 %copy-done = bf16[1,1,4,32,4096]{4,3,2,1,0:T(8,128)(2,1)S(1)} copy-done((bf16[1,1,4,32,4096]{4,3,2,1,0:T(8,128)(2,1)S(1)}, bf16[1,1,4,32,4096]{4,3,2,1,0:T(8,128)(2,1)}, u32[]{:S(2)}) %copy-start) | copy-done | bytes 1048600
  4.9 0.0 copy-start.1
  4.9 0.0 copy-start.2
  4.9 0.0 copy-start.3
  5.0 0.0 copy-start.4
  5.0 0.0 copy-start.5
  5.0 2.1 %collective-permute-start.1 = (bf16[1,4,16,4096]{3,2,1,0:T(8,128)(2,1)S(1)}, bf16[1,4,16,4096]{3,2,1,0:T(8,128)(2,1)S(1)}, u32[]{:S(2)}, u32[]{:S(2)}) collective-permute-start(bf16[1,4,16,4096]{3,2,1,0:T(8,128)(2,1)S(1)} %send_blocks.1), channel_id=1, source_target_pairs={{4,0},{0,4},{1,1},{5,5},{6,2},{2,6},{3,3},{7,7},{12,8},{8,12},{9,9... | collective-permute-start | bytes 1572872 | tf_op jit(solution)/shard_map/ppermute | solution.py:324
  7.0 0.1 wide_blocks.1.blocks_ref
  7.2 0.0 copy-done.1
  7.2 0.0 copy-done.2
  7.2 0.0 copy-done.3
  7.2 0.0 copy-done.4
  7.2 0.0 copy-done.5
  7.2 0.2 group_lines.1
  7.5 0.0 collective-permute-done.other_ref
  7.5 0.6 %first_image.1 = (f32[8,24,128]{2,1,0:T(8,128)S(1)}, f32[16,128]{1,0:T(8,128)}) custom-call(f32[8,128]{1,0:T(8,128)S(1)} %bitcast.14, f32[8,128]{1,0:T(8,128)S(1)} %get-tuple-element.15.lines_ref, f32[1,8,128]{2,1,0:T(8,128)S(1)} %collective-permute-done.other_ref, f32[4,32,4096]{2,1,0:T(8,128)S(1)} %wide_blocks.1.blocks_ref, ...), custom_call_target="tpu_custom_call" | custom-call | tf_op jit(solution)/shard_map/first_image/pallas_call | solution.py:374
  8.2 13.2 %all_to_all.10.group_ref = f32[8,24,128]{2,1,0:T(8,128)S(1)} all-to-all(f32[8,24,128]{2,1,0:T(8,128)S(1)} %get-tuple-element.17), channel_id=1, replica_groups=mesh['sub'=4,'blk'=2,'rep'=4] {'sub','blk'}, dimensions={0} | all-to-all | bytes 196608 | tf_op jit(solution)/shard_map/all_to_all | solution.py:383
  21.4 0.0 collective-permute-done.1.other_ref
  21.4 1.6 %second_image.1 = (f32[8,128]{1,0:T(8,128)S(1)}, f32[1,8,128]{2,1,0:T(8,128)S(1)}, f32[8,128]{1,0:T(8,128)S(1)}) custom-call(f32[8,128]{1,0:T(8,128)S(1)} %bitcast.15, f32[8,24,128]{2,1,0:T(8,128)S(1)} %all_to_all.10.group_ref, f32[4,32,4096]{2,1,0:T(8,128)S(1)} %wide_blocks.1.blocks_ref, bf16[1,4,16,4096]{3,2,1,0:T(8,128)(2,1)S(1)} %collective-permute-done.1.other_ref, ...), custom_call_target="tpu_custom_call" | custom-call | tf_op jit(solution)/shard_map/second_image/pallas_call | solution.py:384
  23.0 0.7 %collective-permute-start.2 = (f32[1,8,128]{2,1,0:T(8,128)S(1)}, f32[1,8,128]{2,1,0:T(8,128)S(1)}, u32[]{:S(2)}, u32[]{:S(2)}) collective-permute-start(f32[1,8,128]{2,1,0:T(8,128)S(1)} %get-tuple-element.21), channel_id=1, source_target_pairs={{0,0},{4,4},{5,1},{1,5},{2,2},{6,6},{7,3},{3,7},{8,8},{12,12},{13,... | collective-permute-start | bytes 12296 | tf_op jit(solution)/shard_map/ppermute | solution.py:324
  23.6 0.0 collective-permute-done.2.other_ref
  23.6 0.1 own_sums.1
  23.7 9.2 %all_to_all.11.sums_ref = f32[32,1,128]{2,1,0:T(1,128)S(1)} all-to-all(f32[32,1,128]{2,1,0:T(1,128)S(1)} %get-tuple-element.23), channel_id=1, replica_groups=mesh['sub'=4,'blk'=2,'rep'=4] {'rep','sub','blk'}, dimensions={0} | all-to-all | bytes 32768 | tf_op jit(solution)/shard_map/all_to_all | solution.py:402
  32.9 0.7 %arnoldi_entries.1 = (f32[8,128]{1,0:T(8,128)}, f32[8,128]{1,0:T(8,128)}, f32[1,5]{1,0:T(1,128)}) custom-call(f32[8,128]{1,0:T(8,128)S(1)} %bitcast.17, f32[8,128]{1,0:T(8,128)S(1)} %get-tuple-element.19.image_ref, f32[8,128]{1,0:T(8,128)S(1)} %get-tuple-element.22.again_ref, f32[32,1,128]{2,1,0:T(1,128)S(1)} %all_to_all.11.sums_ref), custom_call_target="tpu_custom_call" | custom-call | tf_op jit(solution)/shard_map/arnoldi_entries/pallas_call | solution.py:403
  (1 shorter events, 0.0 us)
Async XLA Ops:
  0.6 6.9 %collective-permute-start = (f32[1,8,128]{2,1,0:T(8,128)}, f32[1,8,128]{2,1,0:T(8,128)S(1)}, u32[]{:S(2)}, u32[]{:S(2)}) collective-permute-start(f32[1,8,128]{2,1,0:T(8,128)} %bitcast.12), channel_id=1, source_target_pairs={{4,0},{0,4},{5,1},{1,5},{6,2},{2,6},{7,3},{3,7},{12,8},{8,12},{13,... | collective-permute-start | bytes 12296 | tf_op jit(solution)/shard_map/ppermute | solution.py:324
  3.7 1.2 %copy-start = (bf16[1,1,4,32,4096]{4,3,2,1,0:T(8,128)(2,1)S(1)}, bf16[1,1,4,32,4096]{4,3,2,1,0:T(8,128)(2,1)}, u32[]{:S(2)}) copy-start(bf16[1,1,4,32,4096]{4,3,2,1,0:T(8,128)(2,1)} %param.7) | copy-start | bytes 3145732
  4.9 2.3 %copy-start.1 = (f32[1,1,1024]{2,1,0:T(1,128)S(1)}, f32[1,1,1024]{2,1,0:T(1,128)}, u32[]{:S(2)}) copy-start(f32[1,1,1024]{2,1,0:T(1,128)} %param.6) | copy-start | bytes 12292
  4.9 2.3 %copy-start.2 = (s32[1,1,2]{2,1,0:T(1,128)S(1)}, s32[1,1,2]{2,1,0:T(1,128)}, u32[]{:S(2)}) copy-start(s32[1,1,2]{2,1,0:T(1,128)} %param.10) | copy-start | bytes 28
  4.9 2.3 %copy-start.3 = (s32[1,1,8,32]{3,2,1,0:T(8,128)S(1)}, s32[1,1,8,32]{3,2,1,0:T(8,128)}, u32[]{:S(2)}) copy-start(s32[1,1,8,32]{3,2,1,0:T(8,128)} %param.8) | copy-start | bytes 3076
  5.0 2.3 %copy-start.4 = (f32[1,1,2,128]{3,2,1,0:T(2,128)S(1)}, f32[1,1,2,128]{3,2,1,0:T(2,128)}, u32[]{:S(2)}) copy-start(f32[1,1,2,128]{3,2,1,0:T(2,128)} %param.11) | copy-start | bytes 3076
  5.0 2.3 %copy-start.5 = (s32[1,1,128]{2,1,0:T(1,128)S(1)}, s32[1,1,128]{2,1,0:T(1,128)}, u32[]{:S(2)}) copy-start(s32[1,1,128]{2,1,0:T(1,128)} %param.9) | copy-start | bytes 1540
  5.0 16.4 %collective-permute-start.1 = (bf16[1,4,16,4096]{3,2,1,0:T(8,128)(2,1)S(1)}, bf16[1,4,16,4096]{3,2,1,0:T(8,128)(2,1)S(1)}, u32[]{:S(2)}, u32[]{:S(2)}) collective-permute-start(bf16[1,4,16,4096]{3,2,1,0:T(8,128)(2,1)S(1)} %send_blocks.1), channel_id=1, source_target_pairs={{4,0},{0,4},{1,1},{5,5},{6,2},{2,6},{3,3},{7,7},{12,8},{8,12},{9,9... | collective-permute-start | bytes 1572872 | tf_op jit(solution)/shard_map/ppermute | solution.py:324
  23.0 0.7 %collective-permute-start.2 = (f32[1,8,128]{2,1,0:T(8,128)S(1)}, f32[1,8,128]{2,1,0:T(8,128)S(1)}, u32[]{:S(2)}, u32[]{:S(2)}) collective-permute-start(f32[1,8,128]{2,1,0:T(8,128)S(1)} %get-tuple-element.21), channel_id=1, source_target_pairs={{0,0},{4,4},{5,1},{1,5},{2,2},{6,6},{7,3},{3,7},{8,8},{12,12},{13,... | collective-permute-start | bytes 12296 | tf_op jit(solution)/shard_map/ppermute | solution.py:324

commit v18 on v16

--- a/solution.py
+++ b/solution.py
@@ -315,10 +315,12 @@
 
     smem = pl.BlockSpec(memory_space=pltpu.SMEM)
 
-    def from_others(pick, members=range(reps)):
+    def from_others(pick, members=range(reps), idle=()):
         got = []
         for step in range(1, parts):
             route = [((i + step) % parts * reps + r, i * reps + r) for r in members for i in range(parts)]
+            if idle:
+                route += [(i * reps + idle[n - 1], i * reps + r) for n, r in enumerate(idle) for i in range(parts)]
             got.append(lax.ppermute(pick(step), ("blk", "rep"), route))
         return got[0] if parts == 2 else jnp.concatenate(got, 0)
 
@@ -345,7 +347,7 @@
         compiler_params=params,
         name="send_blocks",
     )(blocks)
-    other_blocks = from_others(lambda step: send if parts == 2 else send[step - 1 : step], range(0, reps, 2))
+    other_blocks = from_others(lambda step: send if parts == 2 else send[step - 1 : step], range(0, reps, 2), range(1, reps, 2))
     wide = pl.pallas_call(
         widen_kernel,
         out_shape=shaped(jnp.float32, *blocks.shape),

time: 33.9 us -> 32.5 us (0.959)
  starting transfers between devices: 5.75 us -> 3.78 us
  local copies, waits for them, and re-layouts: 1.26 us -> 1.69 us
    ppermute x3, starting transfers between devices: 5.75 us -> 3.78 us  [from_others(): got.append(lax.ppermute(pick(step), ('blk', 'rep'), route))]
    all_to_all x1, blocking collectives: 9.17 us -> 9.72 us  [per_device(): sums = lax.all_to_all(sums, ('rep', 'sub', 'blk'), 0, 0, tiled=True)]
    unnamed x12, local copies, waits for them, and re-layouts: 1.26 us -> 1.69 us
    all_to_all x1, blocking collectives: 13.2 us -> 12.9 us  [per_device(): group = lax.all_to_all(partial, ('sub', 'blk'), 0, 0, tiled=True)]
where the time goes in v18:
time: 32.5 us; the launch traced here: 32.2 us
  blocking collectives  22.6 us (70%)
  starting transfers between devices  3.78 us (12%)
  Pallas kernels  3.45 us (11%)
  local copies, waits for them, and re-layouts  1.69 us (5%)
  between operations  0.73 us (2%)
    all_to_all x1, blocking collectives, per_device(): group = lax.all_to_all(partial, ('sub', 'blk'), 0, 0, tiled=True)  12.9 us
    all_to_all x1, blocking collectives, per_device(): sums = lax.all_to_all(sums, ('rep', 'sub', 'blk'), 0, 0, tiled=True)  9.72 us
    ppermute x3, starting transfers between devices, from_others(): got.append(lax.ppermute(pick(step), ('blk', 'rep'), route))  3.78 us
    unnamed x12, local copies, waits for them, and re-layouts  1.69 us
    pallas_call x1, Pallas kernels, per_device(): pl.pallas_call(second_kernel, out_shape=(rowed(own_rows), rowed(parts - 1...  1.55 us
    pallas_call x1, Pallas kernels, per_device(): pl.pallas_call(functools.partial(last_kernel, float(cells)), out_shape=(r...  0.74 us
  transfers between devices with their start and end apart: 3, of which 0 were waited for; matrix products, arithmetic and copies ran while one was open for 0% of the time, Pallas kernels for 3%

profile of v18, /device:TPU:0, one launch (start us, length us, event | category | flops | bytes accessed | tf_op | source)
XLA Modules:
  0.0 32.2 jit_solution(2062450143511386325)
XLA Ops:
  0.6 3.0 %collective-permute-start = (f32[1,8,128]{2,1,0:T(8,128)}, f32[1,8,128]{2,1,0:T(8,128)S(1)}, u32[]{:S(2)}, u32[]{:S(2)}) collective-permute-start(f32[1,8,128]{2,1,0:T(8,128)} %bitcast.12), channel_id=1, source_target_pairs={{4,0},{0,4},{5,1},{1,5},{6,2},{2,6},{7,3},{3,7},{12,8},{8,12},{13,... | collective-permute-start | bytes 12296 | tf_op jit(solution)/shard_map/ppermute | solution.py:324
  3.7 0.0 copy-start
  3.7 1.2 %copy-done = bf16[1,1,4,32,4096]{4,3,2,1,0:T(8,128)(2,1)S(1)} copy-done((bf16[1,1,4,32,4096]{4,3,2,1,0:T(8,128)(2,1)S(1)}, bf16[1,1,4,32,4096]{4,3,2,1,0:T(8,128)(2,1)}, u32[]{:S(2)}) %copy-start) | copy-done | bytes 1048600
  4.9 0.0 copy-start.1
  4.9 0.0 copy-start.2
  4.9 0.0 copy-start.3
  5.0 0.0 copy-start.4
  5.0 0.0 copy-start.5
  5.0 0.1 collective-permute-start.1
  5.1 0.1 wide_blocks.1.blocks_ref
  5.2 0.4 %copy-done.1 = f32[1,1,1024]{2,1,0:T(1,128)S(1)} copy-done((f32[1,1,1024]{2,1,0:T(1,128)S(1)}, f32[1,1,1024]{2,1,0:T(1,128)}, u32[]{:S(2)}) %copy-start.1) | copy-done | bytes 4120
  5.6 0.0 copy-done.2
  5.6 0.0 copy-done.3
  5.6 0.0 copy-done.4
  5.7 0.0 copy-done.5
  5.7 0.2 group_lines.1
  5.9 0.0 collective-permute-done.other_ref
  5.9 0.6 %first_image.1 = (f32[8,24,128]{2,1,0:T(8,128)S(1)}, f32[16,128]{1,0:T(8,128)}) custom-call(f32[8,128]{1,0:T(8,128)S(1)} %bitcast.14, f32[8,128]{1,0:T(8,128)S(1)} %get-tuple-element.15.lines_ref, f32[1,8,128]{2,1,0:T(8,128)S(1)} %collective-permute-done.other_ref, f32[4,32,4096]{2,1,0:T(8,128)S(1)} %wide_blocks.1.blocks_ref, ...), custom_call_target="tpu_custom_call" | custom-call | tf_op jit(solution)/shard_map/first_image/pallas_call | solution.py:374
  6.6 12.9 %all_to_all.10.group_ref = f32[8,24,128]{2,1,0:T(8,128)S(1)} all-to-all(f32[8,24,128]{2,1,0:T(8,128)S(1)} %get-tuple-element.17), channel_id=1, replica_groups=mesh['sub'=4,'blk'=2,'rep'=4] {'sub','blk'}, dimensions={0} | all-to-all | bytes 196608 | tf_op jit(solution)/shard_map/all_to_all | solution.py:383
  19.4 0.0 collective-permute-done.1.other_ref
  19.4 1.6 %second_image.1 = (f32[8,128]{1,0:T(8,128)S(1)}, f32[1,8,128]{2,1,0:T(8,128)S(1)}, f32[8,128]{1,0:T(8,128)S(1)}) custom-call(f32[8,128]{1,0:T(8,128)S(1)} %bitcast.15, f32[8,24,128]{2,1,0:T(8,128)S(1)} %all_to_all.10.group_ref, f32[4,32,4096]{2,1,0:T(8,128)S(1)} %wide_blocks.1.blocks_ref, bf16[1,4,16,4096]{3,2,1,0:T(8,128)(2,1)S(1)} %collective-permute-done.1.other_ref, ...), custom_call_target="tpu_custom_call" | custom-call | tf_op jit(solution)/shard_map/second_image/pallas_call | solution.py:384
  21.0 0.7 %collective-permute-start.2 = (f32[1,8,128]{2,1,0:T(8,128)S(1)}, f32[1,8,128]{2,1,0:T(8,128)S(1)}, u32[]{:S(2)}, u32[]{:S(2)}) collective-permute-start(f32[1,8,128]{2,1,0:T(8,128)S(1)} %get-tuple-element.21), channel_id=1, source_target_pairs={{5,1},{1,5},{7,3},{3,7},{13,9},{9,13},{15,11},{11,15},{21,17},{17,... | collective-permute-start | bytes 12296 | tf_op jit(solution)/shard_map/ppermute | solution.py:324
  21.6 0.0 collective-permute-done.2.other_ref
  21.7 0.1 own_sums.1
  21.8 9.7 %all_to_all.11.sums_ref = f32[32,1,128]{2,1,0:T(1,128)S(1)} all-to-all(f32[32,1,128]{2,1,0:T(1,128)S(1)} %get-tuple-element.23), channel_id=1, replica_groups=mesh['sub'=4,'blk'=2,'rep'=4] {'rep','sub','blk'}, dimensions={0} | all-to-all | bytes 32768 | tf_op jit(solution)/shard_map/all_to_all | solution.py:402
  31.5 0.7 %arnoldi_entries.1 = (f32[8,128]{1,0:T(8,128)}, f32[8,128]{1,0:T(8,128)}, f32[1,5]{1,0:T(1,128)}) custom-call(f32[8,128]{1,0:T(8,128)S(1)} %bitcast.17, f32[8,128]{1,0:T(8,128)S(1)} %get-tuple-element.19.image_ref, f32[8,128]{1,0:T(8,128)S(1)} %get-tuple-element.22.again_ref, f32[32,1,128]{2,1,0:T(1,128)S(1)} %all_to_all.11.sums_ref), custom_call_target="tpu_custom_call" | custom-call | tf_op jit(solution)/shard_map/arnoldi_entries/pallas_call | solution.py:403
  (1 shorter events, 0.0 us)
Async XLA Ops:
  0.6 5.3 %collective-permute-start = (f32[1,8,128]{2,1,0:T(8,128)}, f32[1,8,128]{2,1,0:T(8,128)S(1)}, u32[]{:S(2)}, u32[]{:S(2)}) collective-permute-start(f32[1,8,128]{2,1,0:T(8,128)} %bitcast.12), channel_id=1, source_target_pairs={{4,0},{0,4},{5,1},{1,5},{6,2},{2,6},{7,3},{3,7},{12,8},{8,12},{13,... | collective-permute-start | bytes 12296 | tf_op jit(solution)/shard_map/ppermute | solution.py:324
  3.7 1.2 %copy-start = (bf16[1,1,4,32,4096]{4,3,2,1,0:T(8,128)(2,1)S(1)}, bf16[1,1,4,32,4096]{4,3,2,1,0:T(8,128)(2,1)}, u32[]{:S(2)}) copy-start(bf16[1,1,4,32,4096]{4,3,2,1,0:T(8,128)(2,1)} %param.7) | copy-start | bytes 3145732
  4.9 0.7 %copy-start.1 = (f32[1,1,1024]{2,1,0:T(1,128)S(1)}, f32[1,1,1024]{2,1,0:T(1,128)}, u32[]{:S(2)}) copy-start(f32[1,1,1024]{2,1,0:T(1,128)} %param.6) | copy-start | bytes 12292
  4.9 0.7 %copy-start.2 = (s32[1,1,2]{2,1,0:T(1,128)S(1)}, s32[1,1,2]{2,1,0:T(1,128)}, u32[]{:S(2)}) copy-start(s32[1,1,2]{2,1,0:T(1,128)} %param.10) | copy-start | bytes 28
  4.9 0.7 %copy-start.3 = (s32[1,1,8,32]{3,2,1,0:T(8,128)S(1)}, s32[1,1,8,32]{3,2,1,0:T(8,128)}, u32[]{:S(2)}) copy-start(s32[1,1,8,32]{3,2,1,0:T(8,128)} %param.8) | copy-start | bytes 3076
  5.0 0.7 %copy-start.4 = (f32[1,1,2,128]{3,2,1,0:T(2,128)S(1)}, f32[1,1,2,128]{3,2,1,0:T(2,128)}, u32[]{:S(2)}) copy-start(f32[1,1,2,128]{3,2,1,0:T(2,128)} %param.11) | copy-start | bytes 3076
  5.0 0.7 %copy-start.5 = (s32[1,1,128]{2,1,0:T(1,128)S(1)}, s32[1,1,128]{2,1,0:T(1,128)}, u32[]{:S(2)}) copy-start(s32[1,1,128]{2,1,0:T(1,128)} %param.9) | copy-start | bytes 1540
  5.0 14.4 %collective-permute-start.1 = (bf16[1,4,16,4096]{3,2,1,0:T(8,128)(2,1)S(1)}, bf16[1,4,16,4096]{3,2,1,0:T(8,128)(2,1)S(1)}, u32[]{:S(2)}, u32[]{:S(2)}) collective-permute-start(bf16[1,4,16,4096]{3,2,1,0:T(8,128)(2,1)S(1)} %send_blocks.1), channel_id=1, source_target_pairs={{4,0},{0,4},{6,2},{2,6},{3,1},{7,5},{1,3},{5,7},{12,8},{8,12},{14,... | collective-permute-start | bytes 1572872 | tf_op jit(solution)/shard_map/ppermute | solution.py:324
  21.0 0.7 %collective-permute-start.2 = (f32[1,8,128]{2,1,0:T(8,128)S(1)}, f32[1,8,128]{2,1,0:T(8,128)S(1)}, u32[]{:S(2)}, u32[]{:S(2)}) collective-permute-start(f32[1,8,128]{2,1,0:T(8,128)S(1)} %get-tuple-element.21), channel_id=1, source_target_pairs={{5,1},{1,5},{7,3},{3,7},{13,9},{9,13},{15,11},{11,15},{21,17},{17,... | collective-permute-start | bytes 12296 | tf_op jit(solution)/shard_map/ppermute | solution.py:324

commit v19 on v18

--- a/solution.py
+++ b/solution.py
@@ -212,14 +212,7 @@
     own_blocks = block_rows // parts
     here = pl.ds(pl.multiple_of(blk * own_blocks, 16), own_blocks)
     own = pl.ds(pl.multiple_of(blk * own_rows, SUBL), own_rows)
-    inflow = jnp.zeros((1, LANES), jnp.float32)
-    for n in range(count):
-        source = near_ref[0, n]
-        added, places = landed(group_ref, source, blk, own_rows, count)
-        trace = take_trace(summed(group_ref, source, own) + added, places)
-        inflow = inflow + line(group_ref, sub * parts + blk, 2 + n) * trace
-    places = line(group_ref, sub * parts + blk, 1).astype(jnp.int32) - blk * own_rows * LANES
-    base_ref[...] = spread(inflow, places, own_rows)
+    base_ref[...] = jnp.zeros(base_ref.shape, jnp.float32)
     added = [landed(group_ref, sub, part, own_rows, count)[0] for part in range(parts)]
     whole_ref[...] = summed(group_ref, sub, pl.ds(0, own_rows * parts)) + jnp.concatenate(added, 0)
     image_ref[...] = whole_ref[own, :]
@@ -248,8 +241,22 @@
             give_ref[step - 1] = whole_ref[pl.ds(pl.multiple_of(part * own_rows, SUBL), own_rows), :]
 
 
-def sums_kernel(start_ref, image_ref, base_ref, other_ref, out_ref, again_ref):
-    again = base_ref[...]
+def inflow_kernel(group_ref, near_ref, out_ref):
+    own_rows, count = out_ref.shape[0], near_ref.shape[1]
+    sub, blk, parts = lax.axis_index("sub"), lax.axis_index("blk"), lax.axis_size("blk")
+    own = pl.ds(pl.multiple_of(blk * own_rows, SUBL), own_rows)
+    inflow = jnp.zeros((1, LANES), jnp.float32)
+    for n in range(count):
+        source = near_ref[0, n]
+        added, places = landed(group_ref, source, blk, own_rows, count)
+        trace = take_trace(summed(group_ref, source, own) + added, places)
+        inflow = inflow + line(group_ref, sub * parts + blk, 2 + n) * trace
+    places = line(group_ref, sub * parts + blk, 1).astype(jnp.int32) - blk * own_rows * LANES
+    out_ref[...] = spread(inflow, places, own_rows)
+
+
+def sums_kernel(start_ref, image_ref, base_ref, inflow_ref, other_ref, out_ref, again_ref):
+    again = base_ref[...] + inflow_ref[...]
     for step in range(other_ref.shape[0]):
         again = again + other_ref[step]
     again_ref[...] = again
@@ -391,14 +398,23 @@
         name="second_image",
     )(start, group, wide, other_blocks, chosen, chosen_own, neighbours)
     given = from_others(lambda step: give if parts == 2 else give[step - 1 : step], range(1, reps, 2))
+    inflow = pl.pallas_call(
+        inflow_kernel,
+        out_shape=rowed(own_rows),
+        in_specs=[vmem, smem],
+        out_specs=vmem,
+        compiler_params=params,
+        cost_estimate=long,
+        name="second_inflow",
+    )(group, neighbours)
     sums, again = pl.pallas_call(
         sums_kernel,
         out_shape=(rowed(reps * subs * parts, 1), rowed(own_rows)),
-        in_specs=[vmem] * 4,
+        in_specs=[vmem] * 5,
         out_specs=(vmem, vmem),
         compiler_params=params,
         name="own_sums",
-    )(start, image, base, given)
+    )(start, image, base, inflow, given)
     sums = lax.all_to_all(sums, ("rep", "sub", "blk"), 0, 0, tiled=True)
     second, third, entries = pl.pallas_call(
         functools.partial(last_kernel, float(cells)),

time: 32.5 us -> 32.6 us (level)
  Pallas kernels: 3.45 us -> 4.13 us
  blocking collectives: 22.6 us -> 22 us
    pallas_call x0 -> x1, Pallas kernels: none -> 0.91 us  [per_device(): pl.pallas_call(inflow_kernel, out_shape=rowed(own_rows), in_specs=[vmem,...]
    all_to_all x1, blocking collectives: 9.72 us -> 9.17 us  [per_device(): sums = lax.all_to_all(sums, ('rep', 'sub', 'blk'), 0, 0, tiled=True)]
  transfers between devices with their start and end apart: 3 -> 3, of which waited for: 0 -> 0; matrix products, arithmetic and copies ran while one was open for 0% -> 0% of each run, Pallas kernels for 3% -> 6%
where the time goes in v19:
time: 32.6 us; the launch traced here: 32.4 us
  blocking collectives  22 us (67%)
  Pallas kernels  4.13 us (13%)
  starting transfers between devices  3.78 us (12%)
  local copies, waits for them, and re-layouts  1.69 us (5%)
  between operations  0.73 us (2%)
    all_to_all x1, blocking collectives, per_device(): group = lax.all_to_all(partial, ('sub', 'blk'), 0, 0, tiled=True)  12.9 us
    all_to_all x1, blocking collectives, per_device(): sums = lax.all_to_all(sums, ('rep', 'sub', 'blk'), 0, 0, tiled=True)  9.17 us
    ppermute x3, starting transfers between devices, from_others(): got.append(lax.ppermute(pick(step), ('blk', 'rep'), route))  3.78 us
    unnamed x12, local copies, waits for them, and re-layouts  1.69 us
    pallas_call x1, Pallas kernels, per_device(): pl.pallas_call(second_kernel, out_shape=(rowed(own_rows), rowed(parts - 1...  1.31 us
    pallas_call x1, Pallas kernels, per_device(): pl.pallas_call(inflow_kernel, out_shape=rowed(own_rows), in_specs=[vmem,...  0.91 us
    pallas_call x1, Pallas kernels, per_device(): pl.pallas_call(functools.partial(last_kernel, float(cells)), out_shape=(r...  0.74 us
  transfers between devices with their start and end apart: 3, of which 0 were waited for; matrix products, arithmetic and copies ran while one was open for 0% of the time, Pallas kernels for 6%

profile of v19, /device:TPU:0, one launch (start us, length us, event | category | flops | bytes accessed | tf_op | source)
XLA Modules:
  0.0 32.4 jit_solution(13715935225767578853)
XLA Ops:
  0.6 3.0 %collective-permute-start = (f32[1,8,128]{2,1,0:T(8,128)}, f32[1,8,128]{2,1,0:T(8,128)S(1)}, u32[]{:S(2)}, u32[]{:S(2)}) collective-permute-start(f32[1,8,128]{2,1,0:T(8,128)} %bitcast.12), channel_id=1, source_target_pairs={{4,0},{0,4},{5,1},{1,5},{6,2},{2,6},{7,3},{3,7},{12,8},{8,12},{13,... | collective-permute-start | bytes 12296 | tf_op jit(solution)/shard_map/ppermute | solution.py:331
  3.7 0.0 copy-start
  3.7 1.2 %copy-done = bf16[1,1,4,32,4096]{4,3,2,1,0:T(8,128)(2,1)S(1)} copy-done((bf16[1,1,4,32,4096]{4,3,2,1,0:T(8,128)(2,1)S(1)}, bf16[1,1,4,32,4096]{4,3,2,1,0:T(8,128)(2,1)}, u32[]{:S(2)}) %copy-start) | copy-done | bytes 1048600
  4.9 0.0 copy-start.1
  4.9 0.0 copy-start.2
  4.9 0.0 copy-start.3
  5.0 0.0 copy-start.4
  5.0 0.0 copy-start.5
  5.0 0.1 collective-permute-start.1
  5.1 0.1 wide_blocks.1.blocks_ref
  5.2 0.4 %copy-done.1 = f32[1,1,1024]{2,1,0:T(1,128)S(1)} copy-done((f32[1,1,1024]{2,1,0:T(1,128)S(1)}, f32[1,1,1024]{2,1,0:T(1,128)}, u32[]{:S(2)}) %copy-start.1) | copy-done | bytes 4120
  5.6 0.0 copy-done.2
  5.6 0.0 copy-done.3
  5.6 0.0 copy-done.4
  5.7 0.0 copy-done.5
  5.7 0.2 group_lines.1
  5.9 0.0 collective-permute-done.other_ref
  5.9 0.6 %first_image.1 = (f32[8,24,128]{2,1,0:T(8,128)S(1)}, f32[16,128]{1,0:T(8,128)}) custom-call(f32[8,128]{1,0:T(8,128)S(1)} %bitcast.14, f32[8,128]{1,0:T(8,128)S(1)} %get-tuple-element.15.lines_ref, f32[1,8,128]{2,1,0:T(8,128)S(1)} %collective-permute-done.other_ref, f32[4,32,4096]{2,1,0:T(8,128)S(1)} %wide_blocks.1.blocks_ref, ...), custom_call_target="tpu_custom_call" | custom-call | tf_op jit(solution)/shard_map/first_image/pallas_call | solution.py:381
  6.6 12.9 %all_to_all.10.group_ref = f32[8,24,128]{2,1,0:T(8,128)S(1)} all-to-all(f32[8,24,128]{2,1,0:T(8,128)S(1)} %get-tuple-element.17), channel_id=1, replica_groups=mesh['sub'=4,'blk'=2,'rep'=4] {'sub','blk'}, dimensions={0} | all-to-all | bytes 196608 | tf_op jit(solution)/shard_map/all_to_all | solution.py:390
  19.4 0.0 collective-permute-done.1.other_ref
  19.4 1.3 %second_image.1 = (f32[8,128]{1,0:T(8,128)S(1)}, f32[1,8,128]{2,1,0:T(8,128)S(1)}, f32[8,128]{1,0:T(8,128)S(1)}) custom-call(f32[8,128]{1,0:T(8,128)S(1)} %bitcast.15, f32[8,24,128]{2,1,0:T(8,128)S(1)} %all_to_all.10.group_ref, f32[4,32,4096]{2,1,0:T(8,128)S(1)} %wide_blocks.1.blocks_ref, bf16[1,4,16,4096]{3,2,1,0:T(8,128)(2,1)S(1)} %collective-permute-done.1.other_ref, ...), custom_call_target="tpu_custom_call" | custom-call | tf_op jit(solution)/shard_map/second_image/pallas_call | solution.py:391
  20.7 0.7 %collective-permute-start.2 = (f32[1,8,128]{2,1,0:T(8,128)S(1)}, f32[1,8,128]{2,1,0:T(8,128)S(1)}, u32[]{:S(2)}, u32[]{:S(2)}) collective-permute-start(f32[1,8,128]{2,1,0:T(8,128)S(1)} %get-tuple-element.21), channel_id=1, source_target_pairs={{5,1},{1,5},{7,3},{3,7},{13,9},{9,13},{15,11},{11,15},{21,17},{17,... | collective-permute-start | bytes 12296 | tf_op jit(solution)/shard_map/ppermute | solution.py:331
  21.4 0.9 %second_inflow.1.inflow_ref = f32[8,128]{1,0:T(8,128)S(1)} custom-call(f32[8,24,128]{2,1,0:T(8,128)S(1)} %all_to_all.10.group_ref, s32[1,2]{1,0:T(1,128)S(1)} %bitcast.20), custom_call_target="tpu_custom_call" | custom-call | flops 4294967296 | bytes 1048576 | tf_op jit(solution)/shard_map/second_inflow/pallas_call | solution.py:401
  22.3 0.0 collective-permute-done.2.other_ref
  22.3 0.1 own_sums.1
  22.4 9.2 %all_to_all.11.sums_ref = f32[32,1,128]{2,1,0:T(1,128)S(1)} all-to-all(f32[32,1,128]{2,1,0:T(1,128)S(1)} %get-tuple-element.23), channel_id=1, replica_groups=mesh['sub'=4,'blk'=2,'rep'=4] {'rep','sub','blk'}, dimensions={0} | all-to-all | bytes 32768 | tf_op jit(solution)/shard_map/all_to_all | solution.py:418
  31.6 0.7 %arnoldi_entries.1 = (f32[8,128]{1,0:T(8,128)}, f32[8,128]{1,0:T(8,128)}, f32[1,5]{1,0:T(1,128)}) custom-call(f32[8,128]{1,0:T(8,128)S(1)} %bitcast.17, f32[8,128]{1,0:T(8,128)S(1)} %get-tuple-element.19.image_ref, f32[8,128]{1,0:T(8,128)S(1)} %get-tuple-element.22.again_ref, f32[32,1,128]{2,1,0:T(1,128)S(1)} %all_to_all.11.sums_ref), custom_call_target="tpu_custom_call" | custom-call | tf_op jit(solution)/shard_map/arnoldi_entries/pallas_call | solution.py:419
  (1 shorter events, 0.0 us)
Async XLA Ops:
  0.6 5.3 %collective-permute-start = (f32[1,8,128]{2,1,0:T(8,128)}, f32[1,8,128]{2,1,0:T(8,128)S(1)}, u32[]{:S(2)}, u32[]{:S(2)}) collective-permute-start(f32[1,8,128]{2,1,0:T(8,128)} %bitcast.12), channel_id=1, source_target_pairs={{4,0},{0,4},{5,1},{1,5},{6,2},{2,6},{7,3},{3,7},{12,8},{8,12},{13,... | collective-permute-start | bytes 12296 | tf_op jit(solution)/shard_map/ppermute | solution.py:331
  3.7 1.2 %copy-start = (bf16[1,1,4,32,4096]{4,3,2,1,0:T(8,128)(2,1)S(1)}, bf16[1,1,4,32,4096]{4,3,2,1,0:T(8,128)(2,1)}, u32[]{:S(2)}) copy-start(bf16[1,1,4,32,4096]{4,3,2,1,0:T(8,128)(2,1)} %param.7) | copy-start | bytes 3145732
  4.9 0.7 %copy-start.1 = (f32[1,1,1024]{2,1,0:T(1,128)S(1)}, f32[1,1,1024]{2,1,0:T(1,128)}, u32[]{:S(2)}) copy-start(f32[1,1,1024]{2,1,0:T(1,128)} %param.6) | copy-start | bytes 12292
  4.9 0.7 %copy-start.2 = (s32[1,1,2]{2,1,0:T(1,128)S(1)}, s32[1,1,2]{2,1,0:T(1,128)}, u32[]{:S(2)}) copy-start(s32[1,1,2]{2,1,0:T(1,128)} %param.10) | copy-start | bytes 28
  4.9 0.7 %copy-start.3 = (s32[1,1,8,32]{3,2,1,0:T(8,128)S(1)}, s32[1,1,8,32]{3,2,1,0:T(8,128)}, u32[]{:S(2)}) copy-start(s32[1,1,8,32]{3,2,1,0:T(8,128)} %param.8) | copy-start | bytes 3076
  5.0 0.7 %copy-start.4 = (f32[1,1,2,128]{3,2,1,0:T(2,128)S(1)}, f32[1,1,2,128]{3,2,1,0:T(2,128)}, u32[]{:S(2)}) copy-start(f32[1,1,2,128]{3,2,1,0:T(2,128)} %param.11) | copy-start | bytes 3076
  5.0 0.7 %copy-start.5 = (s32[1,1,128]{2,1,0:T(1,128)S(1)}, s32[1,1,128]{2,1,0:T(1,128)}, u32[]{:S(2)}) copy-start(s32[1,1,128]{2,1,0:T(1,128)} %param.9) | copy-start | bytes 1540
  5.0 14.4 %collective-permute-start.1 = (bf16[1,4,16,4096]{3,2,1,0:T(8,128)(2,1)S(1)}, bf16[1,4,16,4096]{3,2,1,0:T(8,128)(2,1)S(1)}, u32[]{:S(2)}, u32[]{:S(2)}) collective-permute-start(bf16[1,4,16,4096]{3,2,1,0:T(8,128)(2,1)S(1)} %send_blocks.1), channel_id=1, source_target_pairs={{4,0},{0,4},{6,2},{2,6},{3,1},{7,5},{1,3},{5,7},{12,8},{8,12},{14,... | collective-permute-start | bytes 1572872 | tf_op jit(solution)/shard_map/ppermute | solution.py:331
  20.7 1.6 %collective-permute-start.2 = (f32[1,8,128]{2,1,0:T(8,128)S(1)}, f32[1,8,128]{2,1,0:T(8,128)S(1)}, u32[]{:S(2)}, u32[]{:S(2)}) collective-permute-start(f32[1,8,128]{2,1,0:T(8,128)S(1)} %get-tuple-element.21), channel_id=1, source_target_pairs={{5,1},{1,5},{7,3},{3,7},{13,9},{9,13},{15,11},{11,15},{21,17},{17,... | collective-permute-start | bytes 12296 | tf_op jit(solution)/shard_map/ppermute | solution.py:331
